TPU v7x, 32 devices: a whole 2x2x4 slice. The times are simulated.
32 devices in a mesh: req: 16 (over z, y, x), tp: 2 (over core).
Axes of the slice: x: 2, y: 2, z: 4, core: 2. Of those that a mesh axis runs over, the one named last changes fastest.
Arguments:
- attn_heads: bfloat16 [2048, 2048], P('req', 'tp'), may hold values from -6 to 6
- residual_in: bfloat16 [2048, 4096], P('req', 'tp'), may hold values from -45 to 45
- w_out: bfloat16 [2048, 4096], P('tp'), may hold values from -0.125 to 0.125
- gain_attn: float32 [4096], P('tp'), may hold values from 0.1 to 1.9
- router: bfloat16 [4096, 4], P('tp'), may hold values from -0.09375 to 0.09375
- expert_ids: int32 [2048, 2], P('req'), may hold values from 0 to 3, all different within a row; in each aligned block of 64 rows (0 to 63, 64 to 127, ...) at most 48 rows name the same one
- lengths: int32 [16, 5], P('req'), may hold values from 1 to 64, 128 in all within a row
- placement: int32 [8], replicated, may hold values from 0 to 3, as said below
- w_gate_up: bfloat16 [16, 2, 4096, 3584], P('req', None, None, 'tp'), may hold values from -1 to 1, as said below
- w_down: bfloat16 [16, 3584, 4096], P('req', 'tp'), may hold values from -1 to 1, as said below
- gain_final: float32 [4096], P('tp'), may hold values from 0.1 to 1.9
Outputs:
- residual_out: bfloat16 [2048, 4096], P('req', 'tp')
- normed_out: bfloat16 [2048, 4096], P('req', 'tp')
Inputs may be any that keep to these rules, and one draw needn't show every extreme that they name: `expert_ids`: in each aligned block of 64 rows no expert is named by more than 48 rows, and the two experts of a row differ. `placement`: every expert is held by exactly two pairs. `w_gate_up`: index 2 s + h holds the h-th half of the hidden units of expert placement[s]; the two pairs of one expert hold equal values. `w_down`: index 2 s + h holds the h-th half of the hidden units of expert placement[s]; the two pairs of one expert hold equal values.
All inputs are finite; a program needn't handle non-finite values.
Results may differ from a plain program's by a relative error of at most 0.014.
Values may be sent and summed in bfloat16 or wider, within the bound.
No kernel may reach another device: no remote copies, remote signals or barrier semaphores. Data moves between devices by JAX's collectives and lax.ppermute only.
A program may use at most 128 MiB of HBM per device.

v0:
```python
import jax
import jax.numpy as jnp
from jax import lax
from jax.sharding import PartitionSpec as P

epsilon = 1e-05


def on_device(
    attn_heads,
    residual_in,
    w_out,
    gain_attn,
    router,
    expert_ids,
    lengths,
    placement,
    w_gate_up,
    w_down,
    gain_final,
):
    tok_rows = attn_heads.shape[0]
    half_rows = tok_rows // 2
    feat_width = residual_in.shape[1]
    full_width = feat_width * lax.axis_size("tp")
    devices = lax.axis_size("req")
    pair_count = devices // 2
    expert_count = devices // 4
    capacity = min(half_rows, 3 * tok_rows // (2 * expert_count))
    partial_out = jnp.dot(attn_heads, w_out, preferred_element_type=jnp.float32)
    state = residual_in.astype(jnp.float32) + lax.psum_scatter(
        partial_out.astype(jnp.bfloat16), "tp", scatter_dimension=1, tiled=True
    ).astype(jnp.float32)
    router_full = router.astype(jnp.float32)
    square_sum = lax.psum(jnp.sum(state * state, axis=1), "tp")
    inverse = lax.rsqrt(square_sum / full_width + epsilon)[:, None]
    normed = state * inverse * gain_attn
    logits = lax.psum(jnp.dot(normed, router_full, precision=lax.Precision.HIGHEST), "tp")
    normed_bf = normed.astype(jnp.bfloat16)
    expert_range = jnp.arange(expert_count, dtype=jnp.int32)
    match_table = expert_ids[:, :, None] == expert_range
    chosen = jnp.sum(match_table.astype(jnp.float32) * logits[:, None, :], axis=2)
    weights = jax.nn.sigmoid(chosen - chosen[:, ::-1])
    row_index = jnp.arange(tok_rows, dtype=jnp.int32)
    live_rows = row_index < tok_rows - lengths[0, lengths.shape[1] - 1]
    held_table = (placement[:, None] == expert_range).astype(jnp.int32)
    earlier = jnp.cumsum(held_table, axis=0) - held_table
    pair_range = jnp.arange(pair_count, dtype=jnp.int32)[:, None]
    first_pair = jnp.sum(pair_range * held_table * (earlier == 0).astype(jnp.int32), axis=0)
    second_pair = jnp.sum(pair_range * held_table * (earlier == 1).astype(jnp.int32), axis=0)
    upper_half = (row_index >= half_rows)[:, None, None]
    owner_table = jnp.where(upper_half, second_pair, first_pair)
    id_hot = match_table.astype(jnp.int32) * live_rows[:, None, None].astype(jnp.int32)
    target_pair = jnp.sum(id_hot * owner_table, axis=2)
    halves_hot = id_hot.reshape(2, tok_rows, expert_count)
    running = jnp.cumsum(halves_hot, axis=1) - halves_hot
    position = jnp.sum(running * halves_hot, axis=2).reshape(tok_rows, 2)
    slot_index = jnp.where(
        live_rows[:, None], target_pair * capacity + position, pair_count * capacity
    ).reshape(-1)
    source = lax.all_gather(normed_bf, "tp", axis=1, tiled=True)
    feature_dim = source.shape[1]
    sendable = jnp.zeros((pair_count * capacity + 1, feature_dim), jnp.bfloat16)
    sendable = sendable.at[slot_index].set(jnp.repeat(source, 2, axis=0))
    per_pair = sendable[: pair_count * capacity].reshape(pair_count, 1, capacity, feature_dim)
    outgoing = jnp.broadcast_to(per_pair, (pair_count, 2, capacity, feature_dim)).reshape(
        devices, capacity, feature_dim
    )
    gate_weights = w_gate_up[0, 0]
    up_weights = w_gate_up[0, 1]
    down_weights = w_down[0]
    arrived = lax.all_to_all(outgoing, "req", split_axis=0, concat_axis=0, tiled=True)
    source_count = arrived.shape[0]
    slot_count = arrived.shape[1]
    flat_rows = arrived.reshape(source_count * slot_count, full_width)
    gate_proj = jnp.dot(flat_rows, gate_weights, preferred_element_type=jnp.float32)
    up_proj = jnp.dot(flat_rows, up_weights, preferred_element_type=jnp.float32)
    activ = (jax.nn.silu(gate_proj) * up_proj).astype(jnp.bfloat16)
    down_part = jnp.dot(activ, down_weights, preferred_element_type=jnp.float32)
    reduced = lax.psum_scatter(
        down_part.astype(jnp.bfloat16), "tp", scatter_dimension=1, tiled=True
    ).astype(jnp.float32)
    returned = lax.all_to_all(
        reduced.reshape(source_count, slot_count, feat_width).astype(jnp.bfloat16),
        "req",
        split_axis=0,
        concat_axis=0,
        tiled=True,
    ).astype(jnp.float32)
    both_halves = (
        returned.reshape(pair_count, 2, capacity, feat_width)
        .sum(axis=1)
        .reshape(pair_count * capacity, feat_width)
    )
    padded = jnp.concatenate([both_halves, jnp.zeros((1, feat_width), jnp.float32)], axis=0)
    gathered_rows = padded[slot_index].reshape(tok_rows, 2, feat_width)
    mixture = gathered_rows[:, 0] * weights[:, 0:1] + gathered_rows[:, 1] * weights[:, 1:2]
    combined = state + mixture
    final_sum = lax.psum(jnp.sum(combined * combined, axis=1), "tp")
    final_scale = lax.rsqrt(final_sum / full_width + epsilon)[:, None]
    return (
        combined.astype(jnp.bfloat16),
        (combined * final_scale * gain_final).astype(jnp.bfloat16),
    )


def solution(mesh):
    placed = (
        P("req", "tp"),
        P("req", "tp"),
        P("tp", None),
        P("tp"),
        P("tp", None),
        P("req", None),
        P("req", None),
        P(),
        P("req", None, None, "tp"),
        P("req", "tp", None),
        P("tp"),
    )
    return jax.shard_map(
        on_device,
        mesh=mesh,
        in_specs=placed,
        out_specs=(P("req", "tp"), P("req", "tp")),
        check_vma=False,
    )
```

profile of v0, /device:TPU:15, one launch (start us, length us, event | category | flops | bytes accessed | tf_op | source)
XLA Modules:
  0.0 361.8 jit_solution(11574256559749344375)
XLA Ops:
  7.2 0.0 copy-start
  7.2 0.0 copy-start.10
  7.2 0.0 copy-start.5
  7.2 0.0 copy-start.8
  7.2 0.0 copy-start.2
  7.2 0.0 copy-start.6
  7.2 0.0 reduce-scatter.3.cloned.1.call-start
  7.3 0.8 copy-done
  8.1 5.6 %convolution_convert_fusion = bf16[128,4096]{1,0:T(8,128)(2,1)} fusion(bf16[128,1024]{1,0:T(8,128)(2,1)S(1)} %copy-done, bf16[1024,4096]{1,0:T(8,128)(2,1)} %param.13), kind=kOutput, calls=%fused_computation.13 | convolution fusion | flops 1074266112 | bytes 9699328 | tf_op jit(solution)/shard_map/dot_general | solution.py:30
  13.8 0.0 reduce-scatter.3.cloned.1.call-update
  13.8 0.0 all-gather.2.cloned.1.call-start
  13.8 0.0 copy-done.10
  13.8 0.6 slice.24
  15.1 0.1 mul.146
  15.2 0.1 mul.147
  15.3 0.0 copy-done.5
  15.3 0.1 copy.21
  15.4 0.1 eq.54
  15.6 0.0 copy-done.8
  15.6 0.1 fusion.24
  15.8 8.5 %reduce-scatter.3.cloned.1.call-done = bf16[128,2048]{1,0:T(8,128)(2,1)} async-done(((bf16[128,4096]{1,0:T(8,128)(2,1)}), bf16[128,2048]{1,0:T(8,128)(2,1)}) %reduce-scatter.3.cloned.1.call-update) | async-done | bytes 524304 | tf_op jit(solution)/shard_map/reduce_scatter | solution.py:31
  24.3 0.0 copy-done.2
  24.3 1.3 multiply_reduce_fusion.1
  25.6 2.5 psum.21
  28.1 0.0 copy-done.6
  28.1 2.0 fusion.20
  30.1 0.0 all-gather.2.cloned.1.call-update
  30.1 0.0 reduce-scatter.5.cloned.1.call-start
  30.2 0.2 reduce_window_sum.23
  30.4 0.2 reduce_window_sum.22
  30.6 0.1 select_reduce_fusion.2
  30.7 0.1 broadcast_select_fusion
  30.8 0.1 copy.20
  30.9 0.1 mul.145
  31.1 0.1 broadcast_in_dim.60
  31.2 0.1 broadcast_in_dim.61
  31.3 0.2 fusion.23
  31.6 8.9 %all-gather.2.cloned.1.call-done = bf16[128,4096]{1,0:T(8,128)(2,1)} async-done(((bf16[128,2048]{1,0:T(8,128)(2,1)}), bf16[128,4096]{1,0:T(8,128)(2,1)}) %all-gather.2.cloned.1.call-update) | async-done | bytes 1048592 | tf_op jit(solution)/shard_map/all_gather | solution.py:61
  40.5 3.3 broadcast_in_dim.66
  43.8 2.2 reshape.163
  46.1 5.5 %scatter_custom_fusion = bf16[385,4096]{1,0:T(8,128)(2,1)S(1)} fusion(s32[256]{0:T(256)S(1)} %bitcast.57, bf16[256,4096]{1,0:T(8,128)(2,1)} %reshape.163, bf16[]{:T(256)} %constant.14.clone.1), kind=kCustom, calls=%fused_computation.14 | custom fusion | bytes 3154432 | tf_op jit(solution)/shard_map/scatter | solution.py:64
  51.6 0.2 slice.34
  51.8 0.9 broadcast_in_dim.68
  52.7 142.4 %all_to_all.10 = bf16[16,48,4096]{2,1,0:T(8,128)(2,1)S(1)} all-to-all(bf16[16,48,4096]{2,1,0:T(8,128)(2,1)S(1)} %bitcast.50), channel_id=1, replica_groups=mesh['req'=16,'tp'=2] {'req'}, dimensions={0} | all-to-all | bytes 12582912 | tf_op jit(solution)/shard_map/all_to_all | solution.py:72
  195.1 17.9 %fusion.4 = f32[768,1792]{1,0:T(8,128)} fusion(bf16[768,4096]{1,0:T(8,128)(2,1)S(1)} %bitcast.53, bf16[1,2,4096,1792]{3,2,1,0:T(8,128)(2,1)} %param.19), kind=kOutput, calls=%fused_computation.6 | convolution fusion | flops 11274289152 | bytes 26476544 | tf_op jit(solution)/shard_map/dot_general | solution.py:76
  213.1 17.4 %multiply_convert_fusion = bf16[768,1792]{1,0:T(8,128)(2,1)S(1)} fusion(f32[768,1792]{1,0:T(8,128)} %fusion.4, bf16[768,4096]{1,0:T(8,128)(2,1)S(1)} %bitcast.54, bf16[1,2,4096,1792]{3,2,1,0:T(8,128)(2,1)} %param.19), kind=kOutput, calls=%fused_computation.12 | convolution fusion | flops 11282546688 | bytes 29229056 | tf_op jit(solution)/shard_map/dot_general | solution.py:77
  230.5 16.7 %fusion.8 = bf16[768,4096]{1,0:T(8,128)(2,1)} fusion(bf16[768,1792]{1,0:T(8,128)(2,1)S(1)} %multiply_convert_fusion, bf16[1,1792,4096]{2,1,0:T(8,128)(2,1)} %param.20), kind=kOutput, calls=%fused_computation.10 | convolution fusion | flops 11277434880 | bytes 23724032 | tf_op jit(solution)/shard_map/dot_general | solution.py:79
  247.1 0.0 reduce-scatter.5.cloned.1.call-update
  247.2 16.3 %reduce-scatter.5.cloned.1.call-done = bf16[768,2048]{1,0:T(8,128)(2,1)} async-done(((bf16[768,4096]{1,0:T(8,128)(2,1)}), bf16[768,2048]{1,0:T(8,128)(2,1)}) %reduce-scatter.5.cloned.1.call-update) | async-done | bytes 3145744 | tf_op jit(solution)/shard_map/reduce_scatter | solution.py:80
  263.4 6.4 %all-to-all-start.1 = ((bf16[16,48,2048]{2,1,0:T(8,128)(2,1)}), bf16[16,48,2048]{2,1,0:T(8,128)(2,1)S(1)}, u32[]{:S(2)}, u32[]{:S(2)}) async-start(bf16[16,48,2048]{2,1,0:T(8,128)(2,1)} %bitcast.55), calls=%async_computation.3 | async-start | bytes 6291456 | tf_op jit(solution)/shard_map/all_to_all | solution.py:83
  269.9 0.0 copy-done.9
  269.9 2.0 fusion.19
  271.9 2.9 psum.22
  274.8 67.0 %all-to-all-done.1 = bf16[16,48,2048]{2,1,0:T(8,128)(2,1)S(1)} async-done(((bf16[16,48,2048]{2,1,0:T(8,128)(2,1)}), bf16[16,48,2048]{2,1,0:T(8,128)(2,1)S(1)}, u32[]{:S(2)}, u32[]{:S(2)}) %all-to-all-start.1) | async-done | bytes 3145760 | tf_op jit(solution)/shard_map/all_to_all | solution.py:83
  341.8 0.7 convert_reduce_fusion
  342.5 0.3 concatenate.3
  342.8 2.7 gather_fusion
  345.5 2.6 reshape.148
  348.1 1.6 fusion.28
  349.7 0.0 copy-done.3
  349.7 0.0 copy-done.4
  349.8 0.9 multiply_reduce_fusion
  350.7 3.4 psum.23
  354.1 1.1 multiply_convert_fusion.1
  (21 shorter events, 0.2 us)
Async XLA Ops:
  7.2 1.0 copy-start
  7.2 6.7 %copy-start.10 = (s32[1,5]{1,0:T(1,128)S(1)}, s32[1,5]{1,0:T(1,128)}, u32[]{:S(2)}) copy-start(s32[1,5]{1,0:T(1,128)} %param.17) | copy-start | bytes 64
  7.2 8.1 %copy-start.5 = (s32[128,2]{0,1:T(2,128)S(1)}, s32[128,2]{0,1:T(2,128)}, u32[]{:S(2)}) copy-start(s32[128,2]{0,1:T(2,128)} %param.16) | copy-start | bytes 3076
  7.2 8.4 %copy-start.8 = (s32[8]{0:T(128)S(1)}, s32[8]{0:T(128)}, u32[]{:S(2)}) copy-start(s32[8]{0:T(128)} %param.18) | copy-start | bytes 100
  7.2 17.1 %copy-start.2 = (bf16[128,2048]{1,0:T(8,128)(2,1)S(1)}, bf16[128,2048]{1,0:T(8,128)(2,1)}, u32[]{:S(2)}) copy-start(bf16[128,2048]{1,0:T(8,128)(2,1)} %param.12) | copy-start | bytes 1572868
  7.2 20.8 %copy-start.6 = (f32[2048]{0:T(1024)S(1)}, f32[2048]{0:T(1024)}, u32[]{:S(2)}) copy-start(f32[2048]{0:T(1024)} %param.14) | copy-start | bytes 24580
  7.2 17.1 %reduce-scatter.3.cloned.1.call-start = ((), (), s32[]{:S(2)}) async-start(), calls=%async_computation.4 | async-start | bytes 1572864 | tf_op jit(solution)/shard_map/reduce_scatter | solution.py:31
  13.8 26.7 %all-gather.2.cloned.1.call-start = ((), (), s32[]{:S(2)}) async-start(), calls=%async_computation.5 | async-start | bytes 1572864 | tf_op jit(solution)/shard_map/all_gather | solution.py:61
  30.1 233.3 %reduce-scatter.5.cloned.1.call-start = ((), (), s32[]{:S(2)}) async-start(), calls=%async_computation.6 | async-start | bytes 9437184 | tf_op jit(solution)/shard_map/reduce_scatter | solution.py:80
  247.1 22.7 %copy-start.9 = (bf16[2048,4]{0,1:T(4,128)(2,1)S(1)}, bf16[2048,4]{0,1:T(4,128)(2,1)}, u32[]{:S(2)}) copy-start(bf16[2048,4]{0,1:T(4,128)(2,1)} %param.15) | copy-start | bytes 49156
  263.4 78.3 %all-to-all-start.1 = ((bf16[16,48,2048]{2,1,0:T(8,128)(2,1)}), bf16[16,48,2048]{2,1,0:T(8,128)(2,1)S(1)}, u32[]{:S(2)}, u32[]{:S(2)}) async-start(bf16[16,48,2048]{2,1,0:T(8,128)(2,1)} %bitcast.55), calls=%async_computation.3 | async-start | bytes 6291456 | tf_op jit(solution)/shard_map/all_to_all | solution.py:83
  345.5 4.2 %copy-start.3 = (bf16[128,2048]{1,0:T(8,128)(2,1)S(1)}, bf16[128,2048]{1,0:T(8,128)(2,1)}, u32[]{:S(2)}) copy-start(bf16[128,2048]{1,0:T(8,128)(2,1)} %param.12) | copy-start | bytes 1572868
  345.5 4.3 %copy-start.4 = (bf16[128,2048]{1,0:T(8,128)(2,1)S(1)}, bf16[128,2048]{1,0:T(8,128)(2,1)}, u32[]{:S(2)}) copy-start(bf16[128,2048]{1,0:T(8,128)(2,1)} %reduce-scatter.3.cloned.1.call-done) | copy-start | bytes 1572868
  345.5 8.6 %copy-start.7 = (f32[2048]{0:T(1024)S(1)}, f32[2048]{0:T(1024)}, u32[]{:S(2)}) copy-start(f32[2048]{0:T(1024)} %param.21) | copy-start | bytes 24580
  345.5 9.8 %copy-start.1 = (bf16[128,1024]{1,0:T(8,128)(2,1)S(1)}, bf16[128,1024]{1,0:T(8,128)(2,1)}, u32[]{:S(2)}) copy-start(bf16[128,1024]{1,0:T(8,128)(2,1)} %param.11) | copy-start | bytes 786436
Sparse Core Ops, SparseCore 0:
  13.9 10.3 reduce-scatter.2
  30.3 10.2 all-gather.1
  247.3 16.1 reduce-scatter.4
where the time goes:
time: 362 us
  blocking collectives  151 us (42%)
  waiting for transfers between devices  101 us (28%)
  matrix products  59.6 us (16%)
  local copies, waits for them, and re-layouts  21.8 us (6%)
  between operations  14.6 us (4%)
  other arithmetic  7.21 us (2%)
  starting transfers between devices  6.53 us (2%)
    all_to_all x1, blocking collectives, on_device(): lax.all_to_all(outgoing, 'req', split_axis=0, concat_axis=0, tiled=True)  142 us
    all_to_all x1, waiting for transfers between devices, on_device(): lax.all_to_all(reduced.reshape(source_count, slot_count, feat_width).asty...  67 us
    dot_general x1, matrix products, on_device(): jnp.dot(flat_rows, gate_weights, preferred_element_type=jnp.float32)  17.9 us
    dot_general x1, matrix products, on_device(): up_proj = jnp.dot(flat_rows, up_weights, preferred_element_type=jnp.float32)  17.4 us
    dot_general x1, matrix products, on_device(): down_part = jnp.dot(activ, down_weights, preferred_element_type=jnp.float32)  16.7 us
    reduce_scatter x1, waiting for transfers between devices, on_device(): lax.psum_scatter(down_part.astype(jnp.bfloat16), 'tp', scatter_dimension=...  16.3 us
    all_gather x1, waiting for transfers between devices, on_device(): source = lax.all_gather(normed_bf, 'tp', axis=1, tiled=True)  8.95 us
    reduce_scatter x1, waiting for transfers between devices, on_device(): lax.psum_scatter(partial_out.astype(jnp.bfloat16), 'tp', scatter_dimensio...  8.53 us
  transfers between devices with their start and end apart: 4, of which 4 were waited for; matrix products, arithmetic and copies ran while one was open for 1% of the time, Pallas kernels for 0%

commit v1 on v0

v1 whole, which is shorter than its diff:
```python
import jax
import jax.numpy as jnp
from jax import lax
from jax.sharding import PartitionSpec as P

epsilon = 1e-05


def pair_shift(value, k, devices):
    return lax.ppermute(value, "req", [(i, 2 * ((i // 2) ^ k) + i % 2) for i in range(devices)])


def side_swap(value, devices):
    return lax.ppermute(value, "req", [(i, i ^ 1) for i in range(devices)])


def core_swap(value):
    return lax.ppermute(value, "tp", [(0, 1), (1, 0)])


def core_sum(value):
    if lax.axis_size("tp") == 2:
        return value + core_swap(value)
    return lax.psum(value, "tp")


def core_gather(value):
    if lax.axis_size("tp") != 2:
        return lax.all_gather(value, "tp", axis=1, tiled=True)
    other = core_swap(value)
    first = lax.axis_index("tp") == 0
    return jnp.concatenate([jnp.where(first, value, other), jnp.where(first, other, value)], axis=1)


def core_scatter(value):
    if lax.axis_size("tp") != 2:
        return lax.psum_scatter(
            value.astype(jnp.bfloat16), "tp", scatter_dimension=1, tiled=True
        ).astype(jnp.float32)
    width = value.shape[1] // 2
    first = lax.axis_index("tp") == 0
    low, high = value[:, :width], value[:, width:]
    away = jnp.where(first, high, low).astype(jnp.bfloat16)
    return jnp.where(first, low, high) + core_swap(away).astype(jnp.float32)


def on_device(
    attn_heads,
    residual_in,
    w_out,
    gain_attn,
    router,
    expert_ids,
    lengths,
    placement,
    w_gate_up,
    w_down,
    gain_final,
):
    tok_rows = attn_heads.shape[0]
    half_rows = tok_rows // 2
    feat_width = residual_in.shape[1]
    full_width = feat_width * lax.axis_size("tp")
    devices = lax.axis_size("req")
    pair_count = devices // 2
    expert_count = devices // 4
    capacity = min(half_rows, 3 * tok_rows // (2 * expert_count))
    own_pair = lax.axis_index("req") // 2

    expert_range = jnp.arange(expert_count, dtype=jnp.int32)
    row_index = jnp.arange(tok_rows, dtype=jnp.int32)
    live_rows = row_index < tok_rows - lengths[0, lengths.shape[1] - 1]
    held_table = (placement[:, None] == expert_range).astype(jnp.int32)
    pair_range = jnp.arange(pair_count, dtype=jnp.int32)[:, None]
    first_pair = jnp.min(jnp.where(held_table > 0, pair_range, pair_count), axis=0)
    second_pair = jnp.max(jnp.where(held_table > 0, pair_range, -1), axis=0)
    upper_half = (row_index >= half_rows)[:, None, None]
    block_table = jnp.where(upper_half, second_pair ^ own_pair, first_pair ^ own_pair)
    match_table = expert_ids[:, :, None] == expert_range
    id_hot = match_table & live_rows[:, None, None]
    named = jnp.sum(id_hot.astype(jnp.float32), axis=1)
    before = (row_index[:, None] > row_index[None, :]) & (
        (row_index[:, None] >= half_rows) == (row_index[None, :] >= half_rows)
    )
    running = jnp.dot(
        before.astype(jnp.bfloat16), named.astype(jnp.bfloat16), preferred_element_type=jnp.float32
    ).astype(jnp.int32)
    slot_index = jnp.sum(
        jnp.where(id_hot, block_table * capacity + running[:, None, :], 0), axis=2
    )
    slot_index = jnp.where(live_rows[:, None], slot_index, pair_count * capacity)
    slot_range = jnp.arange(pair_count * capacity, dtype=jnp.int32)
    place_hot = (
        (slot_index[:, 0][None, :] == slot_range[:, None])
        | (slot_index[:, 1][None, :] == slot_range[:, None])
    ).astype(jnp.bfloat16)

    partial_out = jnp.dot(attn_heads, w_out, preferred_element_type=jnp.float32)
    state = residual_in.astype(jnp.float32) + core_scatter(partial_out)
    square_sum = core_sum(jnp.sum(state * state, axis=1, keepdims=True))
    inverse = lax.rsqrt(square_sum / full_width + epsilon)
    scaled = state * gain_attn
    normed_bf = (scaled * inverse).astype(jnp.bfloat16)

    outgoing = jnp.dot(place_hot, normed_bf, preferred_element_type=jnp.float32).astype(jnp.bfloat16)
    outgoing = outgoing.reshape(pair_count, capacity, feat_width)
    chunks = [[k for k in range(pair_count) if (k // 2) % 2 == c] for c in range(2)]
    arrived = {}
    for chunk in chunks:
        for k in chunk:
            arrived[k] = pair_shift(outgoing[k], k, devices) if k else outgoing[k]

    logits = inverse * core_sum(
        jnp.dot(scaled, router.astype(jnp.float32), precision=lax.Precision.HIGHEST)
    )
    chosen = jnp.sum(match_table.astype(jnp.float32) * logits[:, None, :], axis=2)
    weights = jax.nn.sigmoid(chosen - chosen[:, ::-1])
    mix = jnp.where(slot_index[:, 0:1] == slot_range, weights[:, 0:1], 0.0) + jnp.where(
        slot_index[:, 1:2] == slot_range, weights[:, 1:2], 0.0
    )
    mix_high = lax.reduce_precision(mix, 8, 7)
    mix_low = (mix - mix_high).astype(jnp.bfloat16)
    mix_high = mix_high.astype(jnp.bfloat16)

    mixture = jnp.zeros_like(state)
    for chunk in chunks:
        groups = [chunk[i : i + 2] for i in range(0, len(chunk), 2)]
        mine = [jnp.concatenate([arrived[k] for k in group], axis=0) for group in groups]
        others = [side_swap(value, devices) for value in mine]
        rows = jnp.concatenate([core_gather(value) for value in mine + others], axis=0)
        gate_proj = jnp.dot(rows, w_gate_up[0, 0], preferred_element_type=jnp.float32)
        up_proj = jnp.dot(rows, w_gate_up[0, 1], preferred_element_type=jnp.float32)
        activ = (jax.nn.silu(gate_proj) * up_proj).astype(jnp.bfloat16)
        down_part = jnp.dot(activ, w_down[0], preferred_element_type=jnp.float32)
        reduced = core_scatter(down_part)
        near = len(chunk) * capacity
        away = reduced[near:].astype(jnp.bfloat16)
        step = 2 * capacity
        back = {}
        for g in reversed(range(len(groups))):
            swapped = side_swap(away[g * step : (g + 1) * step], devices).astype(jnp.float32)
            total = (reduced[g * step : (g + 1) * step] + swapped).astype(jnp.bfloat16)
            for j, k in enumerate(groups[g]):
                block = total[j * capacity : (j + 1) * capacity]
                back[k] = pair_shift(block, k, devices) if k else block
        returned = jnp.concatenate([back[k] for k in chunk], axis=0)
        pick = lambda table: jnp.concatenate(
            [table[:, k * capacity : (k + 1) * capacity] for k in chunk], axis=1
        )
        mixture += jnp.dot(pick(mix_high), returned, preferred_element_type=jnp.float32)
        mixture += jnp.dot(pick(mix_low), returned, preferred_element_type=jnp.float32)

    combined = state + mixture
    final_sum = core_sum(jnp.sum(combined * combined, axis=1, keepdims=True))
    final_scale = lax.rsqrt(final_sum / full_width + epsilon)
    return (
        combined.astype(jnp.bfloat16),
        (combined * final_scale * gain_final).astype(jnp.bfloat16),
    )


def solution(mesh):
    placed = (
        P("req", "tp"),
        P("req", "tp"),
        P("tp", None),
        P("tp"),
        P("tp", None),
        P("req", None),
        P("req", None),
        P(),
        P("req", None, None, "tp"),
        P("req", "tp", None),
        P("tp"),
    )
    return jax.shard_map(
        on_device,
        mesh=mesh,
        in_specs=placed,
        out_specs=(P("req", "tp"), P("req", "tp")),
        check_vma=False,
    )
```

time: 362 us -> 224 us (0.62)
  blocking collectives: 151 us -> 0 us
  starting transfers between devices: 6.53 us -> 34.2 us
  matrix products: 59.6 us -> 78.8 us
  local copies, waits for them, and re-layouts: 21.8 us -> 3.33 us
  between operations: 14.6 us -> 1.79 us
    all_to_all x1 -> x0, blocking collectives: 142 us -> none  [on_device(): lax.all_to_all(outgoing, 'req', split_axis=0, concat_axis=0, tiled=True)]
    ppermute x0 -> x36, waiting for transfers between devices: none -> 98.9 us  [the longest x8 51.2 us: side_swap(): return lax.ppermute(value, 'req', [(i, i ^ 1) for i in range(devices)])]
    all_to_all x1 -> x0, waiting for transfers between devices: 67 us -> none  [on_device(): lax.all_to_all(reduced.reshape(source_count, slot_count, feat_width).asty...]
    ppermute x0 -> x36, starting transfers between devices: none -> 34.2 us  [the longest x14 17.1 us: core_swap(): return lax.ppermute(value, 'tp', [(0, 1), (1, 0)])]
    reduce_scatter x2 -> x0, waiting for transfers between devices: 24.8 us -> none  [the longest x1 16.3 us: on_device(): lax.psum_scatter(down_part.astype(jnp.bfloat16), 'tp', scatter_dimension=...]
    dot_general x4 -> x13, matrix products: 54 us -> 74.2 us  [the longest x2 25.5 us: on_device(): up_proj = jnp.dot(rows, w_gate_up[0, 1], preferred_element_type=jnp.float32)]
    all_gather x1 -> x0, waiting for transfers between devices: 8.95 us -> none  [on_device(): source = lax.all_gather(normed_bf, 'tp', axis=1, tiled=True)]
    psum x3 -> x0, blocking collectives: 8.74 us -> none  [the longest x1 3.41 us: on_device(): final_sum = lax.psum(jnp.sum(combined * combined, axis=1), 'tp')]
  transfers between devices with their start and end apart: 4 -> 36, of which waited for: 4 -> 19; matrix products, arithmetic and copies ran while one was open for 1% -> 19% of each run, Pallas kernels for 0% -> 0%
where the time goes in v1:
time: 224 us
  waiting for transfers between devices  98.9 us (44%)
  matrix products  78.8 us (35%)
  starting transfers between devices  34.2 us (15%)
  other arithmetic  7.06 us (3%)
  local copies, waits for them, and re-layouts  3.33 us (1%)
    ppermute x8, waiting for transfers between devices, side_swap(): return lax.ppermute(value, 'req', [(i, i ^ 1) for i in range(devices)])  51.2 us
    ppermute x14, waiting for transfers between devices, pair_shift(): lax.ppermute(value, 'req', [(i, 2 * (i // 2 ^ k) + i % 2) for i in range(...  44.6 us
    dot_general x2, matrix products, on_device(): up_proj = jnp.dot(rows, w_gate_up[0, 1], preferred_element_type=jnp.float32)  25.5 us
    dot_general x2, matrix products, on_device(): jnp.dot(rows, w_gate_up[0, 0], preferred_element_type=jnp.float32)  25.1 us
    dot_general x2, matrix products, on_device(): down_part = jnp.dot(activ, w_down[0], preferred_element_type=jnp.float32)  20.4 us
    ppermute x14, starting transfers between devices, core_swap(): return lax.ppermute(value, 'tp', [(0, 1), (1, 0)])  17.1 us
    ppermute x14, starting transfers between devices, pair_shift(): lax.ppermute(value, 'req', [(i, 2 * (i // 2 ^ k) + i % 2) for i in range(...  11.9 us
    ppermute x8, starting transfers between devices, side_swap(): return lax.ppermute(value, 'req', [(i, i ^ 1) for i in range(devices)])  5.23 us
  transfers between devices with their start and end apart: 36, of which 19 were waited for; matrix products, arithmetic and copies ran while one was open for 19% of the time, Pallas kernels for 0%

profile of v1, /device:TPU:15, one launch (start us, length us, event | category | flops | bytes accessed | tf_op | source)
XLA Modules:
  0.0 224.1 jit_solution(11956284729796698348)
XLA Ops:
  0.7 0.9 copy-done
  1.6 4.7 %fusion.75 = f32[128,4096]{1,0:T(8,128)S(1)} fusion(bf16[128,1024]{1,0:T(8,128)(2,1)S(1)} %copy-done, bf16[1024,4096]{1,0:T(8,128)(2,1)} %param.13), kind=kOutput, calls=%fused_computation.151 | convolution fusion | flops 1073741824 | bytes 10747904 | tf_op jit(solution)/shard_map/dot_general | solution.py:98
  6.4 0.7 collective-permute-start
  7.1 0.6 slice.173
  8.8 1.6 multiply_reduce_fusion.1
  10.4 0.4 collective-permute-start.1
  10.8 0.6 fusion.22
  11.6 1.0 collective-permute-done.2
  12.9 0.6 convolution_convert_fusion
  13.7 2.4 %collective-permute-start.5 = (bf16[48,2048]{1,0:T(8,128)(2,1)S(1)}, bf16[48,2048]{1,0:T(8,128)(2,1)S(1)}, u32[]{:S(2)}, u32[]{:S(2)}) collective-permute-start(bf16[48,2048]{1,0:T(8,128)(2,1)S(1)} %get-tuple-element.24), channel_id=1, source_target_pairs={{0,16},{2,18},{4,20},{6,22},{8,24},{10,26},{12,28},{14,30},{16,0},... | collective-permute-start | bytes 589832 | tf_op jit(solution)/shard_map/ppermute | solution.py:10
  16.1 1.2 collective-permute-start.3
  17.6 1.2 collective-permute-start.19
  19.0 10.1 %collective-permute-done.5 = bf16[48,2048]{1,0:T(8,128)(2,1)S(1)} collective-permute-done((bf16[48,2048]{1,0:T(8,128)(2,1)S(1)}, bf16[48,2048]{1,0:T(8,128)(2,1)S(1)}, u32[]{:S(2)}, u32[]{:S(2)}) %collective-permute-start.5) | collective-permute-done | bytes 196640 | tf_op jit(solution)/shard_map/ppermute | solution.py:10
  29.1 4.2 %collective-permute-done.6 = bf16[48,2048]{1,0:T(8,128)(2,1)S(1)} collective-permute-done((bf16[48,2048]{1,0:T(8,128)(2,1)S(1)}, bf16[48,2048]{1,0:T(8,128)(2,1)S(1)}, u32[]{:S(2)}, u32[]{:S(2)}) %collective-permute-start.6) | collective-permute-done | bytes 196640 | tf_op jit(solution)/shard_map/ppermute | solution.py:10
  33.3 0.3 collective-permute-start.10
  33.8 8.9 %collective-permute-start.7 = (bf16[96,2048]{1,0:T(8,128)(2,1)S(1)}, bf16[96,2048]{1,0:T(8,128)(2,1)S(1)}, u32[]{:S(2)}, u32[]{:S(2)}) collective-permute-start(bf16[96,2048]{1,0:T(8,128)(2,1)S(1)} %constant_dynamic-update-slice_fusion), channel_id=1, source_target_pairs={{0,1},{1,0},{2,3},{3,2},{4,5},{5,4},{6,7},{7,6},{8,9},{9,8},{10,11... | collective-permute-start | bytes 1179656 | tf_op jit(solution)/shard_map/ppermute | solution.py:18
  42.7 3.2 %collective-permute-done.21 = bf16[48,2048]{1,0:T(8,128)(2,1)S(1)} collective-permute-done((bf16[48,2048]{1,0:T(8,128)(2,1)S(1)}, bf16[48,2048]{1,0:T(8,128)(2,1)S(1)}, u32[]{:S(2)}, u32[]{:S(2)}) %collective-permute-start.21) | collective-permute-done | bytes 196640 | tf_op jit(solution)/shard_map/ppermute | solution.py:10
  45.9 0.9 collective-permute-start.20
  46.9 3.3 %collective-permute-done.22 = bf16[48,2048]{1,0:T(8,128)(2,1)S(1)} collective-permute-done((bf16[48,2048]{1,0:T(8,128)(2,1)S(1)}, bf16[48,2048]{1,0:T(8,128)(2,1)S(1)}, u32[]{:S(2)}, u32[]{:S(2)}) %collective-permute-start.22) | collective-permute-done | bytes 196640 | tf_op jit(solution)/shard_map/ppermute | solution.py:10
  50.1 0.3 collective-permute-start.24
  50.4 0.8 collective-permute-start.23
  51.3 1.3 collective-permute-start.26
  52.6 0.3 collective-permute-start.8
  53.0 0.6 collective-permute-start.4
  53.7 23.5 %collective-permute-done.8 = bf16[96,2048]{1,0:T(8,128)(2,1)S(1)} collective-permute-done((bf16[96,2048]{1,0:T(8,128)(2,1)S(1)}, bf16[96,2048]{1,0:T(8,128)(2,1)S(1)}, u32[]{:S(2)}, u32[]{:S(2)}) %collective-permute-start.8) | collective-permute-done | bytes 393248 | tf_op jit(solution)/shard_map/ppermute | solution.py:14
  77.2 1.3 collective-permute-start.11
  78.5 0.5 collective-permute-start.25
  79.3 0.5 collective-permute-done.11
  80.0 0.5 collective-permute-done.9
  80.5 12.5 %fusion.10 = f32[384,1792]{1,0:T(8,128)} fusion(bf16[1,2,4096,1792]{3,2,1,0:T(8,128)(2,1)} %param.19, bf16[96,2048]{1,0:T(8,128)(2,1)S(1)} %get-tuple-element.37, bf16[96,2048]{1,0:T(8,128)(2,1)S(1)} %get-tuple-element.36, bf16[96,2048]{1,0:T(8,128)(2,1)S(1)} %get-tuple-element.35, bf16[96,2048]{1,0:T(8,128)(2,1)S(1)} %get-tuple-element.34, ...), kind=kOutput, calls=%fused_computation.10 | convolution fusion | flops 5662310400 | bytes 20578304 | tf_op jit(solution)/shard_map/dot_general | solution.py:131
  93.1 12.8 %fusion.6 = f32[384,1792]{1,0:T(8,128)} fusion(bf16[1,2,4096,1792]{3,2,1,0:T(8,128)(2,1)} %param.19, bf16[96,2048]{1,0:T(8,128)(2,1)S(1)} %get-tuple-element.37, bf16[96,2048]{1,0:T(8,128)(2,1)S(1)} %get-tuple-element.36, bf16[96,2048]{1,0:T(8,128)(2,1)S(1)} %get-tuple-element.35, bf16[96,2048]{1,0:T(8,128)(2,1)S(1)} %get-tuple-element.34, ...), kind=kOutput, calls=%fused_computation.6 | convolution fusion | flops 5662310400 | bytes 20578304 | tf_op jit(solution)/shard_map/dot_general | solution.py:132
  106.0 12.6 %fusion.8 = f32[384,1792]{1,0:T(8,128)} fusion(bf16[1,2,4096,1792]{3,2,1,0:T(8,128)(2,1)} %param.19, bf16[96,2048]{1,0:T(8,128)(2,1)S(1)} %get-tuple-element.45, bf16[96,2048]{1,0:T(8,128)(2,1)S(1)} %get-tuple-element.44, bf16[96,2048]{1,0:T(8,128)(2,1)S(1)} %get-tuple-element.43, bf16[96,2048]{1,0:T(8,128)(2,1)S(1)} %get-tuple-element.42, ...), kind=kOutput, calls=%fused_computation.8 | convolution fusion | flops 5662310400 | bytes 20578304 | tf_op jit(solution)/shard_map/dot_general | solution.py:131
  118.6 12.7 %fusion.4 = f32[384,1792]{1,0:T(8,128)} fusion(bf16[1,2,4096,1792]{3,2,1,0:T(8,128)(2,1)} %param.19, bf16[96,2048]{1,0:T(8,128)(2,1)S(1)} %get-tuple-element.45, bf16[96,2048]{1,0:T(8,128)(2,1)S(1)} %get-tuple-element.44, bf16[96,2048]{1,0:T(8,128)(2,1)S(1)} %get-tuple-element.43, bf16[96,2048]{1,0:T(8,128)(2,1)S(1)} %get-tuple-element.42, ...), kind=kOutput, calls=%fused_computation.4 | convolution fusion | flops 5662310400 | bytes 20578304 | tf_op jit(solution)/shard_map/dot_general | solution.py:132
  131.3 10.2 %fusion.2 = f32[384,4096]{1,0:T(8,128)S(1)} fusion(bf16[1,1792,4096]{2,1,0:T(8,128)(2,1)} %param.20, f32[384,1792]{1,0:T(8,128)} %fusion.6, f32[384,1792]{1,0:T(8,128)S(1)} %copy-done.8), kind=kOutput, calls=%fused_computation.2 | convolution fusion | flops 5641273344 | bytes 26476544 | tf_op jit(solution)/shard_map/dot_general | solution.py:134
  141.5 0.3 select_convert_fusion.1
  141.8 0.4 collective-permute-start.12
  142.2 1.1 copy-done.9
  143.2 10.2 %fusion = f32[384,4096]{1,0:T(8,128)S(1)} fusion(bf16[1,1792,4096]{2,1,0:T(8,128)(2,1)} %param.20, f32[384,1792]{1,0:T(8,128)} %fusion.4, f32[384,1792]{1,0:T(8,128)S(1)} %copy-done.9), kind=kOutput, calls=%fused_computation | convolution fusion | flops 5641273344 | bytes 26476544 | tf_op jit(solution)/shard_map/dot_general | solution.py:134
  153.4 0.3 select_convert_fusion
  153.7 0.4 collective-permute-start.28
  154.4 1.1 fusion.64
  155.6 0.3 collective-permute-start.13
  155.9 1.2 collective-permute-start.15
  157.2 1.1 fusion.65
  158.4 0.3 collective-permute-start.29
  158.7 1.2 collective-permute-start.32
  160.0 6.3 %collective-permute-done.13 = bf16[96,2048]{1,0:T(8,128)(2,1)S(1)} collective-permute-done((bf16[96,2048]{1,0:T(8,128)(2,1)S(1)}, bf16[96,2048]{1,0:T(8,128)(2,1)S(1)}, u32[]{:S(2)}, u32[]{:S(2)}) %collective-permute-start.13) | collective-permute-done | bytes 393248 | tf_op jit(solution)/shard_map/ppermute | solution.py:14
  166.2 8.4 %collective-permute-done.15 = bf16[96,2048]{1,0:T(8,128)(2,1)S(1)} collective-permute-done((bf16[96,2048]{1,0:T(8,128)(2,1)S(1)}, bf16[96,2048]{1,0:T(8,128)(2,1)S(1)}, u32[]{:S(2)}, u32[]{:S(2)}) %collective-permute-start.15) | collective-permute-done | bytes 393248 | tf_op jit(solution)/shard_map/ppermute | solution.py:14
  174.9 0.6 collective-permute-start.14
  175.6 3.0 %collective-permute-start.17 = (bf16[48,2048]{1,0:T(8,128)(2,1)S(1)}, bf16[48,2048]{1,0:T(8,128)(2,1)S(1)}, u32[]{:S(2)}, u32[]{:S(2)}) collective-permute-start(bf16[48,2048]{1,0:T(8,128)(2,1)S(1)} %get-tuple-element.49), channel_id=1, source_target_pairs={{0,20},{2,22},{4,16},{6,18},{8,28},{10,30},{12,24},{14,26},{16,4},... | collective-permute-start | bytes 589832 | tf_op jit(solution)/shard_map/ppermute | solution.py:10
  178.6 4.5 %collective-permute-done.29 = bf16[96,2048]{1,0:T(8,128)(2,1)S(1)} collective-permute-done((bf16[96,2048]{1,0:T(8,128)(2,1)S(1)}, bf16[96,2048]{1,0:T(8,128)(2,1)S(1)}, u32[]{:S(2)}, u32[]{:S(2)}) %collective-permute-start.29) | collective-permute-done | bytes 393248 | tf_op jit(solution)/shard_map/ppermute | solution.py:14
  183.1 8.4 %collective-permute-done.32 = bf16[96,2048]{1,0:T(8,128)(2,1)S(1)} collective-permute-done((bf16[96,2048]{1,0:T(8,128)(2,1)S(1)}, bf16[96,2048]{1,0:T(8,128)(2,1)S(1)}, u32[]{:S(2)}, u32[]{:S(2)}) %collective-permute-start.32) | collective-permute-done | bytes 393248 | tf_op jit(solution)/shard_map/ppermute | solution.py:14
  191.8 1.7 collective-permute-start.31
  193.6 5.6 %collective-permute-done.30 = bf16[48,2048]{1,0:T(8,128)(2,1)S(1)} collective-permute-done((bf16[48,2048]{1,0:T(8,128)(2,1)S(1)}, bf16[48,2048]{1,0:T(8,128)(2,1)S(1)}, u32[]{:S(2)}, u32[]{:S(2)}) %collective-permute-start.30) | collective-permute-done | bytes 196640 | tf_op jit(solution)/shard_map/ppermute | solution.py:10
  199.4 4.0 %collective-permute-done.31 = bf16[48,2048]{1,0:T(8,128)(2,1)S(1)} collective-permute-done((bf16[48,2048]{1,0:T(8,128)(2,1)S(1)}, bf16[48,2048]{1,0:T(8,128)(2,1)S(1)}, u32[]{:S(2)}, u32[]{:S(2)}) %collective-permute-start.31) | collective-permute-done | bytes 196640 | tf_op jit(solution)/shard_map/ppermute | solution.py:10
  203.4 1.1 collective-permute-start.34
  204.6 14.1 %collective-permute-done.34 = bf16[48,2048]{1,0:T(8,128)(2,1)S(1)} collective-permute-done((bf16[48,2048]{1,0:T(8,128)(2,1)S(1)}, bf16[48,2048]{1,0:T(8,128)(2,1)S(1)}, u32[]{:S(2)}, u32[]{:S(2)}) %collective-permute-start.34) | collective-permute-done | bytes 196640 | tf_op jit(solution)/shard_map/ppermute | solution.py:10
  218.7 0.4 fusion.43
  219.1 0.4 fusion.47
  219.5 0.4 fusion.34
  219.9 0.6 multiply_reduce_fusion
  220.5 1.7 collective-permute-start.35
  222.2 0.8 collective-permute-done.35
  223.0 1.1 multiply_convert_fusion.4
  (95 shorter events, 3.8 us)
Async XLA Ops:
  0.6 1.0 copy-start
  1.6 5.6 %copy-start.6 = (s32[1,5]{1,0:T(1,128)S(1)}, s32[1,5]{1,0:T(1,128)}, u32[]{:S(2)}) copy-start(s32[1,5]{1,0:T(1,128)} %param.17) | copy-start | bytes 64
  1.6 6.8 %copy-start.7 = (s32[8]{0:T(128)S(1)}, s32[8]{0:T(128)}, u32[]{:S(2)}) copy-start(s32[8]{0:T(128)} %param.18) | copy-start | bytes 100
  6.3 4.6 %copy-start.2 = (f32[2048]{0:T(1024)S(1)}, f32[2048]{0:T(1024)}, u32[]{:S(2)}) copy-start(f32[2048]{0:T(1024)} %param.14) | copy-start | bytes 24580
  6.3 4.5 %copy-start.3 = (bf16[2048,4]{0,1:T(4,128)(2,1)S(1)}, bf16[2048,4]{0,1:T(4,128)(2,1)}, u32[]{:S(2)}) copy-start(bf16[2048,4]{0,1:T(4,128)(2,1)} %param.15) | copy-start | bytes 49156
  6.3 6.3 %copy-start.5 = (s32[128,2]{0,1:T(2,128)S(1)}, s32[128,2]{0,1:T(2,128)}, u32[]{:S(2)}) copy-start(s32[128,2]{0,1:T(2,128)} %param.16) | copy-start | bytes 3076
  6.4 2.4 %collective-permute-start = (bf16[128,2048]{1,0:T(8,128)(2,1)S(1)}, bf16[128,2048]{1,0:T(8,128)(2,1)}, u32[]{:S(2)}, u32[]{:S(2)}) collective-permute-start(bf16[128,2048]{1,0:T(8,128)(2,1)S(1)} %select_convert_fusion.2), channel_id=1, source_target_pairs={{0,1},{1,0},{2,3},{3,2},{4,5},{5,4},{6,7},{7,6},{8,9},{9,8},{10,11... | collective-permute-start | bytes 1572872 | tf_op jit(solution)/shard_map/ppermute | solution.py:18
  10.4 1.3 collective-permute-start.1
  11.4 1.2 collective-permute-start.2
  13.7 15.4 %collective-permute-start.5 = (bf16[48,2048]{1,0:T(8,128)(2,1)S(1)}, bf16[48,2048]{1,0:T(8,128)(2,1)S(1)}, u32[]{:S(2)}, u32[]{:S(2)}) collective-permute-start(bf16[48,2048]{1,0:T(8,128)(2,1)S(1)} %get-tuple-element.24), channel_id=1, source_target_pairs={{0,16},{2,18},{4,20},{6,22},{8,24},{10,26},{12,28},{14,30},{16,0},... | collective-permute-start | bytes 589832 | tf_op jit(solution)/shard_map/ppermute | solution.py:10
  16.0 17.2 %collective-permute-start.6 = (bf16[48,2048]{1,0:T(8,128)(2,1)S(1)}, bf16[48,2048]{1,0:T(8,128)(2,1)S(1)}, u32[]{:S(2)}, u32[]{:S(2)}) collective-permute-start(bf16[48,2048]{1,0:T(8,128)(2,1)S(1)} %get-tuple-element.23), channel_id=1, source_target_pairs={{0,20},{2,22},{4,16},{6,18},{8,28},{10,30},{12,24},{14,26},{16,4},... | collective-permute-start | bytes 589832 | tf_op jit(solution)/shard_map/ppermute | solution.py:10
  16.1 34.3 %collective-permute-start.3 = (bf16[48,2048]{1,0:T(8,128)(2,1)S(1)}, bf16[48,2048]{1,0:T(8,128)(2,1)S(1)}, u32[]{:S(2)}, u32[]{:S(2)}) collective-permute-start(bf16[48,2048]{1,0:T(8,128)(2,1)S(1)} %get-tuple-element.25), channel_id=1, source_target_pairs={{0,4},{2,6},{4,0},{6,2},{8,12},{10,14},{12,8},{14,10},{16,20},{18,... | collective-permute-start | bytes 589832 | tf_op jit(solution)/shard_map/ppermute | solution.py:10
  17.3 16.0 %collective-permute-start.18 = (bf16[48,2048]{1,0:T(8,128)(2,1)S(1)}, bf16[48,2048]{1,0:T(8,128)(2,1)S(1)}, u32[]{:S(2)}, u32[]{:S(2)}) collective-permute-start(bf16[48,2048]{1,0:T(8,128)(2,1)S(1)} %get-tuple-element.22), channel_id=1, source_target_pairs={{0,8},{2,10},{4,12},{6,14},{8,0},{10,2},{12,4},{14,6},{16,24},{18,... | collective-permute-start | bytes 589832 | tf_op jit(solution)/shard_map/ppermute | solution.py:10
  17.6 16.2 %collective-permute-start.19 = (bf16[48,2048]{1,0:T(8,128)(2,1)S(1)}, bf16[48,2048]{1,0:T(8,128)(2,1)S(1)}, u32[]{:S(2)}, u32[]{:S(2)}) collective-permute-start(bf16[48,2048]{1,0:T(8,128)(2,1)S(1)} %get-tuple-element.21), channel_id=1, source_target_pairs={{0,12},{2,14},{4,8},{6,10},{8,4},{10,6},{12,0},{14,2},{16,28},{18,... | collective-permute-start | bytes 589832 | tf_op jit(solution)/shard_map/ppermute | solution.py:10
  29.1 16.9 %collective-permute-start.21 = (bf16[48,2048]{1,0:T(8,128)(2,1)S(1)}, bf16[48,2048]{1,0:T(8,128)(2,1)S(1)}, u32[]{:S(2)}, u32[]{:S(2)}) collective-permute-start(bf16[48,2048]{1,0:T(8,128)(2,1)S(1)} %get-tuple-element.20), channel_id=1, source_target_pairs={{0,24},{2,26},{4,28},{6,30},{8,16},{10,18},{12,20},{14,22},{16,8},... | collective-permute-start | bytes 589832 | tf_op jit(solution)/shard_map/ppermute | solution.py:10
  33.3 16.9 %collective-permute-start.22 = (bf16[48,2048]{1,0:T(8,128)(2,1)S(1)}, bf16[48,2048]{1,0:T(8,128)(2,1)S(1)}, u32[]{:S(2)}, u32[]{:S(2)}) collective-permute-start(bf16[48,2048]{1,0:T(8,128)(2,1)S(1)} %get-tuple-element.19), channel_id=1, source_target_pairs={{0,28},{2,30},{4,24},{6,26},{8,20},{10,22},{12,16},{14,18},{16,12}... | collective-permute-start | bytes 589832 | tf_op jit(solution)/shard_map/ppermute | solution.py:10
  33.3 19.7 %collective-permute-start.10 = (bf16[96,2048]{1,0:T(8,128)(2,1)S(1)}, bf16[96,2048]{1,0:T(8,128)(2,1)S(1)}, u32[]{:S(2)}, u32[]{:S(2)}) collective-permute-start(bf16[96,2048]{1,0:T(8,128)(2,1)S(1)} %constant_dynamic-update-slice_fusion), channel_id=1, source_target_pairs={{0,2},{2,0},{4,6},{6,4},{8,10},{10,8},{12,14},{14,12},{16,18},{18,... | collective-permute-start | bytes 1179656 | tf_op jit(solution)/shard_map/ppermute | solution.py:14
  33.8 17.5 %collective-permute-start.7 = (bf16[96,2048]{1,0:T(8,128)(2,1)S(1)}, bf16[96,2048]{1,0:T(8,128)(2,1)S(1)}, u32[]{:S(2)}, u32[]{:S(2)}) collective-permute-start(bf16[96,2048]{1,0:T(8,128)(2,1)S(1)} %constant_dynamic-update-slice_fusion), channel_id=1, source_target_pairs={{0,1},{1,0},{2,3},{3,2},{4,5},{5,4},{6,7},{7,6},{8,9},{9,8},{10,11... | collective-permute-start | bytes 1179656 | tf_op jit(solution)/shard_map/ppermute | solution.py:18
  45.9 6.7 %collective-permute-start.20 = (bf16[96,2048]{1,0:T(8,128)(2,1)S(1)}, bf16[96,2048]{1,0:T(8,128)(2,1)S(1)}, u32[]{:S(2)}, u32[]{:S(2)}) collective-permute-start(bf16[96,2048]{1,0:T(8,128)(2,1)S(1)} %constant_dynamic-update-slice_fusion.2), channel_id=1, source_target_pairs={{0,1},{1,0},{2,3},{3,2},{4,5},{5,4},{6,7},{7,6},{8,9},{9,8},{10,11... | collective-permute-start | bytes 1179656 | tf_op jit(solution)/shard_map/ppermute | solution.py:18
  50.1 28.4 %collective-permute-start.24 = (bf16[96,2048]{1,0:T(8,128)(2,1)S(1)}, bf16[96,2048]{1,0:T(8,128)(2,1)S(1)}, u32[]{:S(2)}, u32[]{:S(2)}) collective-permute-start(bf16[96,2048]{1,0:T(8,128)(2,1)S(1)} %constant_dynamic-update-slice_fusion.2), channel_id=1, source_target_pairs={{0,2},{2,0},{4,6},{6,4},{8,10},{10,8},{12,14},{14,12},{16,18},{18,... | collective-permute-start | bytes 1179656 | tf_op jit(solution)/shard_map/ppermute | solution.py:14
  50.4 28.1 %collective-permute-start.23 = (bf16[96,2048]{1,0:T(8,128)(2,1)S(1)}, bf16[96,2048]{1,0:T(8,128)(2,1)S(1)}, u32[]{:S(2)}, u32[]{:S(2)}) collective-permute-start(bf16[96,2048]{1,0:T(8,128)(2,1)S(1)} %constant_dynamic-update-slice_fusion.4), channel_id=1, source_target_pairs={{0,1},{1,0},{2,3},{3,2},{4,5},{5,4},{6,7},{7,6},{8,9},{9,8},{10,11... | collective-permute-start | bytes 1179656 | tf_op jit(solution)/shard_map/ppermute | solution.py:18
  51.3 27.8 %collective-permute-start.26 = (bf16[96,2048]{1,0:T(8,128)(2,1)S(1)}, bf16[96,2048]{1,0:T(8,128)(2,1)S(1)}, u32[]{:S(2)}, u32[]{:S(2)}) collective-permute-start(bf16[96,2048]{1,0:T(8,128)(2,1)S(1)} %constant_dynamic-update-slice_fusion.4), channel_id=1, source_target_pairs={{0,2},{2,0},{4,6},{6,4},{8,10},{10,8},{12,14},{14,12},{16,18},{18,... | collective-permute-start | bytes 1179656 | tf_op jit(solution)/shard_map/ppermute | solution.py:14
  52.6 24.6 %collective-permute-start.8 = (bf16[96,2048]{1,0:T(8,128)(2,1)S(1)}, bf16[96,2048]{1,0:T(8,128)(2,1)S(1)}, u32[]{:S(2)}, u32[]{:S(2)}) collective-permute-start(bf16[96,2048]{1,0:T(8,128)(2,1)S(1)} %pad_maximum_fusion.1), channel_id=1, source_target_pairs={{0,2},{2,0},{4,6},{6,4},{8,10},{10,8},{12,14},{14,12},{16,18},{18,... | collective-permute-start | bytes 1179656 | tf_op jit(solution)/shard_map/ppermute | solution.py:14
  53.0 26.2 %collective-permute-start.4 = (bf16[96,2048]{1,0:T(8,128)(2,1)S(1)}, bf16[96,2048]{1,0:T(8,128)(2,1)S(1)}, u32[]{:S(2)}, u32[]{:S(2)}) collective-permute-start(bf16[96,2048]{1,0:T(8,128)(2,1)S(1)} %pad_maximum_fusion.1), channel_id=1, source_target_pairs={{0,1},{1,0},{2,3},{3,2},{4,5},{5,4},{6,7},{7,6},{8,9},{9,8},{10,11... | collective-permute-start | bytes 1179656 | tf_op jit(solution)/shard_map/ppermute | solution.py:18
  77.2 2.7 %collective-permute-start.11 = (bf16[96,2048]{1,0:T(8,128)(2,1)S(1)}, bf16[96,2048]{1,0:T(8,128)(2,1)S(1)}, u32[]{:S(2)}, u32[]{:S(2)}) collective-permute-start(bf16[96,2048]{1,0:T(8,128)(2,1)S(1)} %collective-permute-done.10), channel_id=1, source_target_pairs={{0,1},{1,0},{2,3},{3,2},{4,5},{5,4},{6,7},{7,6},{8,9},{9,8},{10,11... | collective-permute-start | bytes 1179656 | tf_op jit(solution)/shard_map/ppermute | solution.py:18
  78.5 1.9 collective-permute-start.9
  78.5 27.4 %collective-permute-start.25 = (bf16[96,2048]{1,0:T(8,128)(2,1)S(1)}, bf16[96,2048]{1,0:T(8,128)(2,1)S(1)}, u32[]{:S(2)}, u32[]{:S(2)}) collective-permute-start(bf16[96,2048]{1,0:T(8,128)(2,1)S(1)} %collective-permute-done.24), channel_id=1, source_target_pairs={{0,1},{1,0},{2,3},{3,2},{4,5},{5,4},{6,7},{7,6},{8,9},{9,8},{10,11... | collective-permute-start | bytes 1179656 | tf_op jit(solution)/shard_map/ppermute | solution.py:18
  79.0 26.9 %collective-permute-start.27 = (bf16[96,2048]{1,0:T(8,128)(2,1)S(1)}, bf16[96,2048]{1,0:T(8,128)(2,1)S(1)}, u32[]{:S(2)}, u32[]{:S(2)}) collective-permute-start(bf16[96,2048]{1,0:T(8,128)(2,1)S(1)} %collective-permute-done.26), channel_id=1, source_target_pairs={{0,1},{1,0},{2,3},{3,2},{4,5},{5,4},{6,7},{7,6},{8,9},{9,8},{10,11... | collective-permute-start | bytes 1179656 | tf_op jit(solution)/shard_map/ppermute | solution.py:18
  118.6 12.7 %copy-start.8 = (f32[384,1792]{1,0:T(8,128)S(1)}, f32[384,1792]{1,0:T(8,128)}, u32[]{:S(2)}) copy-start(f32[384,1792]{1,0:T(8,128)} %fusion.10) | copy-start | bytes 8257540
  141.5 1.8 copy-start.9
  141.8 12.6 %collective-permute-start.12 = (bf16[384,2048]{1,0:T(8,128)(2,1)S(1)}, bf16[384,2048]{1,0:T(8,128)(2,1)S(1)}, u32[]{:S(2)}, u32[]{:S(2)}) collective-permute-start(bf16[384,2048]{1,0:T(8,128)(2,1)S(1)} %select_convert_fusion.1), channel_id=1, source_target_pairs={{0,1},{1,0},{2,3},{3,2},{4,5},{5,4},{6,7},{7,6},{8,9},{9,8},{10,11... | collective-permute-start | bytes 4718600 | tf_op jit(solution)/shard_map/ppermute | solution.py:18
  153.7 3.5 %collective-permute-start.28 = (bf16[384,2048]{1,0:T(8,128)(2,1)S(1)}, bf16[384,2048]{1,0:T(8,128)(2,1)S(1)}, u32[]{:S(2)}, u32[]{:S(2)}) collective-permute-start(bf16[384,2048]{1,0:T(8,128)(2,1)S(1)} %select_convert_fusion), channel_id=1, source_target_pairs={{0,1},{1,0},{2,3},{3,2},{4,5},{5,4},{6,7},{7,6},{8,9},{9,8},{10,11... | collective-permute-start | bytes 4718600 | tf_op jit(solution)/shard_map/ppermute | solution.py:18
  155.6 10.6 %collective-permute-start.13 = (bf16[96,2048]{1,0:T(8,128)(2,1)S(1)}, bf16[96,2048]{1,0:T(8,128)(2,1)S(1)}, u32[]{:S(2)}, u32[]{:S(2)}) collective-permute-start(bf16[96,2048]{1,0:T(8,128)(2,1)S(1)} %get-tuple-element.16), channel_id=1, source_target_pairs={{0,2},{2,0},{4,6},{6,4},{8,10},{10,8},{12,14},{14,12},{16,18},{18,... | collective-permute-start | bytes 1179656 | tf_op jit(solution)/shard_map/ppermute | solution.py:14
  155.9 18.7 %collective-permute-start.15 = (bf16[96,2048]{1,0:T(8,128)(2,1)S(1)}, bf16[96,2048]{1,0:T(8,128)(2,1)S(1)}, u32[]{:S(2)}, u32[]{:S(2)}) collective-permute-start(bf16[96,2048]{1,0:T(8,128)(2,1)S(1)} %get-tuple-element.17), channel_id=1, source_target_pairs={{0,2},{2,0},{4,6},{6,4},{8,10},{10,8},{12,14},{14,12},{16,18},{18,... | collective-permute-start | bytes 1179656 | tf_op jit(solution)/shard_map/ppermute | solution.py:14
  158.4 24.7 %collective-permute-start.29 = (bf16[96,2048]{1,0:T(8,128)(2,1)S(1)}, bf16[96,2048]{1,0:T(8,128)(2,1)S(1)}, u32[]{:S(2)}, u32[]{:S(2)}) collective-permute-start(bf16[96,2048]{1,0:T(8,128)(2,1)S(1)} %get-tuple-element.27), channel_id=1, source_target_pairs={{0,2},{2,0},{4,6},{6,4},{8,10},{10,8},{12,14},{14,12},{16,18},{18,... | collective-permute-start | bytes 1179656 | tf_op jit(solution)/shard_map/ppermute | solution.py:14
  158.7 32.8 %collective-permute-start.32 = (bf16[96,2048]{1,0:T(8,128)(2,1)S(1)}, bf16[96,2048]{1,0:T(8,128)(2,1)S(1)}, u32[]{:S(2)}, u32[]{:S(2)}) collective-permute-start(bf16[96,2048]{1,0:T(8,128)(2,1)S(1)} %get-tuple-element.26), channel_id=1, source_target_pairs={{0,2},{2,0},{4,6},{6,4},{8,10},{10,8},{12,14},{14,12},{16,18},{18,... | collective-permute-start | bytes 1179656 | tf_op jit(solution)/shard_map/ppermute | solution.py:14
  174.9 44.5 %collective-permute-start.14 = (bf16[48,2048]{1,0:T(8,128)(2,1)S(1)}, bf16[48,2048]{1,0:T(8,128)(2,1)S(1)}, u32[]{:S(2)}, u32[]{:S(2)}) collective-permute-start(bf16[48,2048]{1,0:T(8,128)(2,1)S(1)} %get-tuple-element.47), channel_id=1, source_target_pairs={{0,4},{2,6},{4,0},{6,2},{8,12},{10,14},{12,8},{14,10},{16,20},{18,... | collective-permute-start | bytes 589832 | tf_op jit(solution)/shard_map/ppermute | solution.py:10
  175.6 43.9 %collective-permute-start.16 = (bf16[48,2048]{1,0:T(8,128)(2,1)S(1)}, bf16[48,2048]{1,0:T(8,128)(2,1)S(1)}, u32[]{:S(2)}, u32[]{:S(2)}) collective-permute-start(bf16[48,2048]{1,0:T(8,128)(2,1)S(1)} %get-tuple-element.48), channel_id=1, source_target_pairs={{0,16},{2,18},{4,20},{6,22},{8,24},{10,26},{12,28},{14,30},{16,0},... | collective-permute-start | bytes 589832 | tf_op jit(solution)/shard_map/ppermute | solution.py:10
  175.6 43.8 %collective-permute-start.17 = (bf16[48,2048]{1,0:T(8,128)(2,1)S(1)}, bf16[48,2048]{1,0:T(8,128)(2,1)S(1)}, u32[]{:S(2)}, u32[]{:S(2)}) collective-permute-start(bf16[48,2048]{1,0:T(8,128)(2,1)S(1)} %get-tuple-element.49), channel_id=1, source_target_pairs={{0,20},{2,22},{4,16},{6,18},{8,28},{10,30},{12,24},{14,26},{16,4},... | collective-permute-start | bytes 589832 | tf_op jit(solution)/shard_map/ppermute | solution.py:10
  191.8 7.4 %collective-permute-start.30 = (bf16[48,2048]{1,0:T(8,128)(2,1)S(1)}, bf16[48,2048]{1,0:T(8,128)(2,1)S(1)}, u32[]{:S(2)}, u32[]{:S(2)}) collective-permute-start(bf16[48,2048]{1,0:T(8,128)(2,1)S(1)} %get-tuple-element.53), channel_id=1, source_target_pairs={{0,8},{2,10},{4,12},{6,14},{8,0},{10,2},{12,4},{14,6},{16,24},{18,... | collective-permute-start | bytes 589832 | tf_op jit(solution)/shard_map/ppermute | solution.py:10
  191.8 11.5 %collective-permute-start.31 = (bf16[48,2048]{1,0:T(8,128)(2,1)S(1)}, bf16[48,2048]{1,0:T(8,128)(2,1)S(1)}, u32[]{:S(2)}, u32[]{:S(2)}) collective-permute-start(bf16[48,2048]{1,0:T(8,128)(2,1)S(1)} %get-tuple-element.52), channel_id=1, source_target_pairs={{0,12},{2,14},{4,8},{6,10},{8,4},{10,6},{12,0},{14,2},{16,28},{18,... | collective-permute-start | bytes 589832 | tf_op jit(solution)/shard_map/ppermute | solution.py:10
  199.2 5.3 %collective-permute-start.33 = (bf16[48,2048]{1,0:T(8,128)(2,1)S(1)}, bf16[48,2048]{1,0:T(8,128)(2,1)S(1)}, u32[]{:S(2)}, u32[]{:S(2)}) collective-permute-start(bf16[48,2048]{1,0:T(8,128)(2,1)S(1)} %get-tuple-element.51), channel_id=1, source_target_pairs={{0,24},{2,26},{4,28},{6,30},{8,16},{10,18},{12,20},{14,22},{16,8},... | collective-permute-start | bytes 589832 | tf_op jit(solution)/shard_map/ppermute | solution.py:10
  203.4 15.3 %collective-permute-start.34 = (bf16[48,2048]{1,0:T(8,128)(2,1)S(1)}, bf16[48,2048]{1,0:T(8,128)(2,1)S(1)}, u32[]{:S(2)}, u32[]{:S(2)}) collective-permute-start(bf16[48,2048]{1,0:T(8,128)(2,1)S(1)} %get-tuple-element.50), channel_id=1, source_target_pairs={{0,28},{2,30},{4,24},{6,26},{8,20},{10,22},{12,16},{14,18},{16,12}... | collective-permute-start | bytes 589832 | tf_op jit(solution)/shard_map/ppermute | solution.py:10
  219.8 3.2 %copy-start.4 = (f32[2048]{0:T(1024)S(1)}, f32[2048]{0:T(1024)}, u32[]{:S(2)}) copy-start(f32[2048]{0:T(1024)} %param.21) | copy-start | bytes 24580
  219.8 4.3 %copy-start.1 = (bf16[128,1024]{1,0:T(8,128)(2,1)S(1)}, bf16[128,1024]{1,0:T(8,128)(2,1)}, u32[]{:S(2)}) copy-start(bf16[128,1024]{1,0:T(8,128)(2,1)} %param.11) | copy-start | bytes 786436
  220.5 2.5 %collective-permute-start.35 = (f32[128,1]{0,1:T(1,128)S(1)}, f32[128,1]{0,1:T(1,128)S(1)}, u32[]{:S(2)}, u32[]{:S(2)}) collective-permute-start(f32[128,1]{0,1:T(1,128)S(1)} %bitcast.38), channel_id=1, source_target_pairs={{0,1},{1,0},{2,3},{3,2},{4,5},{5,4},{6,7},{7,6},{8,9},{9,8},{10,11... | collective-permute-start | bytes 1544 | tf_op jit(solution)/shard_map/ppermute | solution.py:18

commit v2 on v1

--- a/solution.py
+++ b/solution.py
@@ -1,9 +1,14 @@
 import jax
 import jax.numpy as jnp
 from jax import lax
+from jax.experimental import pallas as pl
+from jax.experimental.pallas import tpu as pltpu
 from jax.sharding import PartitionSpec as P
 
 epsilon = 1e-05
+LONG = 20_000_000_000
+WHOLE = pl.BlockSpec(memory_space=pltpu.VMEM)
+ANYWHERE = pl.BlockSpec(memory_space=pl.ANY)
 
 
 def pair_shift(value, k, devices):
@@ -42,6 +47,333 @@
     low, high = value[:, :width], value[:, width:]
     away = jnp.where(first, high, low).astype(jnp.bfloat16)
     return jnp.where(first, low, high) + core_swap(away).astype(jnp.float32)
+
+
+def slot_rows_kernel(blocks, slots_ref, rows_ref, *refs):
+    slots = slots_ref[...]
+    for out_ref, block in zip(refs[-len(blocks) :], blocks):
+        shape = (out_ref.shape[0], slots.shape[1])
+        here = lax.broadcasted_iota(jnp.int32, shape, 0) + block * shape[0]
+        hot = jnp.where((slots[0:1] == here) | (slots[1:2] == here), 1.0, 0.0)
+        out_ref[...] = jnp.dot(
+            hot.astype(jnp.bfloat16), rows_ref[...], preferred_element_type=jnp.float32
+        ).astype(jnp.bfloat16)
+
+
+def slot_rows(blocks, capacity, slots, rows, after):
+    outs = pl.pallas_call(
+        lambda *refs: slot_rows_kernel(blocks, *refs),
+        in_specs=[WHOLE, WHOLE] + [ANYWHERE] * len(after),
+        out_specs=[WHOLE] * len(blocks),
+        out_shape=[jax.ShapeDtypeStruct((capacity, rows.shape[1]), jnp.bfloat16)] * len(blocks),
+        compiler_params=pltpu.CompilerParams(vmem_limit_bytes=16 << 20),
+        name="slot_rows",
+    )(slots, rows, *after)
+    return dict(zip(blocks, outs))
+
+
+def join_kernel(count, *refs):
+    out_ref = refs[-1]
+    start = 0
+    for ref in refs[:count]:
+        out_ref[start : start + ref.shape[0]] = ref[...]
+        start += ref.shape[0]
+
+
+def join(values, after, flops=0):
+    rows = sum(value.shape[0] for value in values)
+    return pl.pallas_call(
+        lambda *refs: join_kernel(len(values), *refs),
+        in_specs=[WHOLE] * len(values) + [ANYWHERE] * len(after),
+        out_specs=WHOLE,
+        out_shape=jax.ShapeDtypeStruct((rows, values[0].shape[1]), values[0].dtype),
+        compiler_params=pltpu.CompilerParams(vmem_limit_bytes=16 << 20),
+        cost_estimate=pl.CostEstimate(flops=flops, bytes_accessed=0, transcendentals=0),
+        name="join",
+    )(*values, *after)
+
+
+def add_cores_kernel(counts, kept_ref, other_ref, *refs):
+    outs = refs[-len(counts) - 1 :]
+    start = outs[0].shape[0]
+    outs[0][...] = kept_ref[:start] + other_ref[:start].astype(jnp.float32)
+    for out_ref, count in zip(outs[1:], counts):
+        part = slice(start, start + count)
+        out_ref[...] = (kept_ref[part] + other_ref[part].astype(jnp.float32)).astype(jnp.bfloat16)
+        start += count
+
+
+def add_cores(kept, other, counts, after):
+    rows, width = kept.shape
+    return pl.pallas_call(
+        lambda *refs: add_cores_kernel(counts, *refs),
+        in_specs=[WHOLE, WHOLE] + [ANYWHERE] * len(after),
+        out_specs=[WHOLE] * (len(counts) + 1),
+        out_shape=[jax.ShapeDtypeStruct((rows - sum(counts), width), jnp.float32)]
+        + [jax.ShapeDtypeStruct((count, width), jnp.bfloat16) for count in counts],
+        compiler_params=pltpu.CompilerParams(vmem_limit_bytes=16 << 20),
+        name="add_cores",
+    )(kept, other, *after)
+
+
+def add_sides_kernel(start, own_ref, other_ref, *refs):
+    total = own_ref[start : start + other_ref.shape[0]] + other_ref[...].astype(jnp.float32)
+    first = 0
+    for out_ref in refs:
+        out_ref[...] = total[first : first + out_ref.shape[0]].astype(jnp.bfloat16)
+        first += out_ref.shape[0]
+
+
+def add_sides(own, start, other, counts, after):
+    return pl.pallas_call(
+        lambda *refs: add_sides_kernel(start, *refs[:2], *refs[-len(counts) :]),
+        in_specs=[WHOLE, WHOLE] + [ANYWHERE] * len(after),
+        out_specs=[WHOLE] * len(counts),
+        out_shape=[jax.ShapeDtypeStruct((n, own.shape[1]), jnp.bfloat16) for n in counts],
+        compiler_params=pltpu.CompilerParams(vmem_limit_bytes=16 << 20),
+        name="add_sides",
+    )(own, other, *after)
+
+
+def gate_up_kernel(counts, core_ref, *refs):
+    pieces = refs[: 2 * len(counts)]
+    weights_ref = refs[2 * len(counts)]
+    out_ref, rows_ref = refs[-2:]
+    width = pieces[0].shape[1]
+
+    @pl.when(pl.program_id(0) == 0)
+    def _():
+        start = 0
+        own = pl.multiple_of(core_ref[0] * width, width)
+        other = pl.multiple_of((1 - core_ref[0]) * width, width)
+        for i, count in enumerate(counts):
+            rows_ref[start : start + count, pl.ds(own, width)] = pieces[2 * i][...]
+            rows_ref[start : start + count, pl.ds(other, width)] = pieces[2 * i + 1][...]
+            start += count
+
+    rows = rows_ref[...]
+    gate = jnp.dot(rows, weights_ref[0, 0], preferred_element_type=jnp.float32)
+    up = jnp.dot(rows, weights_ref[0, 1], preferred_element_type=jnp.float32)
+    out_ref[...] = (gate * jax.nn.sigmoid(gate) * up).astype(jnp.bfloat16)
+
+
+def gate_up(core, pieces, weights, after):
+    counts = [own.shape[0] for own, _ in pieces]
+    rows = sum(counts)
+    _, _, depth, units = weights.shape
+    block = 256
+    return pl.pallas_call(
+        lambda *refs: gate_up_kernel(counts, *refs),
+        grid_spec=pltpu.PrefetchScalarGridSpec(
+            num_scalar_prefetch=1,
+            grid=(units // block,),
+            in_specs=[WHOLE] * (2 * len(counts))
+            + [pl.BlockSpec((1, 2, depth, block), lambda i, core: (0, 0, 0, i))]
+            + [ANYWHERE] * len(after),
+            out_specs=pl.BlockSpec((rows, block), lambda i, core: (0, i)),
+            scratch_shapes=[pltpu.VMEM((rows, depth), jnp.bfloat16)],
+        ),
+        out_shape=jax.ShapeDtypeStruct((rows, units), jnp.bfloat16),
+        compiler_params=pltpu.CompilerParams(vmem_limit_bytes=36 << 20),
+        cost_estimate=pl.CostEstimate(
+            flops=rows * depth, bytes_accessed=depth, transcendentals=0
+        ),
+        name="gate_up",
+    )(core, *[part for piece in pieces for part in piece], weights, *after)
+
+
+def down_kernel(core_ref, activ_ref, weights_ref, *refs):
+    out_ref = refs[-1]
+    out_ref[...] = jnp.dot(
+        activ_ref[...], weights_ref[0], preferred_element_type=jnp.float32
+    ).astype(out_ref.dtype)
+
+
+def down(core, activ, weights, away, after):
+    rows, units = activ.shape
+    width = weights.shape[2] // 2
+    block = 1024
+    steps = width // block
+    return pl.pallas_call(
+        down_kernel,
+        grid_spec=pltpu.PrefetchScalarGridSpec(
+            num_scalar_prefetch=1,
+            grid=(steps,),
+            in_specs=[
+                pl.BlockSpec((rows, units), lambda i, core: (0, 0)),
+                pl.BlockSpec(
+                    (1, units, block),
+                    lambda i, core: (0, 0, (1 - core[0] if away else core[0]) * steps + i),
+                ),
+            ]
+            + [ANYWHERE] * len(after),
+            out_specs=pl.BlockSpec((rows, block), lambda i, core: (0, i)),
+        ),
+        out_shape=jax.ShapeDtypeStruct((rows, width), jnp.bfloat16 if away else jnp.float32),
+        compiler_params=pltpu.CompilerParams(vmem_limit_bytes=44 << 20),
+        cost_estimate=pl.CostEstimate(
+            flops=rows * units, bytes_accessed=units, transcendentals=0
+        ),
+        name="down_away" if away else "down_own",
+    )(core, activ, weights, *after)
+
+
+def down_both_kernel(core_ref, activ_ref, weights_ref, *refs):
+    away_ref, own_ref = refs[-2:]
+    product = jnp.dot(activ_ref[...], weights_ref[0], preferred_element_type=jnp.float32)
+    half = pl.num_programs(0) // 2
+
+    @pl.when(pl.program_id(0) < half)
+    def _():
+        away_ref[...] = product.astype(jnp.bfloat16)
+
+    @pl.when(pl.program_id(0) >= half)
+    def _():
+        own_ref[...] = product
+
+
+def down_both(core, activ, weights, after):
+    rows, units = activ.shape
+    width = weights.shape[2] // 2
+    block = 1024
+    half = width // block
+
+    def columns(i, core):
+        side = jnp.where(i < half, 1 - core[0], core[0])
+        return (0, 0, side * half + lax.rem(i, half))
+
+    return pl.pallas_call(
+        down_both_kernel,
+        grid_spec=pltpu.PrefetchScalarGridSpec(
+            num_scalar_prefetch=1,
+            grid=(2 * half,),
+            in_specs=[
+                pl.BlockSpec((rows, units), lambda i, core: (0, 0)),
+                pl.BlockSpec((1, units, block), columns),
+            ]
+            + [ANYWHERE] * len(after),
+            out_specs=[
+                pl.BlockSpec((rows, block), lambda i, core: (0, jnp.minimum(i, half - 1))),
+                pl.BlockSpec((rows, block), lambda i, core: (0, jnp.maximum(i - half, 0))),
+            ],
+        ),
+        out_shape=[
+            jax.ShapeDtypeStruct((rows, width), jnp.bfloat16),
+            jax.ShapeDtypeStruct((rows, width), jnp.float32),
+        ],
+        compiler_params=pltpu.CompilerParams(vmem_limit_bytes=44 << 20),
+        cost_estimate=pl.CostEstimate(flops=rows * units, bytes_accessed=units, transcendentals=0),
+        name="down_both",
+    )(core, activ, weights, *after)
+
+
+def mix_kernel(count, high_ref, low_ref, base_ref, *refs):
+    out_ref = refs[-1]
+    total = base_ref[...]
+    width = high_ref.shape[1] // count
+    for j, ref in enumerate(refs[:count]):
+        part = slice(j * width, (j + 1) * width)
+        total += jnp.dot(high_ref[:, part], ref[...], preferred_element_type=jnp.float32)
+        total += jnp.dot(low_ref[:, part], ref[...], preferred_element_type=jnp.float32)
+    out_ref[...] = total
+
+
+def mix(tables, base, values, after, flops=0):
+    return pl.pallas_call(
+        lambda *refs: mix_kernel(len(values), *refs),
+        in_specs=[WHOLE] * (3 + len(values)) + [ANYWHERE] * len(after),
+        out_specs=WHOLE,
+        out_shape=jax.ShapeDtypeStruct(base.shape, jnp.float32),
+        compiler_params=pltpu.CompilerParams(vmem_limit_bytes=16 << 20),
+        cost_estimate=pl.CostEstimate(flops=flops, bytes_accessed=0, transcendentals=0),
+        name="mix",
+    )(*tables, base, *values, *after)
+
+
+def experts_of_two_cores(slots, rows, capacity, tables, state, w_gate_up, w_down, devices):
+    pair_count = devices // 2
+    core = lax.axis_index("tp").reshape(1)
+    blocks = list(range(pair_count))
+    quarter = pair_count // 4
+    near, near_later, far, far_later = [
+        blocks[i * quarter : (i + 1) * quarter] for i in range(4)
+    ]
+    size = quarter * capacity
+
+    def columns(first):
+        return [table[:, first * capacity : (first + quarter) * capacity] for table in tables]
+
+    def send(group, values):
+        return [pair_shift(x, k, devices) if k else x for k, x in zip(group, values)]
+
+    outgoing = slot_rows(far + near + near_later, capacity, slots, rows, [])
+    arrived = dict(zip(far, send(far, [outgoing[k] for k in far])))
+    arrived |= zip(near, send(near, [outgoing[k] for k in near]))
+    arrived |= zip(near_later, send(near_later, [outgoing[k] for k in near_later]))
+    outgoing = slot_rows(far_later, capacity, slots, rows, [arrived[near[-1]]])
+    arrived |= zip(far_later, send(far_later, [outgoing[k] for k in far_later]))
+
+    near_own = join([arrived[k] for k in near], [])
+    near_nbr = side_swap(near_own, devices)
+    far_own = join([arrived[k] for k in far], [], LONG)
+    far_nbr = side_swap(far_own, devices)
+    near_later_own = join([arrived[k] for k in near_later], [])
+    near_later_nbr = side_swap(near_later_own, devices)
+    far_later_own = join([arrived[k] for k in far_later], [], LONG)
+    far_later_nbr = side_swap(far_later_own, devices)
+
+    pieces = [(x, core_swap(x)) for x in (far_own, near_own, far_nbr, near_nbr)]
+    activ = gate_up(core, pieces, w_gate_up, [near_later_own, far_later_own])
+    later = join([far_later_nbr, near_later_nbr], [activ])
+    away = core_swap(down(core, activ, w_down, True, [later]))
+    kept = down(core, activ, w_down, False, [])
+    own, far_other, near_other = add_cores(kept, away, [size, size], [])
+    pieces = [(x, core_swap(x)) for x in (far_later_own, near_later_own, later)]
+    activ = gate_up(core, pieces, w_gate_up, [own])
+
+    far_other = side_swap(far_other, devices)
+    near_other = side_swap(near_other, devices)
+    far_back = send(far, add_sides(own, 0, far_other, [capacity] * quarter, [activ]))
+    totals = add_sides(own, size, near_other, [capacity] * quarter, [activ])
+    near_back = send(near, totals)
+    away, kept = down_both(core, activ, w_down, totals)
+    state = mix(columns(far[0]), state, far_back, [kept], LONG)
+    state = mix(columns(near[0]), state, near_back, [])
+    counts = [capacity] * quarter + [size]
+    own, *others = add_cores(kept, core_swap(away), counts, [state])
+    far_back = []
+    for j, k in enumerate(far_later):
+        other = side_swap(others[j], devices)
+        (total,) = add_sides(own, j * capacity, other, [capacity], [])
+        far_back += send([k], [total])
+    other = side_swap(others[-1], devices)
+    near_back = send(near_later, add_sides(own, size, other, [capacity] * quarter, []))
+    state = mix(columns(near_later[0]), state, near_back, [])
+    return mix(columns(far_later[0]), state, far_back, [])
+
+
+def experts_of_any(slots, rows, capacity, tables, state, w_gate_up, w_down, devices):
+    pair_count = devices // 2
+    slot_range = jnp.arange(pair_count * capacity, dtype=jnp.int32)[:, None]
+    hot = ((slots[0:1] == slot_range) | (slots[1:2] == slot_range)).astype(jnp.bfloat16)
+    outgoing = jnp.dot(hot, rows, preferred_element_type=jnp.float32).astype(jnp.bfloat16)
+    outgoing = outgoing.reshape(pair_count, capacity, -1)
+    own = [pair_shift(outgoing[k], k, devices) if k else outgoing[k] for k in range(pair_count)]
+    own = jnp.concatenate(own, axis=0)
+    rows = core_gather(jnp.concatenate([own, side_swap(own, devices)], axis=0))
+    gate_proj = jnp.dot(rows, w_gate_up[0, 0], preferred_element_type=jnp.float32)
+    up_proj = jnp.dot(rows, w_gate_up[0, 1], preferred_element_type=jnp.float32)
+    activ = (jax.nn.silu(gate_proj) * up_proj).astype(jnp.bfloat16)
+    reduced = core_scatter(jnp.dot(activ, w_down[0], preferred_element_type=jnp.float32))
+    half = own.shape[0]
+    swapped = side_swap(reduced[half:].astype(jnp.bfloat16), devices)
+    total = (reduced[:half] + swapped.astype(jnp.float32)).astype(jnp.bfloat16)
+    total = total.reshape(pair_count, capacity, -1)
+    back = [pair_shift(total[k], k, devices) if k else total[k] for k in range(pair_count)]
+    back = jnp.concatenate(back, axis=0)
+    for table in tables:
+        state += jnp.dot(table, back, preferred_element_type=jnp.float32)
+    return state
 
 
 def on_device(
@@ -75,7 +407,8 @@
     first_pair = jnp.min(jnp.where(held_table > 0, pair_range, pair_count), axis=0)
     second_pair = jnp.max(jnp.where(held_table > 0, pair_range, -1), axis=0)
     upper_half = (row_index >= half_rows)[:, None, None]
-    block_table = jnp.where(upper_half, second_pair ^ own_pair, first_pair ^ own_pair)
+    dest_table = jnp.where(upper_half, second_pair, first_pair)
+    block_table = dest_table ^ own_pair
     match_table = expert_ids[:, :, None] == expert_range
     id_hot = match_table & live_rows[:, None, None]
     named = jnp.sum(id_hot.astype(jnp.float32), axis=1)
@@ -90,10 +423,6 @@
     )
     slot_index = jnp.where(live_rows[:, None], slot_index, pair_count * capacity)
     slot_range = jnp.arange(pair_count * capacity, dtype=jnp.int32)
-    place_hot = (
-        (slot_index[:, 0][None, :] == slot_range[:, None])
-        | (slot_index[:, 1][None, :] == slot_range[:, None])
-    ).astype(jnp.bfloat16)
 
     partial_out = jnp.dot(attn_heads, w_out, preferred_element_type=jnp.float32)
     state = residual_in.astype(jnp.float32) + core_scatter(partial_out)
@@ -102,14 +431,6 @@
     scaled = state * gain_attn
     normed_bf = (scaled * inverse).astype(jnp.bfloat16)
 
-    outgoing = jnp.dot(place_hot, normed_bf, preferred_element_type=jnp.float32).astype(jnp.bfloat16)
-    outgoing = outgoing.reshape(pair_count, capacity, feat_width)
-    chunks = [[k for k in range(pair_count) if (k // 2) % 2 == c] for c in range(2)]
-    arrived = {}
-    for chunk in chunks:
-        for k in chunk:
-            arrived[k] = pair_shift(outgoing[k], k, devices) if k else outgoing[k]
-
     logits = inverse * core_sum(
         jnp.dot(scaled, router.astype(jnp.float32), precision=lax.Precision.HIGHEST)
     )
@@ -122,35 +443,9 @@
     mix_low = (mix - mix_high).astype(jnp.bfloat16)
     mix_high = mix_high.astype(jnp.bfloat16)
 
-    mixture = jnp.zeros_like(state)
-    for chunk in chunks:
-        groups = [chunk[i : i + 2] for i in range(0, len(chunk), 2)]
-        mine = [jnp.concatenate([arrived[k] for k in group], axis=0) for group in groups]
-        others = [side_swap(value, devices) for value in mine]
-        rows = jnp.concatenate([core_gather(value) for value in mine + others], axis=0)
-        gate_proj = jnp.dot(rows, w_gate_up[0, 0], preferred_element_type=jnp.float32)
-        up_proj = jnp.dot(rows, w_gate_up[0, 1], preferred_element_type=jnp.float32)
-        activ = (jax.nn.silu(gate_proj) * up_proj).astype(jnp.bfloat16)
-        down_part = jnp.dot(activ, w_down[0], preferred_element_type=jnp.float32)
-        reduced = core_scatter(down_part)
-        near = len(chunk) * capacity
-        away = reduced[near:].astype(jnp.bfloat16)
-        step = 2 * capacity
-        back = {}
-        for g in reversed(range(len(groups))):
-            swapped = side_swap(away[g * step : (g + 1) * step], devices).astype(jnp.float32)
-            total = (reduced[g * step : (g + 1) * step] + swapped).astype(jnp.bfloat16)
-            for j, k in enumerate(groups[g]):
-                block = total[j * capacity : (j + 1) * capacity]
-                back[k] = pair_shift(block, k, devices) if k else block
-        returned = jnp.concatenate([back[k] for k in chunk], axis=0)
-        pick = lambda table: jnp.concatenate(
-            [table[:, k * capacity : (k + 1) * capacity] for k in chunk], axis=1
-        )
-        mixture += jnp.dot(pick(mix_high), returned, preferred_element_type=jnp.float32)
-        mixture += jnp.dot(pick(mix_low), returned, preferred_element_type=jnp.float32)
-
-    combined = state + mixture
+    run = experts_of_two_cores if lax.axis_size("tp") == 2 else experts_of_any
+    tables = (mix_high, mix_low)
+    combined = run(slot_index.T, normed_bf, capacity, tables, state, w_gate_up, w_down, devices)
     final_sum = core_sum(jnp.sum(combined * combined, axis=1, keepdims=True))
     final_scale = lax.rsqrt(final_sum / full_width + epsilon)
     return (

time: 224 us -> 169 us (0.75)
  matrix products: 78.8 us -> 5.48 us
  Pallas kernels: 0 us -> 60.4 us
  waiting for transfers between devices: 98.9 us -> 55.8 us
  starting transfers between devices: 34.2 us -> 39.2 us
  other arithmetic: 7.06 us -> 3.47 us
    dot_general x11 -> x0, matrix products: 73.3 us -> none  [the longest x2 25.5 us: on_device(): up_proj = jnp.dot(rows, w_gate_up[0, 1], preferred_element_type=jnp.float32)]
    pallas_call x0 -> x23, Pallas kernels: none -> 60.4 us  [the longest x2 33.3 us: gate_up(): pl.pallas_call(lambda *refs: gate_up_kernel(counts, *refs), grid_spec=plt...]
    ppermute x8 -> x9, waiting for transfers between devices: 51.2 us -> 11.8 us  [side_swap(): return lax.ppermute(value, 'req', [(i, i ^ 1) for i in range(devices)])]
    ppermute x14, starting transfers between devices: 11.9 us -> 18.7 us  [pair_shift(): lax.ppermute(value, 'req', [(i, 2 * (i // 2 ^ k) + i % 2) for i in range(...]
    ppermute x14, waiting for transfers between devices: 44.6 us -> 40 us  [pair_shift(): lax.ppermute(value, 'req', [(i, 2 * (i // 2 ^ k) + i % 2) for i in range(...]
    another operation x2 -> x0, other arithmetic: 2.29 us -> none
    ppermute x14 -> x13, starting transfers between devices: 17.1 us -> 15 us  [core_swap(): return lax.ppermute(value, 'tp', [(0, 1), (1, 0)])]
    ppermute x8 -> x9, starting transfers between devices: 5.23 us -> 5.54 us  [side_swap(): return lax.ppermute(value, 'req', [(i, i ^ 1) for i in range(devices)])]
  transfers between devices with their start and end apart: 36 -> 36, of which waited for: 19 -> 17; matrix products, arithmetic and copies ran while one was open for 19% -> 1% of each run, Pallas kernels for 0% -> 31%
where the time goes in v2:
time: 169 us; the launch traced here: 168 us
  Pallas kernels  60.4 us (36%)
  waiting for transfers between devices  55.8 us (33%)
  starting transfers between devices  39.2 us (23%)
  matrix products  5.48 us (3%)
  other arithmetic  3.47 us (2%)
  local copies, waits for them, and re-layouts  1.74 us (1%)
  between operations  1.73 us (1%)
    ppermute x14, waiting for transfers between devices, pair_shift(): lax.ppermute(value, 'req', [(i, 2 * (i // 2 ^ k) + i % 2) for i in range(...  40 us
    pallas_call x2, Pallas kernels, gate_up(): pl.pallas_call(lambda *refs: gate_up_kernel(counts, *refs), grid_spec=plt...  33.3 us
    ppermute x14, starting transfers between devices, pair_shift(): lax.ppermute(value, 'req', [(i, 2 * (i // 2 ^ k) + i % 2) for i in range(...  18.7 us
    ppermute x13, starting transfers between devices, core_swap(): return lax.ppermute(value, 'tp', [(0, 1), (1, 0)])  15 us
    ppermute x9, waiting for transfers between devices, side_swap(): return lax.ppermute(value, 'req', [(i, i ^ 1) for i in range(devices)])  11.8 us
    pallas_call x2, Pallas kernels, down(): pl.pallas_call(down_kernel, grid_spec=pltpu.PrefetchScalarGridSpec(num_sc...  11.6 us
    pallas_call x1, Pallas kernels, down_both(): pl.pallas_call(down_both_kernel, grid_spec=pltpu.PrefetchScalarGridSpec(n...  9.54 us
    ppermute x9, starting transfers between devices, side_swap(): return lax.ppermute(value, 'req', [(i, i ^ 1) for i in range(devices)])  5.54 us
  transfers between devices with their start and end apart: 36, of which 17 were waited for; matrix products, arithmetic and copies ran while one was open for 1% of the time, Pallas kernels for 31%

profile of v2, /device:TPU:15, one launch (start us, length us, event | category | flops | bytes accessed | tf_op | source)
XLA Modules:
  0.0 167.8 jit_solution(17791308433265284805)
XLA Ops:
  0.7 0.9 copy-done
  1.6 4.7 %fusion.14 = f32[128,4096]{1,0:T(8,128)S(1)} fusion(bf16[128,1024]{1,0:T(8,128)(2,1)S(1)} %copy-done, bf16[1024,4096]{1,0:T(8,128)(2,1)} %param.13), kind=kOutput, calls=%fused_computation.45 | convolution fusion | flops 1073741824 | bytes 10747904 | tf_op jit(solution)/shard_map/dot_general | solution.py:427
  6.4 0.7 collective-permute-start
  7.1 0.6 slice.45
  8.8 1.6 multiply_reduce_fusion.1
  10.4 0.4 collective-permute-start.1
  10.8 0.6 fusion.1
  11.8 0.8 collective-permute-done.2
  12.9 0.6 slot_rows.2
  13.4 0.3 collective-permute-start.6
  13.7 2.3 %collective-permute-start.3 = (bf16[48,2048]{1,0:T(8,128)(2,1)S(1)}, bf16[48,2048]{1,0:T(8,128)(2,1)S(1)}, u32[]{:S(2)}, u32[]{:S(2)}) collective-permute-start(bf16[48,2048]{1,0:T(8,128)(2,1)S(1)} %get-tuple-element.25), channel_id=1, source_target_pairs={{0,16},{2,18},{4,20},{6,22},{8,24},{10,26},{12,28},{14,30},{16,0},... | collective-permute-start | bytes 589832 | tf_op jit(solution)/shard_map/ppermute | solution.py:15
  16.0 1.0 collective-permute-start.4
  17.2 2.6 %collective-permute-done.6.refs_1_.refs_2_ = bf16[48,2048]{1,0:T(8,128)(2,1)S(1)} collective-permute-done((bf16[48,2048]{1,0:T(8,128)(2,1)S(1)}, bf16[48,2048]{1,0:T(8,128)(2,1)S(1)}, u32[]{:S(2)}, u32[]{:S(2)}) %collective-permute-start.6) | collective-permute-done | bytes 196640 | tf_op jit(solution)/shard_map/ppermute | solution.py:15
  19.9 0.3 collective-permute-start.10
  20.2 8.8 %collective-permute-done.3.refs_0_ = bf16[48,2048]{1,0:T(8,128)(2,1)S(1)} collective-permute-done((bf16[48,2048]{1,0:T(8,128)(2,1)S(1)}, bf16[48,2048]{1,0:T(8,128)(2,1)S(1)}, u32[]{:S(2)}, u32[]{:S(2)}) %collective-permute-start.3) | collective-permute-done | bytes 196640 | tf_op jit(solution)/shard_map/ppermute | solution.py:15
  29.0 4.2 %collective-permute-done.4.refs_1_ = bf16[48,2048]{1,0:T(8,128)(2,1)S(1)} collective-permute-done((bf16[48,2048]{1,0:T(8,128)(2,1)S(1)}, bf16[48,2048]{1,0:T(8,128)(2,1)S(1)}, u32[]{:S(2)}, u32[]{:S(2)}) %collective-permute-start.4) | collective-permute-done | bytes 196640 | tf_op jit(solution)/shard_map/ppermute | solution.py:15
  33.2 0.3 collective-permute-start.8
  33.5 1.4 collective-permute-start.13
  35.0 0.3 slot_rows.3
  35.3 2.9 %collective-permute-start.14 = (bf16[48,2048]{1,0:T(8,128)(2,1)S(1)}, bf16[48,2048]{1,0:T(8,128)(2,1)S(1)}, u32[]{:S(2)}, u32[]{:S(2)}) collective-permute-start(bf16[48,2048]{1,0:T(8,128)(2,1)S(1)} %get-tuple-element.31), channel_id=1, source_target_pairs={{0,24},{2,26},{4,28},{6,30},{8,16},{10,18},{12,20},{14,22},{16,8},... | collective-permute-start | bytes 589832 | tf_op jit(solution)/shard_map/ppermute | solution.py:15
  38.2 1.0 collective-permute-start.15
  39.2 0.9 collective-permute-done.13.refs_1_
  40.1 2.6 %collective-permute-start.7 = (bf16[96,2048]{1,0:T(8,128)(2,1)S(1)}, bf16[96,2048]{1,0:T(8,128)(2,1)S(1)}, u32[]{:S(2)}, u32[]{:S(2)}) collective-permute-start(bf16[96,2048]{1,0:T(8,128)(2,1)S(1)} %join.6.refs_3_), channel_id=1, source_target_pairs={{0,1},{1,0},{2,3},{3,2},{4,5},{5,4},{6,7},{7,6},{8,9},{9,8},{10,11... | collective-permute-start | bytes 1179656 | tf_op jit(solution)/shard_map/ppermute | solution.py:23
  42.8 7.4 %collective-permute-done.14.refs_0_ = bf16[48,2048]{1,0:T(8,128)(2,1)S(1)} collective-permute-done((bf16[48,2048]{1,0:T(8,128)(2,1)S(1)}, bf16[48,2048]{1,0:T(8,128)(2,1)S(1)}, u32[]{:S(2)}, u32[]{:S(2)}) %collective-permute-start.14) | collective-permute-done | bytes 196640 | tf_op jit(solution)/shard_map/ppermute | solution.py:15
  50.1 3.6 %collective-permute-start.5 = (bf16[96,2048]{1,0:T(8,128)(2,1)S(1)}, bf16[96,2048]{1,0:T(8,128)(2,1)S(1)}, u32[]{:S(2)}, u32[]{:S(2)}) collective-permute-start(bf16[96,2048]{1,0:T(8,128)(2,1)S(1)} %join.5.refs_1_), channel_id=1, source_target_pairs={{0,1},{1,0},{2,3},{3,2},{4,5},{5,4},{6,7},{7,6},{8,9},{9,8},{10,11... | collective-permute-start | bytes 1179656 | tf_op jit(solution)/shard_map/ppermute | solution.py:23
  53.7 2.3 %collective-permute-done.15.refs_1_ = bf16[48,2048]{1,0:T(8,128)(2,1)S(1)} collective-permute-done((bf16[48,2048]{1,0:T(8,128)(2,1)S(1)}, bf16[48,2048]{1,0:T(8,128)(2,1)S(1)}, u32[]{:S(2)}, u32[]{:S(2)}) %collective-permute-start.15) | collective-permute-done | bytes 196640 | tf_op jit(solution)/shard_map/ppermute | solution.py:15
  56.0 1.2 collective-permute-start.17
  57.2 1.9 %collective-permute-start.11 = (bf16[96,2048]{1,0:T(8,128)(2,1)S(1)}, bf16[96,2048]{1,0:T(8,128)(2,1)S(1)}, u32[]{:S(2)}, u32[]{:S(2)}) collective-permute-start(bf16[96,2048]{1,0:T(8,128)(2,1)S(1)} %collective-permute-done.10.refs_7_), channel_id=1, source_target_pairs={{0,1},{1,0},{2,3},{3,2},{4,5},{5,4},{6,7},{7,6},{8,9},{9,8},{10,11... | collective-permute-start | bytes 1179656 | tf_op jit(solution)/shard_map/ppermute | solution.py:23
  59.3 0.3 collective-permute-start.16
  59.6 0.9 collective-permute-done.11.refs_8_
  60.5 0.6 collective-permute-done.9.refs_6_
  61.0 16.5 %gate_up.2.activ_ref.refs_2_ = bf16[384,1792]{1,0:T(8,128)(2,1)S(1)} custom-call(s32[1]{0:T(128)} %bitcast.7.refs_0_.core_ref, bf16[96,2048]{1,0:T(8,128)(2,1)S(1)} %join.5.refs_1_, bf16[96,2048]{1,0:T(8,128)(2,1)S(1)} %collective-permute-done.5.refs_2_, bf16[96,2048]{1,0:T(8,128)(2,1)S(1)} %join.6.refs_3_, ...), custom_call_target="tpu_custom_call" | custom-call | flops 1572864 | bytes 4096 | tf_op jit(solution)/shard_map/gate_up/pallas_call | solution.py:165
  77.7 6.2 %down_away.1 = bf16[384,2048]{1,0:T(8,128)(2,1)} custom-call(s32[1]{0:T(128)} %bitcast.7.refs_0_.core_ref, bf16[384,1792]{1,0:T(8,128)(2,1)S(1)} %gate_up.2.activ_ref.refs_2_, bf16[1,1792,4096]{2,1,0:T(8,128)(2,1)} %weights_ref.5, bf16[192,2048]{1,0:T(8,128)(2,1)S(1)} %join.9.refs_0_.refs_5_), custom_call_target="tpu_custom_call" | custom-call | flops 688128 | bytes 1792 | tf_op jit(solution)/shard_map/down_away/pallas_call | solution.py:197
  83.8 0.4 collective-permute-start.18
  84.4 0.4 collective-permute-start.21
  84.9 5.4 %down_own.1.refs_0_ = f32[384,2048]{1,0:T(8,128)S(1)} custom-call(s32[1]{0:T(128)} %bitcast.7.refs_0_.core_ref, bf16[384,1792]{1,0:T(8,128)(2,1)S(1)} %gate_up.2.activ_ref.refs_2_, bf16[1,1792,4096]{2,1,0:T(8,128)(2,1)} %weights_ref.5), custom_call_target="tpu_custom_call" | custom-call | flops 688128 | bytes 1792 | tf_op jit(solution)/shard_map/down_own/pallas_call | solution.py:197
  90.4 1.7 %add_cores.2 = (f32[192,2048]{1,0:T(8,128)S(1)}, bf16[96,2048]{1,0:T(8,128)(2,1)S(1)}, bf16[96,2048]{1,0:T(8,128)(2,1)S(1)}) custom-call(f32[384,2048]{1,0:T(8,128)S(1)} %down_own.1.refs_0_, bf16[384,2048]{1,0:T(8,128)(2,1)} %collective-permute-done.18.refs_1_), custom_call_target="tpu_custom_call" | custom-call | tf_op jit(solution)/shard_map/add_cores/pallas_call | solution.py:108
  92.1 0.3 collective-permute-start.19
  92.5 1.2 collective-permute-start.25
  93.9 16.8 %gate_up.3.refs_2_.activ_ref = bf16[384,1792]{1,0:T(8,128)(2,1)S(1)} custom-call(s32[1]{0:T(128)} %bitcast.7.refs_0_.core_ref, bf16[96,2048]{1,0:T(8,128)(2,1)S(1)} %copy-done.5, bf16[96,2048]{1,0:T(8,128)(2,1)S(1)} %collective-permute-done.20.refs_2_, bf16[96,2048]{1,0:T(8,128)(2,1)S(1)} %copy-done.3, bf16[96,2048]{1,0:T(8,128)(2,1)S(1)} %collective-permute-done.21.refs_4_, ...), custom_call_target="tpu_custom_call" | custom-call | flops 1572864 | bytes 4096 | tf_op jit(solution)/shard_map/gate_up/pallas_call | solution.py:165
  110.8 2.3 %collective-permute-start.24 = (bf16[48,2048]{1,0:T(8,128)(2,1)S(1)}, bf16[48,2048]{1,0:T(8,128)(2,1)S(1)}, u32[]{:S(2)}, u32[]{:S(2)}) collective-permute-start(bf16[48,2048]{1,0:T(8,128)(2,1)S(1)} %get-tuple-element.36), channel_id=1, source_target_pairs={{0,20},{2,22},{4,16},{6,18},{8,28},{10,30},{12,24},{14,26},{16,4},... | collective-permute-start | bytes 589832 | tf_op jit(solution)/shard_map/ppermute | solution.py:15
  113.3 1.3 collective-permute-start.26
  114.6 9.5 %down_both.1 = (bf16[384,2048]{1,0:T(8,128)(2,1)S(1)}, f32[384,2048]{1,0:T(8,128)S(1)}) custom-call(s32[1]{0:T(128)} %bitcast.7.refs_0_.core_ref, bf16[384,1792]{1,0:T(8,128)(2,1)S(1)} %gate_up.3.refs_2_.activ_ref, bf16[1,1792,4096]{2,1,0:T(8,128)(2,1)} %weights_ref.5, bf16[48,2048]{1,0:T(8,128)(2,1)S(1)} %get-tuple-element.38.refs_0_.refs_3_, ...), custom_call_target="tpu_custom_call" | custom-call | flops 688128 | bytes 1792 | tf_op jit(solution)/shard_map/down_both/pallas_call | solution.py:245
  124.2 1.8 %collective-permute-start.27 = (bf16[384,2048]{1,0:T(8,128)(2,1)S(1)}, bf16[384,2048]{1,0:T(8,128)(2,1)S(1)}, u32[]{:S(2)}, u32[]{:S(2)}) collective-permute-start(bf16[384,2048]{1,0:T(8,128)(2,1)S(1)} %get-tuple-element.41), channel_id=1, source_target_pairs={{0,1},{1,0},{2,3},{3,2},{4,5},{5,4},{6,7},{7,6},{8,9},{9,8},{10,11... | collective-permute-start | bytes 4718600 | tf_op jit(solution)/shard_map/ppermute | solution.py:23
  126.0 1.0 collective-permute-done.24.refs_4_
  127.0 0.7 mix.4.refs_2_
  127.7 0.7 mix.5.refs_2_
  128.4 0.6 collective-permute-done.27.refs_1_
  129.3 0.4 collective-permute-start.28
  129.7 1.2 collective-permute-start.33
  130.8 0.3 collective-permute-start.31
  131.1 8.0 %collective-permute-done.28.refs_1_ = bf16[96,2048]{1,0:T(8,128)(2,1)S(1)} collective-permute-done((bf16[96,2048]{1,0:T(8,128)(2,1)S(1)}, bf16[96,2048]{1,0:T(8,128)(2,1)S(1)}, u32[]{:S(2)}, u32[]{:S(2)}) %collective-permute-start.28) | collective-permute-done | bytes 393248 | tf_op jit(solution)/shard_map/ppermute | solution.py:19
  139.2 2.4 %collective-permute-start.29 = (bf16[48,2048]{1,0:T(8,128)(2,1)S(1)}, bf16[48,2048]{1,0:T(8,128)(2,1)S(1)}, u32[]{:S(2)}, u32[]{:S(2)}) collective-permute-start(bf16[48,2048]{1,0:T(8,128)(2,1)S(1)} %get-tuple-element.44), channel_id=1, source_target_pairs={{0,8},{2,10},{4,12},{6,14},{8,0},{10,2},{12,4},{14,6},{16,24},{18,... | collective-permute-start | bytes 589832 | tf_op jit(solution)/shard_map/ppermute | solution.py:15
  141.5 0.7 collective-permute-start.30
  142.2 1.1 collective-permute-done.33.refs_1_
  143.3 1.5 collective-permute-start.34
  144.8 2.7 %collective-permute-done.31.refs_1_ = bf16[48,2048]{1,0:T(8,128)(2,1)S(1)} collective-permute-done((bf16[48,2048]{1,0:T(8,128)(2,1)S(1)}, bf16[48,2048]{1,0:T(8,128)(2,1)S(1)}, u32[]{:S(2)}, u32[]{:S(2)}) %collective-permute-start.31) | collective-permute-done | bytes 196640 | tf_op jit(solution)/shard_map/ppermute | solution.py:19
  147.6 1.4 collective-permute-start.32
  149.0 0.7 mix.6.refs_2_
  149.7 12.8 %collective-permute-done.32.refs_3_ = bf16[48,2048]{1,0:T(8,128)(2,1)S(1)} collective-permute-done((bf16[48,2048]{1,0:T(8,128)(2,1)S(1)}, bf16[48,2048]{1,0:T(8,128)(2,1)S(1)}, u32[]{:S(2)}, u32[]{:S(2)}) %collective-permute-start.32) | collective-permute-done | bytes 196640 | tf_op jit(solution)/shard_map/ppermute | solution.py:15
  162.5 0.7 mix.7
  163.3 2.6 %collective-permute-start.35 = (f32[128,1]{0,1:T(1,128)S(1)}, f32[128,1]{0,1:T(1,128)S(1)}, u32[]{:S(2)}, u32[]{:S(2)}) collective-permute-start(f32[128,1]{0,1:T(1,128)S(1)} %bitcast.25), channel_id=1, source_target_pairs={{0,1},{1,0},{2,3},{3,2},{4,5},{5,4},{6,7},{7,6},{8,9},{9,8},{10,11... | collective-permute-start | bytes 1544 | tf_op jit(solution)/shard_map/ppermute | solution.py:23
  165.9 0.8 collective-permute-done.35
  166.7 1.1 multiply_convert_fusion
  (80 shorter events, 3.0 us)
Async XLA Ops:
  0.6 1.0 copy-start
  1.6 5.5 %copy-start.10 = (s32[1,5]{1,0:T(1,128)S(1)}, s32[1,5]{1,0:T(1,128)}, u32[]{:S(2)}) copy-start(s32[1,5]{1,0:T(1,128)} %param.17) | copy-start | bytes 64
  1.6 6.8 %copy-start.11 = (s32[8]{0:T(128)S(1)}, s32[8]{0:T(128)}, u32[]{:S(2)}) copy-start(s32[8]{0:T(128)} %param.18) | copy-start | bytes 100
  6.4 2.4 %collective-permute-start = (bf16[128,2048]{1,0:T(8,128)(2,1)S(1)}, bf16[128,2048]{1,0:T(8,128)(2,1)}, u32[]{:S(2)}, u32[]{:S(2)}) collective-permute-start(bf16[128,2048]{1,0:T(8,128)(2,1)S(1)} %select_convert_fusion), channel_id=1, source_target_pairs={{0,1},{1,0},{2,3},{3,2},{4,5},{5,4},{6,7},{7,6},{8,9},{9,8},{10,11... | collective-permute-start | bytes 1572872 | tf_op jit(solution)/shard_map/ppermute | solution.py:23
  8.5 2.3 %copy-start.6 = (f32[2048]{0:T(1024)S(1)}, f32[2048]{0:T(1024)}, u32[]{:S(2)}) copy-start(f32[2048]{0:T(1024)} %param.14) | copy-start | bytes 24580
  8.5 2.3 %copy-start.7 = (bf16[2048,4]{0,1:T(4,128)(2,1)S(1)}, bf16[2048,4]{0,1:T(4,128)(2,1)}, u32[]{:S(2)}) copy-start(bf16[2048,4]{0,1:T(4,128)(2,1)} %param.15) | copy-start | bytes 49156
  10.3 2.3 %copy-start.9 = (s32[128,2]{0,1:T(2,128)S(1)}, s32[128,2]{0,1:T(2,128)}, u32[]{:S(2)}) copy-start(s32[128,2]{0,1:T(2,128)} %param.16) | copy-start | bytes 3076
  10.4 1.3 collective-permute-start.1
  11.4 1.2 collective-permute-start.2
  13.4 6.4 %collective-permute-start.6 = (bf16[48,2048]{1,0:T(8,128)(2,1)S(1)}, bf16[48,2048]{1,0:T(8,128)(2,1)S(1)}, u32[]{:S(2)}, u32[]{:S(2)}) collective-permute-start(bf16[48,2048]{1,0:T(8,128)(2,1)S(1)} %get-tuple-element.28), channel_id=1, source_target_pairs={{0,4},{2,6},{4,0},{6,2},{8,12},{10,14},{12,8},{14,10},{16,20},{18,... | collective-permute-start | bytes 589832 | tf_op jit(solution)/shard_map/ppermute | solution.py:15
  13.7 15.3 %collective-permute-start.3 = (bf16[48,2048]{1,0:T(8,128)(2,1)S(1)}, bf16[48,2048]{1,0:T(8,128)(2,1)S(1)}, u32[]{:S(2)}, u32[]{:S(2)}) collective-permute-start(bf16[48,2048]{1,0:T(8,128)(2,1)S(1)} %get-tuple-element.25), channel_id=1, source_target_pairs={{0,16},{2,18},{4,20},{6,22},{8,24},{10,26},{12,28},{14,30},{16,0},... | collective-permute-start | bytes 589832 | tf_op jit(solution)/shard_map/ppermute | solution.py:15
  16.0 17.2 %collective-permute-start.4 = (bf16[48,2048]{1,0:T(8,128)(2,1)S(1)}, bf16[48,2048]{1,0:T(8,128)(2,1)S(1)}, u32[]{:S(2)}, u32[]{:S(2)}) collective-permute-start(bf16[48,2048]{1,0:T(8,128)(2,1)S(1)} %get-tuple-element.26), channel_id=1, source_target_pairs={{0,20},{2,22},{4,16},{6,18},{8,28},{10,30},{12,24},{14,26},{16,4},... | collective-permute-start | bytes 589832 | tf_op jit(solution)/shard_map/ppermute | solution.py:15
  17.1 21.1 %collective-permute-start.12 = (bf16[48,2048]{1,0:T(8,128)(2,1)S(1)}, bf16[48,2048]{1,0:T(8,128)(2,1)S(1)}, u32[]{:S(2)}, u32[]{:S(2)}) collective-permute-start(bf16[48,2048]{1,0:T(8,128)(2,1)S(1)} %get-tuple-element.29), channel_id=1, source_target_pairs={{0,8},{2,10},{4,12},{6,14},{8,0},{10,2},{12,4},{14,6},{16,24},{18,... | collective-permute-start | bytes 589832 | tf_op jit(solution)/shard_map/ppermute | solution.py:15
  19.9 37.3 %collective-permute-start.10 = (bf16[96,2048]{1,0:T(8,128)(2,1)S(1)}, bf16[96,2048]{1,0:T(8,128)(2,1)S(1)}, u32[]{:S(2)}, u32[]{:S(2)}) collective-permute-start(bf16[96,2048]{1,0:T(8,128)(2,1)S(1)} %join.6.refs_3_), channel_id=1, source_target_pairs={{0,2},{2,0},{4,6},{6,4},{8,10},{10,8},{12,14},{14,12},{16,18},{18,... | collective-permute-start | bytes 1179656 | tf_op jit(solution)/shard_map/ppermute | solution.py:19
  33.2 25.9 %collective-permute-start.8 = (bf16[96,2048]{1,0:T(8,128)(2,1)S(1)}, bf16[96,2048]{1,0:T(8,128)(2,1)S(1)}, u32[]{:S(2)}, u32[]{:S(2)}) collective-permute-start(bf16[96,2048]{1,0:T(8,128)(2,1)S(1)} %join.5.refs_1_), channel_id=1, source_target_pairs={{0,2},{2,0},{4,6},{6,4},{8,10},{10,8},{12,14},{14,12},{16,18},{18,... | collective-permute-start | bytes 1179656 | tf_op jit(solution)/shard_map/ppermute | solution.py:19
  33.5 6.6 %collective-permute-start.13 = (bf16[48,2048]{1,0:T(8,128)(2,1)S(1)}, bf16[48,2048]{1,0:T(8,128)(2,1)S(1)}, u32[]{:S(2)}, u32[]{:S(2)}) collective-permute-start(bf16[48,2048]{1,0:T(8,128)(2,1)S(1)} %get-tuple-element.30), channel_id=1, source_target_pairs={{0,12},{2,14},{4,8},{6,10},{8,4},{10,6},{12,0},{14,2},{16,28},{18,... | collective-permute-start | bytes 589832 | tf_op jit(solution)/shard_map/ppermute | solution.py:15
  35.3 14.9 %collective-permute-start.14 = (bf16[48,2048]{1,0:T(8,128)(2,1)S(1)}, bf16[48,2048]{1,0:T(8,128)(2,1)S(1)}, u32[]{:S(2)}, u32[]{:S(2)}) collective-permute-start(bf16[48,2048]{1,0:T(8,128)(2,1)S(1)} %get-tuple-element.31), channel_id=1, source_target_pairs={{0,24},{2,26},{4,28},{6,30},{8,16},{10,18},{12,20},{14,22},{16,8},... | collective-permute-start | bytes 589832 | tf_op jit(solution)/shard_map/ppermute | solution.py:15
  38.2 17.8 %collective-permute-start.15 = (bf16[48,2048]{1,0:T(8,128)(2,1)S(1)}, bf16[48,2048]{1,0:T(8,128)(2,1)S(1)}, u32[]{:S(2)}, u32[]{:S(2)}) collective-permute-start(bf16[48,2048]{1,0:T(8,128)(2,1)S(1)} %get-tuple-element.32), channel_id=1, source_target_pairs={{0,28},{2,30},{4,24},{6,26},{8,20},{10,22},{12,16},{14,18},{16,12}... | collective-permute-start | bytes 589832 | tf_op jit(solution)/shard_map/ppermute | solution.py:15
  40.1 19.1 %collective-permute-start.7 = (bf16[96,2048]{1,0:T(8,128)(2,1)S(1)}, bf16[96,2048]{1,0:T(8,128)(2,1)S(1)}, u32[]{:S(2)}, u32[]{:S(2)}) collective-permute-start(bf16[96,2048]{1,0:T(8,128)(2,1)S(1)} %join.6.refs_3_), channel_id=1, source_target_pairs={{0,1},{1,0},{2,3},{3,2},{4,5},{5,4},{6,7},{7,6},{8,9},{9,8},{10,11... | collective-permute-start | bytes 1179656 | tf_op jit(solution)/shard_map/ppermute | solution.py:23
  42.8 18.3 %copy-start.2 = (bf16[96,2048]{1,0:T(8,128)(2,1)}, bf16[96,2048]{1,0:T(8,128)(2,1)S(1)}, u32[]{:S(2)}) copy-start(bf16[96,2048]{1,0:T(8,128)(2,1)S(1)} %join.7.refs_10_.refs_3_) | copy-start | bytes 1179652
  50.1 9.4 %collective-permute-start.5 = (bf16[96,2048]{1,0:T(8,128)(2,1)S(1)}, bf16[96,2048]{1,0:T(8,128)(2,1)S(1)}, u32[]{:S(2)}, u32[]{:S(2)}) collective-permute-start(bf16[96,2048]{1,0:T(8,128)(2,1)S(1)} %join.5.refs_1_), channel_id=1, source_target_pairs={{0,1},{1,0},{2,3},{3,2},{4,5},{5,4},{6,7},{7,6},{8,9},{9,8},{10,11... | collective-permute-start | bytes 1179656 | tf_op jit(solution)/shard_map/ppermute | solution.py:23
  56.0 21.6 %collective-permute-start.17 = (bf16[96,2048]{1,0:T(8,128)(2,1)S(1)}, bf16[96,2048]{1,0:T(8,128)(2,1)S(1)}, u32[]{:S(2)}, u32[]{:S(2)}) collective-permute-start(bf16[96,2048]{1,0:T(8,128)(2,1)S(1)} %join.7.refs_10_.refs_3_), channel_id=1, source_target_pairs={{0,2},{2,0},{4,6},{6,4},{8,10},{10,8},{12,14},{14,12},{16,18},{18,... | collective-permute-start | bytes 1179656 | tf_op jit(solution)/shard_map/ppermute | solution.py:19
  57.2 3.3 %collective-permute-start.11 = (bf16[96,2048]{1,0:T(8,128)(2,1)S(1)}, bf16[96,2048]{1,0:T(8,128)(2,1)S(1)}, u32[]{:S(2)}, u32[]{:S(2)}) collective-permute-start(bf16[96,2048]{1,0:T(8,128)(2,1)S(1)} %collective-permute-done.10.refs_7_), channel_id=1, source_target_pairs={{0,1},{1,0},{2,3},{3,2},{4,5},{5,4},{6,7},{7,6},{8,9},{9,8},{10,11... | collective-permute-start | bytes 1179656 | tf_op jit(solution)/shard_map/ppermute | solution.py:23
  59.1 1.9 %collective-permute-start.9 = (bf16[96,2048]{1,0:T(8,128)(2,1)S(1)}, bf16[96,2048]{1,0:T(8,128)(2,1)S(1)}, u32[]{:S(2)}, u32[]{:S(2)}) collective-permute-start(bf16[96,2048]{1,0:T(8,128)(2,1)S(1)} %collective-permute-done.8.refs_5_), channel_id=1, source_target_pairs={{0,1},{1,0},{2,3},{3,2},{4,5},{5,4},{6,7},{7,6},{8,9},{9,8},{10,11... | collective-permute-start | bytes 1179656 | tf_op jit(solution)/shard_map/ppermute | solution.py:23
  59.2 18.3 %copy-start.4 = (bf16[96,2048]{1,0:T(8,128)(2,1)}, bf16[96,2048]{1,0:T(8,128)(2,1)S(1)}, u32[]{:S(2)}) copy-start(bf16[96,2048]{1,0:T(8,128)(2,1)S(1)} %join.8.refs_11_.refs_1_) | copy-start | bytes 1179652
  59.3 18.3 %collective-permute-start.16 = (bf16[96,2048]{1,0:T(8,128)(2,1)S(1)}, bf16[96,2048]{1,0:T(8,128)(2,1)S(1)}, u32[]{:S(2)}, u32[]{:S(2)}) collective-permute-start(bf16[96,2048]{1,0:T(8,128)(2,1)S(1)} %join.8.refs_11_.refs_1_), channel_id=1, source_target_pairs={{0,2},{2,0},{4,6},{6,4},{8,10},{10,8},{12,14},{14,12},{16,18},{18,... | collective-permute-start | bytes 1179656 | tf_op jit(solution)/shard_map/ppermute | solution.py:19
  83.8 6.6 %collective-permute-start.18 = (bf16[384,2048]{1,0:T(8,128)(2,1)}, bf16[384,2048]{1,0:T(8,128)(2,1)}, u32[]{:S(2)}, u32[]{:S(2)}) collective-permute-start(bf16[384,2048]{1,0:T(8,128)(2,1)} %down_away.1), channel_id=1, source_target_pairs={{0,1},{1,0},{2,3},{3,2},{4,5},{5,4},{6,7},{7,6},{8,9},{9,8},{10,11... | collective-permute-start | bytes 4718600 | tf_op jit(solution)/shard_map/ppermute | solution.py:23
  84.2 9.7 %collective-permute-start.22 = (bf16[192,2048]{1,0:T(8,128)(2,1)S(1)}, bf16[192,2048]{1,0:T(8,128)(2,1)}, u32[]{:S(2)}, u32[]{:S(2)}) collective-permute-start(bf16[192,2048]{1,0:T(8,128)(2,1)S(1)} %join.9.refs_0_.refs_5_), channel_id=1, source_target_pairs={{0,1},{1,0},{2,3},{3,2},{4,5},{5,4},{6,7},{7,6},{8,9},{9,8},{10,11... | collective-permute-start | bytes 2359304 | tf_op jit(solution)/shard_map/ppermute | solution.py:23
  84.4 9.5 %collective-permute-start.21 = (bf16[96,2048]{1,0:T(8,128)(2,1)}, bf16[96,2048]{1,0:T(8,128)(2,1)S(1)}, u32[]{:S(2)}, u32[]{:S(2)}) collective-permute-start(bf16[96,2048]{1,0:T(8,128)(2,1)} %copy-done.2), channel_id=1, source_target_pairs={{0,1},{1,0},{2,3},{3,2},{4,5},{5,4},{6,7},{7,6},{8,9},{9,8},{10,11... | collective-permute-start | bytes 1179656 | tf_op jit(solution)/shard_map/ppermute | solution.py:23
  84.8 9.0 %collective-permute-start.20 = (bf16[96,2048]{1,0:T(8,128)(2,1)}, bf16[96,2048]{1,0:T(8,128)(2,1)S(1)}, u32[]{:S(2)}, u32[]{:S(2)}) collective-permute-start(bf16[96,2048]{1,0:T(8,128)(2,1)} %copy-done.4), channel_id=1, source_target_pairs={{0,1},{1,0},{2,3},{3,2},{4,5},{5,4},{6,7},{7,6},{8,9},{9,8},{10,11... | collective-permute-start | bytes 1179656 | tf_op jit(solution)/shard_map/ppermute | solution.py:23
  90.4 3.5 %copy-start.3 = (bf16[96,2048]{1,0:T(8,128)(2,1)S(1)}, bf16[96,2048]{1,0:T(8,128)(2,1)}, u32[]{:S(2)}) copy-start(bf16[96,2048]{1,0:T(8,128)(2,1)} %copy-done.2) | copy-start | bytes 1179652
  90.4 3.5 %copy-start.5 = (bf16[96,2048]{1,0:T(8,128)(2,1)S(1)}, bf16[96,2048]{1,0:T(8,128)(2,1)}, u32[]{:S(2)}) copy-start(bf16[96,2048]{1,0:T(8,128)(2,1)} %copy-done.4) | copy-start | bytes 1179652
  92.1 18.5 %collective-permute-start.19 = (bf16[96,2048]{1,0:T(8,128)(2,1)S(1)}, bf16[96,2048]{1,0:T(8,128)(2,1)S(1)}, u32[]{:S(2)}, u32[]{:S(2)}) collective-permute-start(bf16[96,2048]{1,0:T(8,128)(2,1)S(1)} %get-tuple-element.34), channel_id=1, source_target_pairs={{0,2},{2,0},{4,6},{6,4},{8,10},{10,8},{12,14},{14,12},{16,18},{18,... | collective-permute-start | bytes 1179656 | tf_op jit(solution)/shard_map/ppermute | solution.py:19
  92.5 20.8 %collective-permute-start.25 = (bf16[96,2048]{1,0:T(8,128)(2,1)S(1)}, bf16[96,2048]{1,0:T(8,128)(2,1)S(1)}, u32[]{:S(2)}, u32[]{:S(2)}) collective-permute-start(bf16[96,2048]{1,0:T(8,128)(2,1)S(1)} %get-tuple-element.37), channel_id=1, source_target_pairs={{0,2},{2,0},{4,6},{6,4},{8,10},{10,8},{12,14},{14,12},{16,18},{18,... | collective-permute-start | bytes 1179656 | tf_op jit(solution)/shard_map/ppermute | solution.py:19
  110.7 15.3 %collective-permute-start.23 = (bf16[48,2048]{1,0:T(8,128)(2,1)S(1)}, bf16[48,2048]{1,0:T(8,128)(2,1)S(1)}, u32[]{:S(2)}, u32[]{:S(2)}) collective-permute-start(bf16[48,2048]{1,0:T(8,128)(2,1)S(1)} %get-tuple-element.35), channel_id=1, source_target_pairs={{0,16},{2,18},{4,20},{6,22},{8,24},{10,26},{12,28},{14,30},{16,0},... | collective-permute-start | bytes 589832 | tf_op jit(solution)/shard_map/ppermute | solution.py:15
  110.8 16.2 %collective-permute-start.24 = (bf16[48,2048]{1,0:T(8,128)(2,1)S(1)}, bf16[48,2048]{1,0:T(8,128)(2,1)S(1)}, u32[]{:S(2)}, u32[]{:S(2)}) collective-permute-start(bf16[48,2048]{1,0:T(8,128)(2,1)S(1)} %get-tuple-element.36), channel_id=1, source_target_pairs={{0,20},{2,22},{4,16},{6,18},{8,28},{10,30},{12,24},{14,26},{16,4},... | collective-permute-start | bytes 589832 | tf_op jit(solution)/shard_map/ppermute | solution.py:15
  113.3 14.4 %collective-permute-start.26 = (bf16[48,2048]{1,0:T(8,128)(2,1)S(1)}, bf16[48,2048]{1,0:T(8,128)(2,1)S(1)}, u32[]{:S(2)}, u32[]{:S(2)}) collective-permute-start(bf16[48,2048]{1,0:T(8,128)(2,1)S(1)} %get-tuple-element.39.refs_1_), channel_id=1, source_target_pairs={{0,4},{2,6},{4,0},{6,2},{8,12},{10,14},{12,8},{14,10},{16,20},{18,... | collective-permute-start | bytes 589832 | tf_op jit(solution)/shard_map/ppermute | solution.py:15
  124.2 4.9 %collective-permute-start.27 = (bf16[384,2048]{1,0:T(8,128)(2,1)S(1)}, bf16[384,2048]{1,0:T(8,128)(2,1)S(1)}, u32[]{:S(2)}, u32[]{:S(2)}) collective-permute-start(bf16[384,2048]{1,0:T(8,128)(2,1)S(1)} %get-tuple-element.41), channel_id=1, source_target_pairs={{0,1},{1,0},{2,3},{3,2},{4,5},{5,4},{6,7},{7,6},{8,9},{9,8},{10,11... | collective-permute-start | bytes 4718600 | tf_op jit(solution)/shard_map/ppermute | solution.py:23
  129.3 9.8 %collective-permute-start.28 = (bf16[96,2048]{1,0:T(8,128)(2,1)S(1)}, bf16[96,2048]{1,0:T(8,128)(2,1)S(1)}, u32[]{:S(2)}, u32[]{:S(2)}) collective-permute-start(bf16[96,2048]{1,0:T(8,128)(2,1)S(1)} %get-tuple-element.43), channel_id=1, source_target_pairs={{0,2},{2,0},{4,6},{6,4},{8,10},{10,8},{12,14},{14,12},{16,18},{18,... | collective-permute-start | bytes 1179656 | tf_op jit(solution)/shard_map/ppermute | solution.py:19
  129.7 13.6 %collective-permute-start.33 = (bf16[48,2048]{1,0:T(8,128)(2,1)S(1)}, bf16[48,2048]{1,0:T(8,128)(2,1)S(1)}, u32[]{:S(2)}, u32[]{:S(2)}) collective-permute-start(bf16[48,2048]{1,0:T(8,128)(2,1)S(1)} %get-tuple-element.47), channel_id=1, source_target_pairs={{0,2},{2,0},{4,6},{6,4},{8,10},{10,8},{12,14},{14,12},{16,18},{18,... | collective-permute-start | bytes 589832 | tf_op jit(solution)/shard_map/ppermute | solution.py:19
  130.8 16.7 %collective-permute-start.31 = (bf16[48,2048]{1,0:T(8,128)(2,1)S(1)}, bf16[48,2048]{1,0:T(8,128)(2,1)S(1)}, u32[]{:S(2)}, u32[]{:S(2)}) collective-permute-start(bf16[48,2048]{1,0:T(8,128)(2,1)S(1)} %get-tuple-element.46), channel_id=1, source_target_pairs={{0,2},{2,0},{4,6},{6,4},{8,10},{10,8},{12,14},{14,12},{16,18},{18,... | collective-permute-start | bytes 589832 | tf_op jit(solution)/shard_map/ppermute | solution.py:19
  139.2 9.8 %collective-permute-start.29 = (bf16[48,2048]{1,0:T(8,128)(2,1)S(1)}, bf16[48,2048]{1,0:T(8,128)(2,1)S(1)}, u32[]{:S(2)}, u32[]{:S(2)}) collective-permute-start(bf16[48,2048]{1,0:T(8,128)(2,1)S(1)} %get-tuple-element.44), channel_id=1, source_target_pairs={{0,8},{2,10},{4,12},{6,14},{8,0},{10,2},{12,4},{14,6},{16,24},{18,... | collective-permute-start | bytes 589832 | tf_op jit(solution)/shard_map/ppermute | solution.py:15
  141.5 7.4 %collective-permute-start.30 = (bf16[48,2048]{1,0:T(8,128)(2,1)S(1)}, bf16[48,2048]{1,0:T(8,128)(2,1)S(1)}, u32[]{:S(2)}, u32[]{:S(2)}) collective-permute-start(bf16[48,2048]{1,0:T(8,128)(2,1)S(1)} %get-tuple-element.45), channel_id=1, source_target_pairs={{0,12},{2,14},{4,8},{6,10},{8,4},{10,6},{12,0},{14,2},{16,28},{18,... | collective-permute-start | bytes 589832 | tf_op jit(solution)/shard_map/ppermute | solution.py:15
  143.3 6.3 %collective-permute-start.34 = (bf16[48,2048]{1,0:T(8,128)(2,1)S(1)}, bf16[48,2048]{1,0:T(8,128)(2,1)S(1)}, u32[]{:S(2)}, u32[]{:S(2)}) collective-permute-start(bf16[48,2048]{1,0:T(8,128)(2,1)S(1)} %add_sides.9), channel_id=1, source_target_pairs={{0,28},{2,30},{4,24},{6,26},{8,20},{10,22},{12,16},{14,18},{16,12}... | collective-permute-start | bytes 589832 | tf_op jit(solution)/shard_map/ppermute | solution.py:15
  147.6 14.9 %collective-permute-start.32 = (bf16[48,2048]{1,0:T(8,128)(2,1)S(1)}, bf16[48,2048]{1,0:T(8,128)(2,1)S(1)}, u32[]{:S(2)}, u32[]{:S(2)}) collective-permute-start(bf16[48,2048]{1,0:T(8,128)(2,1)S(1)} %add_sides.8), channel_id=1, source_target_pairs={{0,24},{2,26},{4,28},{6,30},{8,16},{10,18},{12,20},{14,22},{16,8},... | collective-permute-start | bytes 589832 | tf_op jit(solution)/shard_map/ppermute | solution.py:15
  149.6 17.1 %copy-start.8 = (f32[2048]{0:T(1024)S(1)}, f32[2048]{0:T(1024)}, u32[]{:S(2)}) copy-start(f32[2048]{0:T(1024)} %param.21) | copy-start | bytes 24580
  162.5 5.4 %copy-start.1 = (bf16[128,1024]{1,0:T(8,128)(2,1)S(1)}, bf16[128,1024]{1,0:T(8,128)(2,1)}, u32[]{:S(2)}) copy-start(bf16[128,1024]{1,0:T(8,128)(2,1)} %param.11) | copy-start | bytes 786436
  163.3 3.4 %collective-permute-start.35 = (f32[128,1]{0,1:T(1,128)S(1)}, f32[128,1]{0,1:T(1,128)S(1)}, u32[]{:S(2)}, u32[]{:S(2)}) collective-permute-start(f32[128,1]{0,1:T(1,128)S(1)} %bitcast.25), channel_id=1, source_target_pairs={{0,1},{1,0},{2,3},{3,2},{4,5},{5,4},{6,7},{7,6},{8,9},{9,8},{10,11... | collective-permute-start | bytes 1544 | tf_op jit(solution)/shard_map/ppermute | solution.py:23

commit v3 on v2

--- a/solution.py
+++ b/solution.py
@@ -6,6 +6,7 @@
 from jax.sharding import PartitionSpec as P
 
 epsilon = 1e-05
+UNITS = 256
 LONG = 20_000_000_000
 WHOLE = pl.BlockSpec(memory_space=pltpu.VMEM)
 ANYWHERE = pl.BlockSpec(memory_space=pl.ANY)
@@ -157,18 +158,20 @@
     out_ref[...] = (gate * jax.nn.sigmoid(gate) * up).astype(jnp.bfloat16)
 
 
-def gate_up(core, pieces, weights, after):
+def gate_up(core, pieces, weights, after, blocks=None):
     counts = [own.shape[0] for own, _ in pieces]
     rows = sum(counts)
-    _, _, depth, units = weights.shape
-    block = 256
+    depth = weights.shape[2]
+    block = UNITS
+    first, last = blocks or (0, weights.shape[3] // block)
+    units = (last - first) * block
     return pl.pallas_call(
         lambda *refs: gate_up_kernel(counts, *refs),
         grid_spec=pltpu.PrefetchScalarGridSpec(
             num_scalar_prefetch=1,
             grid=(units // block,),
             in_specs=[WHOLE] * (2 * len(counts))
-            + [pl.BlockSpec((1, 2, depth, block), lambda i, core: (0, 0, 0, i))]
+            + [pl.BlockSpec((1, 2, depth, block), lambda i, core: (0, 0, 0, first + i))]
             + [ANYWHERE] * len(after),
             out_specs=pl.BlockSpec((rows, block), lambda i, core: (0, i)),
             scratch_shapes=[pltpu.VMEM((rows, depth), jnp.bfloat16)],
@@ -189,7 +192,7 @@
     ).astype(out_ref.dtype)
 
 
-def down(core, activ, weights, away, after):
+def down(core, activ, weights, away, after, flops=0):
     rows, units = activ.shape
     width = weights.shape[2] // 2
     block = 1024
@@ -212,15 +215,20 @@
         out_shape=jax.ShapeDtypeStruct((rows, width), jnp.bfloat16 if away else jnp.float32),
         compiler_params=pltpu.CompilerParams(vmem_limit_bytes=44 << 20),
         cost_estimate=pl.CostEstimate(
-            flops=rows * units, bytes_accessed=units, transcendentals=0
+            flops=flops or rows * units, bytes_accessed=units, transcendentals=0
         ),
         name="down_away" if away else "down_own",
     )(core, activ, weights, *after)
 
 
-def down_both_kernel(core_ref, activ_ref, weights_ref, *refs):
+def down_both_kernel(count, core_ref, *refs):
+    weights_ref = refs[count]
     away_ref, own_ref = refs[-2:]
-    product = jnp.dot(activ_ref[...], weights_ref[0], preferred_element_type=jnp.float32)
+    product, start = 0.0, 0
+    for ref in refs[:count]:
+        part = weights_ref[0, start : start + ref.shape[1]]
+        product += jnp.dot(ref[...], part, preferred_element_type=jnp.float32)
+        start += ref.shape[1]
     half = pl.num_programs(0) // 2
 
     @pl.when(pl.program_id(0) < half)
@@ -233,7 +241,7 @@
 
 
 def down_both(core, activ, weights, after):
-    rows, units = activ.shape
+    rows, units = activ[0].shape[0], weights.shape[1]
     width = weights.shape[2] // 2
     block = 1024
     half = width // block
@@ -243,14 +251,14 @@
         return (0, 0, side * half + lax.rem(i, half))
 
     return pl.pallas_call(
-        down_both_kernel,
+        lambda *refs: down_both_kernel(len(activ), *refs),
         grid_spec=pltpu.PrefetchScalarGridSpec(
             num_scalar_prefetch=1,
             grid=(2 * half,),
             in_specs=[
-                pl.BlockSpec((rows, units), lambda i, core: (0, 0)),
-                pl.BlockSpec((1, units, block), columns),
+                pl.BlockSpec((rows, part.shape[1]), lambda i, core: (0, 0)) for part in activ
             ]
+            + [pl.BlockSpec((1, units, block), columns)]
             + [ANYWHERE] * len(after),
             out_specs=[
                 pl.BlockSpec((rows, block), lambda i, core: (0, jnp.minimum(i, half - 1))),
@@ -264,7 +272,7 @@
         compiler_params=pltpu.CompilerParams(vmem_limit_bytes=44 << 20),
         cost_estimate=pl.CostEstimate(flops=rows * units, bytes_accessed=units, transcendentals=0),
         name="down_both",
-    )(core, activ, weights, *after)
+    )(core, *activ, weights, *after)
 
 
 def mix_kernel(count, high_ref, low_ref, base_ref, *refs):
@@ -310,46 +318,50 @@
     arrived = dict(zip(far, send(far, [outgoing[k] for k in far])))
     arrived |= zip(near, send(near, [outgoing[k] for k in near]))
     arrived |= zip(near_later, send(near_later, [outgoing[k] for k in near_later]))
-    outgoing = slot_rows(far_later, capacity, slots, rows, [arrived[near[-1]]])
-    arrived |= zip(far_later, send(far_later, [outgoing[k] for k in far_later]))
-
+    later = slot_rows(far_later, capacity, slots, rows, [arrived[near[-1]]])
+    arrived |= zip(far_later, send(far_later, [later[k] for k in far_later]))
+
+    spare = join([outgoing[near[0]]], [], LONG)
     near_own = join([arrived[k] for k in near], [])
-    near_nbr = side_swap(near_own, devices)
-    far_own = join([arrived[k] for k in far], [], LONG)
+    near_nbr = join([side_swap(near_own, devices)], [spare])
+    far_own = join([arrived[k] for k in far], [near_nbr])
     far_nbr = side_swap(far_own, devices)
-    near_later_own = join([arrived[k] for k in near_later], [])
+    near_later_own = join([arrived[k] for k in near_later], [near_nbr])
     near_later_nbr = side_swap(near_later_own, devices)
-    far_later_own = join([arrived[k] for k in far_later], [], LONG)
+
+    pieces = [(x, core_swap(x)) for x in (far_own, near_own, far_nbr, near_nbr)]
+    activ = gate_up(core, pieces, w_gate_up, [near_later_own])
+    far_later_own = join([arrived[k] for k in far_later], [activ])
     far_later_nbr = side_swap(far_later_own, devices)
-
-    pieces = [(x, core_swap(x)) for x in (far_own, near_own, far_nbr, near_nbr)]
-    activ = gate_up(core, pieces, w_gate_up, [near_later_own, far_later_own])
-    later = join([far_later_nbr, near_later_nbr], [activ])
-    away = core_swap(down(core, activ, w_down, True, [later]))
-    kept = down(core, activ, w_down, False, [])
+    near_later_nbr = join([near_later_nbr], [activ])
+    away = down(core, activ, w_down, True, [far_later_own, near_later_nbr])
+    far_later_nbr = join([far_later_nbr], [away])
+    away = core_swap(away)
+    kept = down(core, activ, w_down, False, [far_later_nbr], LONG)
     own, far_other, near_other = add_cores(kept, away, [size, size], [])
-    pieces = [(x, core_swap(x)) for x in (far_later_own, near_later_own, later)]
-    activ = gate_up(core, pieces, w_gate_up, [own])
+    pieces = [far_later_own, near_later_own, far_later_nbr, near_later_nbr]
+    pieces = [(x, core_swap(x)) for x in pieces]
+    unit_blocks = w_gate_up.shape[3] // UNITS
+    split = unit_blocks // 2 + 1
+    activ = [gate_up(core, pieces, w_gate_up, [own], (0, split))]
 
     far_other = side_swap(far_other, devices)
     near_other = side_swap(near_other, devices)
-    far_back = send(far, add_sides(own, 0, far_other, [capacity] * quarter, [activ]))
-    totals = add_sides(own, size, near_other, [capacity] * quarter, [activ])
+    totals = add_sides(own, 0, far_other, [capacity] * quarter, activ[:1])
+    far_back = send(far, totals)
+    activ.append(gate_up(core, pieces, w_gate_up, totals, (split, unit_blocks)))
+    totals = add_sides(own, size, near_other, [capacity] * quarter, activ[1:])
     near_back = send(near, totals)
     away, kept = down_both(core, activ, w_down, totals)
     state = mix(columns(far[0]), state, far_back, [kept], LONG)
     state = mix(columns(near[0]), state, near_back, [])
-    counts = [capacity] * quarter + [size]
-    own, *others = add_cores(kept, core_swap(away), counts, [state])
-    far_back = []
-    for j, k in enumerate(far_later):
+    own, *others = add_cores(kept, core_swap(away), [capacity] * 2 * quarter, [state])
+    back = []
+    for j, k in enumerate(far_later + near_later):
         other = side_swap(others[j], devices)
-        (total,) = add_sides(own, j * capacity, other, [capacity], [])
-        far_back += send([k], [total])
-    other = side_swap(others[-1], devices)
-    near_back = send(near_later, add_sides(own, size, other, [capacity] * quarter, []))
-    state = mix(columns(near_later[0]), state, near_back, [])
-    return mix(columns(far_later[0]), state, far_back, [])
+        back += send([k], add_sides(own, j * capacity, other, [capacity], []))
+    state = mix(columns(far_later[0]), state, back[:quarter], [], LONG)
+    return mix(columns(near_later[0]), state, back[quarter:], [])
 
 
 def experts_of_any(slots, rows, capacity, tables, state, w_gate_up, w_down, devices):

time: 169 us -> 161 us (0.953)
  waiting for transfers between devices: 55.8 us -> 47.9 us
  starting transfers between devices: 39.2 us -> 35.3 us
  Pallas kernels: 60.4 us -> 62.3 us
    ppermute x14, waiting for transfers between devices: 40 us -> 17.2 us  [pair_shift(): lax.ppermute(value, 'req', [(i, 2 * (i // 2 ^ k) + i % 2) for i in range(...]
    ppermute x9 -> x10, waiting for transfers between devices: 11.8 us -> 27.2 us  [side_swap(): return lax.ppermute(value, 'req', [(i, i ^ 1) for i in range(devices)])]
    ppermute x14, starting transfers between devices: 18.7 us -> 15.9 us  [pair_shift(): lax.ppermute(value, 'req', [(i, 2 * (i // 2 ^ k) + i % 2) for i in range(...]
    pallas_call x2 -> x3, Pallas kernels: 33.3 us -> 35.9 us  [gate_up(): pl.pallas_call(lambda *refs: gate_up_kernel(counts, *refs), grid_spec=plt...]
    ppermute x13 -> x14, starting transfers between devices: 15 us -> 12.6 us  [core_swap(): return lax.ppermute(value, 'tp', [(0, 1), (1, 0)])]
    ppermute x9 -> x10, starting transfers between devices: 5.54 us -> 6.76 us  [side_swap(): return lax.ppermute(value, 'req', [(i, i ^ 1) for i in range(devices)])]
    ppermute x13 -> x14, waiting for transfers between devices: 4.04 us -> 3.59 us  [core_swap(): return lax.ppermute(value, 'tp', [(0, 1), (1, 0)])]
  transfers between devices with their start and end apart: 36 -> 38, of which waited for: 17 -> 18; matrix products, arithmetic and copies ran while one was open for 1% -> 1% of each run, Pallas kernels for 31% -> 38%
where the time goes in v3:
time: 161 us; the launch traced here: 159 us
  Pallas kernels  62.3 us (39%)
  waiting for transfers between devices  47.9 us (30%)
  starting transfers between devices  35.3 us (22%)
  matrix products  5.48 us (3%)
  other arithmetic  3.47 us (2%)
  local copies, waits for them, and re-layouts  2.56 us (2%)
  between operations  1.72 us (1%)
    pallas_call x3, Pallas kernels, gate_up(): pl.pallas_call(lambda *refs: gate_up_kernel(counts, *refs), grid_spec=plt...  35.9 us
    ppermute x10, waiting for transfers between devices, side_swap(): return lax.ppermute(value, 'req', [(i, i ^ 1) for i in range(devices)])  27.2 us
    ppermute x14, waiting for transfers between devices, pair_shift(): lax.ppermute(value, 'req', [(i, 2 * (i // 2 ^ k) + i % 2) for i in range(...  17.2 us
    ppermute x14, starting transfers between devices, pair_shift(): lax.ppermute(value, 'req', [(i, 2 * (i // 2 ^ k) + i % 2) for i in range(...  15.9 us
    ppermute x14, starting transfers between devices, core_swap(): return lax.ppermute(value, 'tp', [(0, 1), (1, 0)])  12.6 us
    pallas_call x2, Pallas kernels, down(): pl.pallas_call(down_kernel, grid_spec=pltpu.PrefetchScalarGridSpec(num_sc...  10.8 us
    pallas_call x1, Pallas kernels, down_both(): pl.pallas_call(lambda *refs: down_both_kernel(len(activ), *refs), grid_sp...  9.53 us
    ppermute x10, starting transfers between devices, side_swap(): return lax.ppermute(value, 'req', [(i, i ^ 1) for i in range(devices)])  6.76 us
  transfers between devices with their start and end apart: 38, of which 18 were waited for; matrix products, arithmetic and copies ran while one was open for 1% of the time, Pallas kernels for 38%

profile of v3, /device:TPU:15, one launch (start us, length us, event | category | flops | bytes accessed | tf_op | source)
XLA Modules:
  0.0 158.8 jit_solution(7468992749956122853)
XLA Ops:
  0.7 0.9 copy-done
  1.6 4.7 %fusion.14 = f32[128,4096]{1,0:T(8,128)S(1)} fusion(bf16[128,1024]{1,0:T(8,128)(2,1)S(1)} %copy-done, bf16[1024,4096]{1,0:T(8,128)(2,1)} %param.13), kind=kOutput, calls=%fused_computation.45 | convolution fusion | flops 1073741824 | bytes 10747904 | tf_op jit(solution)/shard_map/dot_general | solution.py:439
  6.4 0.7 collective-permute-start
  7.1 0.6 slice.45
  8.8 1.6 multiply_reduce_fusion.1
  10.4 0.4 collective-permute-start.1
  10.8 0.6 fusion.1
  11.8 0.8 collective-permute-done.2
  12.9 1.2 slot_rows.2
  14.3 2.3 %collective-permute-start.3 = (bf16[48,2048]{1,0:T(8,128)(2,1)S(1)}, bf16[48,2048]{1,0:T(8,128)(2,1)S(1)}, u32[]{:S(2)}, u32[]{:S(2)}) collective-permute-start(bf16[48,2048]{1,0:T(8,128)(2,1)S(1)} %get-tuple-element.24), channel_id=1, source_target_pairs={{0,16},{2,18},{4,20},{6,22},{8,24},{10,26},{12,28},{14,30},{16,0},... | collective-permute-start | bytes 589832 | tf_op jit(solution)/shard_map/ppermute | solution.py:16
  16.7 1.0 collective-permute-start.4
  17.7 2.8 %collective-permute-done.5.refs_1_.refs_2_ = bf16[48,2048]{1,0:T(8,128)(2,1)S(1)} collective-permute-done((bf16[48,2048]{1,0:T(8,128)(2,1)S(1)}, bf16[48,2048]{1,0:T(8,128)(2,1)S(1)}, u32[]{:S(2)}, u32[]{:S(2)}) %collective-permute-start.5) | collective-permute-done | bytes 196640 | tf_op jit(solution)/shard_map/ppermute | solution.py:16
  20.5 0.3 collective-permute-start.6
  20.8 9.4 %collective-permute-done.6.refs_0_ = bf16[96,2048]{1,0:T(8,128)(2,1)S(1)} collective-permute-done((bf16[96,2048]{1,0:T(8,128)(2,1)S(1)}, bf16[96,2048]{1,0:T(8,128)(2,1)S(1)}, u32[]{:S(2)}, u32[]{:S(2)}) %collective-permute-start.6) | collective-permute-done | bytes 393248 | tf_op jit(solution)/shard_map/ppermute | solution.py:20
  30.2 3.6 %collective-permute-done.4.refs_1_ = bf16[48,2048]{1,0:T(8,128)(2,1)S(1)} collective-permute-done((bf16[48,2048]{1,0:T(8,128)(2,1)S(1)}, bf16[48,2048]{1,0:T(8,128)(2,1)S(1)}, u32[]{:S(2)}, u32[]{:S(2)}) %collective-permute-start.4) | collective-permute-done | bytes 196640 | tf_op jit(solution)/shard_map/ppermute | solution.py:16
  34.2 0.8 collective-permute-start.8
  34.9 2.0 %collective-permute-start.12 = (bf16[48,2048]{1,0:T(8,128)(2,1)S(1)}, bf16[48,2048]{1,0:T(8,128)(2,1)S(1)}, u32[]{:S(2)}, u32[]{:S(2)}) collective-permute-start(bf16[48,2048]{1,0:T(8,128)(2,1)S(1)} %get-tuple-element.28), channel_id=1, source_target_pairs={{0,8},{2,10},{4,12},{6,14},{8,0},{10,2},{12,4},{14,6},{16,24},{18,... | collective-permute-start | bytes 589832 | tf_op jit(solution)/shard_map/ppermute | solution.py:16
  37.0 0.4 collective-permute-start.13
  37.3 0.6 collective-permute-start.7
  37.9 4.3 %collective-permute-done.12.refs_0_ = bf16[48,2048]{1,0:T(8,128)(2,1)S(1)} collective-permute-done((bf16[48,2048]{1,0:T(8,128)(2,1)S(1)}, bf16[48,2048]{1,0:T(8,128)(2,1)S(1)}, u32[]{:S(2)}, u32[]{:S(2)}) %collective-permute-start.12) | collective-permute-done | bytes 196640 | tf_op jit(solution)/shard_map/ppermute | solution.py:16
  42.2 0.8 collective-permute-start.11
  43.0 1.2 collective-permute-done.9.refs_5_
  44.2 1.2 collective-permute-start.10
  45.4 0.6 rev.3
  46.3 0.4 collective-permute-done.13.refs_1_
  46.7 2.1 %collective-permute-start.14 = (bf16[48,2048]{1,0:T(8,128)(2,1)S(1)}, bf16[48,2048]{1,0:T(8,128)(2,1)S(1)}, u32[]{:S(2)}, u32[]{:S(2)}) collective-permute-start(bf16[48,2048]{1,0:T(8,128)(2,1)S(1)} %get-tuple-element.30), channel_id=1, source_target_pairs={{0,24},{2,26},{4,28},{6,30},{8,16},{10,18},{12,20},{14,22},{16,8},... | collective-permute-start | bytes 589832 | tf_op jit(solution)/shard_map/ppermute | solution.py:16
  48.8 1.0 collective-permute-start.15
  49.8 1.0 join.12.refs_10_.refs_3_
  50.7 1.3 collective-permute-start.17
  52.0 17.2 %gate_up.3.refs_2_.refs_1_.activ_ref = bf16[384,1792]{1,0:T(8,128)(2,1)S(1)} custom-call(s32[1]{0:T(128)} %bitcast.7.refs_0_.core_ref, bf16[96,2048]{1,0:T(8,128)(2,1)S(1)} %join.11.refs_1_, bf16[96,2048]{1,0:T(8,128)(2,1)} %collective-permute-done.7.refs_2_, bf16[96,2048]{1,0:T(8,128)(2,1)S(1)} %join.8.refs_3_, ...), custom_call_target="tpu_custom_call" | custom-call | flops 1572864 | bytes 4096 | tf_op jit(solution)/shard_map/gate_up/pallas_call | solution.py:168
  69.3 0.3 collective-permute-start.16
  69.9 1.2 collective-permute-start.21
  71.3 0.5 collective-permute-start.23
  71.8 5.3 %down_away.1.refs_1_ = bf16[384,2048]{1,0:T(8,128)(2,1)S(1)} custom-call(s32[1]{0:T(128)} %bitcast.7.refs_0_.core_ref, bf16[384,1792]{1,0:T(8,128)(2,1)S(1)} %gate_up.3.refs_2_.refs_1_.activ_ref, bf16[1,1792,4096]{2,1,0:T(8,128)(2,1)} %refs_3_.1, bf16[96,2048]{1,0:T(8,128)(2,1)S(1)} %join.13.refs_0_.refs_1_, bf16[96,2048]{1,0:T(8,128)(2,1)S(1)} %join.14.refs_1_.refs_7_), custom_call_target="tpu_custom_call" | custom-call | flops 688128 | bytes 1792 | tf_op jit(solution)/shard_map/down_away/pallas_call | solution.py:200
  77.2 1.6 %collective-permute-done.16.refs_0_ = bf16[96,2048]{1,0:T(8,128)(2,1)S(1)} collective-permute-done((bf16[96,2048]{1,0:T(8,128)(2,1)S(1)}, bf16[96,2048]{1,0:T(8,128)(2,1)S(1)}, u32[]{:S(2)}, u32[]{:S(2)}) %collective-permute-start.16) | collective-permute-done | bytes 393248 | tf_op jit(solution)/shard_map/ppermute | solution.py:20
  78.9 5.4 %down_own.1.refs_0_ = f32[384,2048]{1,0:T(8,128)S(1)} custom-call(s32[1]{0:T(128)} %bitcast.7.refs_0_.core_ref, bf16[384,1792]{1,0:T(8,128)(2,1)S(1)} %gate_up.3.refs_2_.refs_1_.activ_ref, bf16[1,1792,4096]{2,1,0:T(8,128)(2,1)} %refs_3_.1, bf16[96,2048]{1,0:T(8,128)(2,1)S(1)} %join.15.refs_0_.refs_5_), custom_call_target="tpu_custom_call" | custom-call | flops 20000000000 | bytes 1792 | tf_op jit(solution)/shard_map/down_own/pallas_call | solution.py:200
  84.3 2.1 %collective-permute-start.22 = (bf16[96,2048]{1,0:T(8,128)(2,1)S(1)}, bf16[96,2048]{1,0:T(8,128)(2,1)S(1)}, u32[]{:S(2)}, u32[]{:S(2)}) collective-permute-start(bf16[96,2048]{1,0:T(8,128)(2,1)S(1)} %join.15.refs_0_.refs_5_), channel_id=1, source_target_pairs={{0,1},{1,0},{2,3},{3,2},{4,5},{5,4},{6,7},{7,6},{8,9},{9,8},{10,11... | collective-permute-start | bytes 1179656 | tf_op jit(solution)/shard_map/ppermute | solution.py:24
  86.7 0.3 collective-permute-start.19
  87.1 1.2 collective-permute-start.26
  88.4 10.3 %gate_up.4.refs_2_.refs_1_ = bf16[384,1024]{1,0:T(8,128)(2,1)S(1)} custom-call(s32[1]{0:T(128)} %bitcast.7.refs_0_.core_ref, bf16[96,2048]{1,0:T(8,128)(2,1)S(1)} %join.13.refs_0_.refs_1_, bf16[96,2048]{1,0:T(8,128)(2,1)S(1)} %collective-permute-done.20.refs_2_, bf16[96,2048]{1,0:T(8,128)(2,1)S(1)} %join.12.refs_10_.refs_3_, ...), custom_call_target="tpu_custom_call" | custom-call | flops 1572864 | bytes 4096 | tf_op jit(solution)/shard_map/gate_up/pallas_call | solution.py:168
  98.8 4.3 %collective-permute-start.24 = (bf16[48,2048]{1,0:T(8,128)(2,1)S(1)}, bf16[48,2048]{1,0:T(8,128)(2,1)S(1)}, u32[]{:S(2)}, u32[]{:S(2)}) collective-permute-start(bf16[48,2048]{1,0:T(8,128)(2,1)S(1)} %get-tuple-element.34.refs_10_), channel_id=1, source_target_pairs={{0,16},{2,18},{4,20},{6,22},{8,24},{10,26},{12,28},{14,30},{16,0},... | collective-permute-start | bytes 589832 | tf_op jit(solution)/shard_map/ppermute | solution.py:16
  103.3 8.4 %gate_up.5.refs_2_ = bf16[384,768]{1,0:T(8,128)(2,1)S(1)} custom-call(s32[1]{0:T(128)} %bitcast.7.refs_0_.core_ref, bf16[96,2048]{1,0:T(8,128)(2,1)S(1)} %join.13.refs_0_.refs_1_, bf16[96,2048]{1,0:T(8,128)(2,1)S(1)} %collective-permute-done.20.refs_2_, bf16[96,2048]{1,0:T(8,128)(2,1)S(1)} %join.12.refs_10_.refs_3_, ...), custom_call_target="tpu_custom_call" | custom-call | flops 1572864 | bytes 4096 | tf_op jit(solution)/shard_map/gate_up/pallas_call | solution.py:168
  111.7 1.3 collective-permute-start.27
  113.1 9.5 %down_both.1 = (bf16[384,2048]{1,0:T(8,128)(2,1)S(1)}, f32[384,2048]{1,0:T(8,128)S(1)}) custom-call(s32[1]{0:T(128)} %bitcast.7.refs_0_.core_ref, bf16[384,1024]{1,0:T(8,128)(2,1)S(1)} %gate_up.4.refs_2_.refs_1_, bf16[384,768]{1,0:T(8,128)(2,1)S(1)} %gate_up.5.refs_2_, bf16[1,1792,4096]{2,1,0:T(8,128)(2,1)} %refs_3_.1, ...), custom_call_target="tpu_custom_call" | custom-call | flops 688128 | bytes 1792 | tf_op jit(solution)/shard_map/down_both/pallas_call | solution.py:253
  122.6 1.2 collective-permute-start.28
  123.8 0.7 mix.4.refs_2_
  124.5 0.7 mix.5.refs_2_
  125.2 1.7 %collective-permute-done.28.refs_1_ = bf16[384,2048]{1,0:T(8,128)(2,1)S(1)} collective-permute-done((bf16[384,2048]{1,0:T(8,128)(2,1)S(1)}, bf16[384,2048]{1,0:T(8,128)(2,1)S(1)}, u32[]{:S(2)}, u32[]{:S(2)}) %collective-permute-start.28) | collective-permute-done | bytes 1572896 | tf_op jit(solution)/shard_map/ppermute | solution.py:24
  127.4 1.2 collective-permute-start.29
  128.9 1.2 collective-permute-start.33
  130.1 3.1 %collective-permute-done.31.refs_1_ = bf16[48,2048]{1,0:T(8,128)(2,1)S(1)} collective-permute-done((bf16[48,2048]{1,0:T(8,128)(2,1)S(1)}, bf16[48,2048]{1,0:T(8,128)(2,1)S(1)}, u32[]{:S(2)}, u32[]{:S(2)}) %collective-permute-start.31) | collective-permute-done | bytes 196640 | tf_op jit(solution)/shard_map/ppermute | solution.py:20
  133.4 4.1 %collective-permute-done.29.refs_1_ = bf16[48,2048]{1,0:T(8,128)(2,1)S(1)} collective-permute-done((bf16[48,2048]{1,0:T(8,128)(2,1)S(1)}, bf16[48,2048]{1,0:T(8,128)(2,1)S(1)}, u32[]{:S(2)}, u32[]{:S(2)}) %collective-permute-start.29) | collective-permute-done | bytes 196640 | tf_op jit(solution)/shard_map/ppermute | solution.py:20
  137.6 4.1 %collective-permute-done.35.refs_1_ = bf16[48,2048]{1,0:T(8,128)(2,1)S(1)} collective-permute-done((bf16[48,2048]{1,0:T(8,128)(2,1)S(1)}, bf16[48,2048]{1,0:T(8,128)(2,1)S(1)}, u32[]{:S(2)}, u32[]{:S(2)}) %collective-permute-start.35) | collective-permute-done | bytes 196640 | tf_op jit(solution)/shard_map/ppermute | solution.py:20
  141.7 0.6 collective-permute-start.36
  142.3 3.6 %collective-permute-done.33.refs_1_ = bf16[48,2048]{1,0:T(8,128)(2,1)S(1)} collective-permute-done((bf16[48,2048]{1,0:T(8,128)(2,1)S(1)}, bf16[48,2048]{1,0:T(8,128)(2,1)S(1)}, u32[]{:S(2)}, u32[]{:S(2)}) %collective-permute-start.33) | collective-permute-done | bytes 196640 | tf_op jit(solution)/shard_map/ppermute | solution.py:20
  145.9 0.6 collective-permute-start.34
  146.5 1.7 %collective-permute-done.32.refs_4_ = bf16[48,2048]{1,0:T(8,128)(2,1)S(1)} collective-permute-done((bf16[48,2048]{1,0:T(8,128)(2,1)S(1)}, bf16[48,2048]{1,0:T(8,128)(2,1)S(1)}, u32[]{:S(2)}, u32[]{:S(2)}) %collective-permute-start.32) | collective-permute-done | bytes 196640 | tf_op jit(solution)/shard_map/ppermute | solution.py:16
  148.3 3.3 %collective-permute-done.30.refs_3_ = bf16[48,2048]{1,0:T(8,128)(2,1)S(1)} collective-permute-done((bf16[48,2048]{1,0:T(8,128)(2,1)S(1)}, bf16[48,2048]{1,0:T(8,128)(2,1)S(1)}, u32[]{:S(2)}, u32[]{:S(2)}) %collective-permute-start.30) | collective-permute-done | bytes 196640 | tf_op jit(solution)/shard_map/ppermute | solution.py:16
  151.6 0.7 mix.6.refs_2_
  152.3 1.0 collective-permute-done.34.refs_3_
  153.3 0.7 mix.7
  154.1 2.7 %collective-permute-start.37 = (f32[128,1]{0,1:T(1,128)S(1)}, f32[128,1]{0,1:T(1,128)S(1)}, u32[]{:S(2)}, u32[]{:S(2)}) collective-permute-start(f32[128,1]{0,1:T(1,128)S(1)} %bitcast.25), channel_id=1, source_target_pairs={{0,1},{1,0},{2,3},{3,2},{4,5},{5,4},{6,7},{7,6},{8,9},{9,8},{10,11... | collective-permute-start | bytes 1544 | tf_op jit(solution)/shard_map/ppermute | solution.py:24
  156.8 0.8 collective-permute-done.37
  157.7 1.1 multiply_convert_fusion
  (83 shorter events, 4.6 us)
Async XLA Ops:
  0.6 1.0 copy-start
  1.6 5.5 %copy-start.7 = (s32[1,5]{1,0:T(1,128)S(1)}, s32[1,5]{1,0:T(1,128)}, u32[]{:S(2)}) copy-start(s32[1,5]{1,0:T(1,128)} %param.17) | copy-start | bytes 64
  1.6 6.8 %copy-start.8 = (s32[8]{0:T(128)S(1)}, s32[8]{0:T(128)}, u32[]{:S(2)}) copy-start(s32[8]{0:T(128)} %param.18) | copy-start | bytes 100
  6.4 2.4 %collective-permute-start = (bf16[128,2048]{1,0:T(8,128)(2,1)S(1)}, bf16[128,2048]{1,0:T(8,128)(2,1)}, u32[]{:S(2)}, u32[]{:S(2)}) collective-permute-start(bf16[128,2048]{1,0:T(8,128)(2,1)S(1)} %select_convert_fusion), channel_id=1, source_target_pairs={{0,1},{1,0},{2,3},{3,2},{4,5},{5,4},{6,7},{7,6},{8,9},{9,8},{10,11... | collective-permute-start | bytes 1572872 | tf_op jit(solution)/shard_map/ppermute | solution.py:24
  8.5 2.3 %copy-start.2 = (f32[2048]{0:T(1024)S(1)}, f32[2048]{0:T(1024)}, u32[]{:S(2)}) copy-start(f32[2048]{0:T(1024)} %param.14) | copy-start | bytes 24580
  8.5 2.3 %copy-start.3 = (bf16[2048,4]{0,1:T(4,128)(2,1)S(1)}, bf16[2048,4]{0,1:T(4,128)(2,1)}, u32[]{:S(2)}) copy-start(bf16[2048,4]{0,1:T(4,128)(2,1)} %param.15) | copy-start | bytes 49156
  10.3 2.3 %copy-start.6 = (s32[128,2]{0,1:T(2,128)S(1)}, s32[128,2]{0,1:T(2,128)}, u32[]{:S(2)}) copy-start(s32[128,2]{0,1:T(2,128)} %param.16) | copy-start | bytes 3076
  10.4 1.3 collective-permute-start.1
  11.4 1.2 collective-permute-start.2
  14.1 6.3 %collective-permute-start.5 = (bf16[48,2048]{1,0:T(8,128)(2,1)S(1)}, bf16[48,2048]{1,0:T(8,128)(2,1)S(1)}, u32[]{:S(2)}, u32[]{:S(2)}) collective-permute-start(bf16[48,2048]{1,0:T(8,128)(2,1)S(1)} %get-tuple-element.27), channel_id=1, source_target_pairs={{0,4},{2,6},{4,0},{6,2},{8,12},{10,14},{12,8},{14,10},{16,20},{18,... | collective-permute-start | bytes 589832 | tf_op jit(solution)/shard_map/ppermute | solution.py:16
  14.3 15.9 %collective-permute-start.3 = (bf16[48,2048]{1,0:T(8,128)(2,1)S(1)}, bf16[48,2048]{1,0:T(8,128)(2,1)S(1)}, u32[]{:S(2)}, u32[]{:S(2)}) collective-permute-start(bf16[48,2048]{1,0:T(8,128)(2,1)S(1)} %get-tuple-element.24), channel_id=1, source_target_pairs={{0,16},{2,18},{4,20},{6,22},{8,24},{10,26},{12,28},{14,30},{16,0},... | collective-permute-start | bytes 589832 | tf_op jit(solution)/shard_map/ppermute | solution.py:16
  16.7 17.2 %collective-permute-start.4 = (bf16[48,2048]{1,0:T(8,128)(2,1)S(1)}, bf16[48,2048]{1,0:T(8,128)(2,1)S(1)}, u32[]{:S(2)}, u32[]{:S(2)}) collective-permute-start(bf16[48,2048]{1,0:T(8,128)(2,1)S(1)} %get-tuple-element.25), channel_id=1, source_target_pairs={{0,20},{2,22},{4,16},{6,18},{8,28},{10,30},{12,24},{14,26},{16,4},... | collective-permute-start | bytes 589832 | tf_op jit(solution)/shard_map/ppermute | solution.py:16
  20.5 9.7 %collective-permute-start.6 = (bf16[96,2048]{1,0:T(8,128)(2,1)S(1)}, bf16[96,2048]{1,0:T(8,128)(2,1)S(1)}, u32[]{:S(2)}, u32[]{:S(2)}) collective-permute-start(bf16[96,2048]{1,0:T(8,128)(2,1)S(1)} %join.8.refs_3_), channel_id=1, source_target_pairs={{0,2},{2,0},{4,6},{6,4},{8,10},{10,8},{12,14},{14,12},{16,18},{18,... | collective-permute-start | bytes 1179656 | tf_op jit(solution)/shard_map/ppermute | solution.py:20
  33.8 10.4 %collective-permute-start.9 = (bf16[96,2048]{1,0:T(8,128)(2,1)S(1)}, bf16[96,2048]{1,0:T(8,128)(2,1)S(1)}, u32[]{:S(2)}, u32[]{:S(2)}) collective-permute-start(bf16[96,2048]{1,0:T(8,128)(2,1)S(1)} %join.11.refs_1_), channel_id=1, source_target_pairs={{0,2},{2,0},{4,6},{6,4},{8,10},{10,8},{12,14},{14,12},{16,18},{18,... | collective-permute-start | bytes 1179656 | tf_op jit(solution)/shard_map/ppermute | solution.py:20
  34.2 14.6 %collective-permute-start.8 = (bf16[96,2048]{1,0:T(8,128)(2,1)S(1)}, bf16[96,2048]{1,0:T(8,128)(2,1)}, u32[]{:S(2)}, u32[]{:S(2)}) collective-permute-start(bf16[96,2048]{1,0:T(8,128)(2,1)S(1)} %join.8.refs_3_), channel_id=1, source_target_pairs={{0,1},{1,0},{2,3},{3,2},{4,5},{5,4},{6,7},{7,6},{8,9},{9,8},{10,11... | collective-permute-start | bytes 1179656 | tf_op jit(solution)/shard_map/ppermute | solution.py:24
  34.9 7.3 %collective-permute-start.12 = (bf16[48,2048]{1,0:T(8,128)(2,1)S(1)}, bf16[48,2048]{1,0:T(8,128)(2,1)S(1)}, u32[]{:S(2)}, u32[]{:S(2)}) collective-permute-start(bf16[48,2048]{1,0:T(8,128)(2,1)S(1)} %get-tuple-element.28), channel_id=1, source_target_pairs={{0,8},{2,10},{4,12},{6,14},{8,0},{10,2},{12,4},{14,6},{16,24},{18,... | collective-permute-start | bytes 589832 | tf_op jit(solution)/shard_map/ppermute | solution.py:16
  37.0 9.8 %collective-permute-start.13 = (bf16[48,2048]{1,0:T(8,128)(2,1)}, bf16[48,2048]{1,0:T(8,128)(2,1)}, u32[]{:S(2)}, u32[]{:S(2)}) collective-permute-start(bf16[48,2048]{1,0:T(8,128)(2,1)} %get-tuple-element.29), channel_id=1, source_target_pairs={{0,12},{2,14},{4,8},{6,10},{8,4},{10,6},{12,0},{14,2},{16,28},{18,... | collective-permute-start | bytes 589832 | tf_op jit(solution)/shard_map/ppermute | solution.py:16
  37.3 13.4 %collective-permute-start.7 = (bf16[96,2048]{1,0:T(8,128)(2,1)S(1)}, bf16[96,2048]{1,0:T(8,128)(2,1)}, u32[]{:S(2)}, u32[]{:S(2)}) collective-permute-start(bf16[96,2048]{1,0:T(8,128)(2,1)S(1)} %join.11.refs_1_), channel_id=1, source_target_pairs={{0,1},{1,0},{2,3},{3,2},{4,5},{5,4},{6,7},{7,6},{8,9},{9,8},{10,11... | collective-permute-start | bytes 1179656 | tf_op jit(solution)/shard_map/ppermute | solution.py:24
  42.2 9.8 %collective-permute-start.11 = (bf16[96,2048]{1,0:T(8,128)(2,1)S(1)}, bf16[96,2048]{1,0:T(8,128)(2,1)}, u32[]{:S(2)}, u32[]{:S(2)}) collective-permute-start(bf16[96,2048]{1,0:T(8,128)(2,1)S(1)} %join.10.refs_2_.refs_7_), channel_id=1, source_target_pairs={{0,1},{1,0},{2,3},{3,2},{4,5},{5,4},{6,7},{7,6},{8,9},{9,8},{10,11... | collective-permute-start | bytes 1179656 | tf_op jit(solution)/shard_map/ppermute | solution.py:24
  44.2 7.8 %collective-permute-start.10 = (bf16[96,2048]{1,0:T(8,128)(2,1)S(1)}, bf16[96,2048]{1,0:T(8,128)(2,1)}, u32[]{:S(2)}, u32[]{:S(2)}) collective-permute-start(bf16[96,2048]{1,0:T(8,128)(2,1)S(1)} %collective-permute-done.9.refs_5_), channel_id=1, source_target_pairs={{0,1},{1,0},{2,3},{3,2},{4,5},{5,4},{6,7},{7,6},{8,9},{9,8},{10,11... | collective-permute-start | bytes 1179656 | tf_op jit(solution)/shard_map/ppermute | solution.py:24
  46.7 22.5 %collective-permute-start.14 = (bf16[48,2048]{1,0:T(8,128)(2,1)S(1)}, bf16[48,2048]{1,0:T(8,128)(2,1)S(1)}, u32[]{:S(2)}, u32[]{:S(2)}) collective-permute-start(bf16[48,2048]{1,0:T(8,128)(2,1)S(1)} %get-tuple-element.30), channel_id=1, source_target_pairs={{0,24},{2,26},{4,28},{6,30},{8,16},{10,18},{12,20},{14,22},{16,8},... | collective-permute-start | bytes 589832 | tf_op jit(solution)/shard_map/ppermute | solution.py:16
  48.8 20.5 %collective-permute-start.15 = (bf16[48,2048]{1,0:T(8,128)(2,1)S(1)}, bf16[48,2048]{1,0:T(8,128)(2,1)S(1)}, u32[]{:S(2)}, u32[]{:S(2)}) collective-permute-start(bf16[48,2048]{1,0:T(8,128)(2,1)S(1)} %get-tuple-element.31), channel_id=1, source_target_pairs={{0,28},{2,30},{4,24},{6,26},{8,20},{10,22},{12,16},{14,18},{16,12}... | collective-permute-start | bytes 589832 | tf_op jit(solution)/shard_map/ppermute | solution.py:16
  50.7 20.5 %collective-permute-start.17 = (bf16[96,2048]{1,0:T(8,128)(2,1)S(1)}, bf16[96,2048]{1,0:T(8,128)(2,1)S(1)}, u32[]{:S(2)}, u32[]{:S(2)}) collective-permute-start(bf16[96,2048]{1,0:T(8,128)(2,1)S(1)} %join.12.refs_10_.refs_3_), channel_id=1, source_target_pairs={{0,2},{2,0},{4,6},{6,4},{8,10},{10,8},{12,14},{14,12},{16,18},{18,... | collective-permute-start | bytes 1179656 | tf_op jit(solution)/shard_map/ppermute | solution.py:20
  69.3 0.7 copy-start.5
  69.3 9.5 %collective-permute-start.16 = (bf16[96,2048]{1,0:T(8,128)(2,1)S(1)}, bf16[96,2048]{1,0:T(8,128)(2,1)S(1)}, u32[]{:S(2)}, u32[]{:S(2)}) collective-permute-start(bf16[96,2048]{1,0:T(8,128)(2,1)S(1)} %join.13.refs_0_.refs_1_), channel_id=1, source_target_pairs={{0,2},{2,0},{4,6},{6,4},{8,10},{10,8},{12,14},{14,12},{16,18},{18,... | collective-permute-start | bytes 1179656 | tf_op jit(solution)/shard_map/ppermute | solution.py:20
  69.9 17.1 %collective-permute-start.21 = (bf16[96,2048]{1,0:T(8,128)(2,1)S(1)}, bf16[96,2048]{1,0:T(8,128)(2,1)S(1)}, u32[]{:S(2)}, u32[]{:S(2)}) collective-permute-start(bf16[96,2048]{1,0:T(8,128)(2,1)S(1)} %join.12.refs_10_.refs_3_), channel_id=1, source_target_pairs={{0,1},{1,0},{2,3},{3,2},{4,5},{5,4},{6,7},{7,6},{8,9},{9,8},{10,11... | collective-permute-start | bytes 1179656 | tf_op jit(solution)/shard_map/ppermute | solution.py:24
  71.1 17.3 %collective-permute-start.20 = (bf16[96,2048]{1,0:T(8,128)(2,1)S(1)}, bf16[96,2048]{1,0:T(8,128)(2,1)S(1)}, u32[]{:S(2)}, u32[]{:S(2)}) collective-permute-start(bf16[96,2048]{1,0:T(8,128)(2,1)S(1)} %join.13.refs_0_.refs_1_), channel_id=1, source_target_pairs={{0,1},{1,0},{2,3},{3,2},{4,5},{5,4},{6,7},{7,6},{8,9},{9,8},{10,11... | collective-permute-start | bytes 1179656 | tf_op jit(solution)/shard_map/ppermute | solution.py:24
  71.3 17.2 %collective-permute-start.23 = (bf16[96,2048]{1,0:T(8,128)(2,1)S(1)}, bf16[96,2048]{1,0:T(8,128)(2,1)S(1)}, u32[]{:S(2)}, u32[]{:S(2)}) collective-permute-start(bf16[96,2048]{1,0:T(8,128)(2,1)S(1)} %join.14.refs_1_.refs_7_), channel_id=1, source_target_pairs={{0,1},{1,0},{2,3},{3,2},{4,5},{5,4},{6,7},{7,6},{8,9},{9,8},{10,11... | collective-permute-start | bytes 1179656 | tf_op jit(solution)/shard_map/ppermute | solution.py:24
  77.1 9.4 %collective-permute-start.18 = (bf16[384,2048]{1,0:T(8,128)(2,1)S(1)}, bf16[384,2048]{1,0:T(8,128)(2,1)S(1)}, u32[]{:S(2)}, u32[]{:S(2)}) collective-permute-start(bf16[384,2048]{1,0:T(8,128)(2,1)S(1)} %down_away.1.refs_1_), channel_id=1, source_target_pairs={{0,1},{1,0},{2,3},{3,2},{4,5},{5,4},{6,7},{7,6},{8,9},{9,8},{10,11... | collective-permute-start | bytes 4718600 | tf_op jit(solution)/shard_map/ppermute | solution.py:24
  84.3 4.1 %collective-permute-start.22 = (bf16[96,2048]{1,0:T(8,128)(2,1)S(1)}, bf16[96,2048]{1,0:T(8,128)(2,1)S(1)}, u32[]{:S(2)}, u32[]{:S(2)}) collective-permute-start(bf16[96,2048]{1,0:T(8,128)(2,1)S(1)} %join.15.refs_0_.refs_5_), channel_id=1, source_target_pairs={{0,1},{1,0},{2,3},{3,2},{4,5},{5,4},{6,7},{7,6},{8,9},{9,8},{10,11... | collective-permute-start | bytes 1179656 | tf_op jit(solution)/shard_map/ppermute | solution.py:24
  86.7 12.0 %collective-permute-start.19 = (bf16[96,2048]{1,0:T(8,128)(2,1)S(1)}, bf16[96,2048]{1,0:T(8,128)(2,1)S(1)}, u32[]{:S(2)}, u32[]{:S(2)}) collective-permute-start(bf16[96,2048]{1,0:T(8,128)(2,1)S(1)} %get-tuple-element.33), channel_id=1, source_target_pairs={{0,2},{2,0},{4,6},{6,4},{8,10},{10,8},{12,14},{14,12},{16,18},{18,... | collective-permute-start | bytes 1179656 | tf_op jit(solution)/shard_map/ppermute | solution.py:20
  87.1 24.6 %collective-permute-start.26 = (bf16[96,2048]{1,0:T(8,128)(2,1)S(1)}, bf16[96,2048]{1,0:T(8,128)(2,1)S(1)}, u32[]{:S(2)}, u32[]{:S(2)}) collective-permute-start(bf16[96,2048]{1,0:T(8,128)(2,1)S(1)} %get-tuple-element.36), channel_id=1, source_target_pairs={{0,2},{2,0},{4,6},{6,4},{8,10},{10,8},{12,14},{14,12},{16,18},{18,... | collective-permute-start | bytes 1179656 | tf_op jit(solution)/shard_map/ppermute | solution.py:20
  98.8 25.0 %collective-permute-start.24 = (bf16[48,2048]{1,0:T(8,128)(2,1)S(1)}, bf16[48,2048]{1,0:T(8,128)(2,1)S(1)}, u32[]{:S(2)}, u32[]{:S(2)}) collective-permute-start(bf16[48,2048]{1,0:T(8,128)(2,1)S(1)} %get-tuple-element.34.refs_10_), channel_id=1, source_target_pairs={{0,16},{2,18},{4,20},{6,22},{8,24},{10,26},{12,28},{14,30},{16,0},... | collective-permute-start | bytes 589832 | tf_op jit(solution)/shard_map/ppermute | solution.py:16
  103.1 20.7 %collective-permute-start.25 = (bf16[48,2048]{1,0:T(8,128)(2,1)S(1)}, bf16[48,2048]{1,0:T(8,128)(2,1)S(1)}, u32[]{:S(2)}, u32[]{:S(2)}) collective-permute-start(bf16[48,2048]{1,0:T(8,128)(2,1)S(1)} %get-tuple-element.35.refs_11_), channel_id=1, source_target_pairs={{0,20},{2,22},{4,16},{6,18},{8,28},{10,30},{12,24},{14,26},{16,4},... | collective-permute-start | bytes 589832 | tf_op jit(solution)/shard_map/ppermute | solution.py:16
  111.7 12.8 %collective-permute-start.27 = (bf16[48,2048]{1,0:T(8,128)(2,1)S(1)}, bf16[48,2048]{1,0:T(8,128)(2,1)S(1)}, u32[]{:S(2)}, u32[]{:S(2)}) collective-permute-start(bf16[48,2048]{1,0:T(8,128)(2,1)S(1)} %get-tuple-element.38.refs_5_), channel_id=1, source_target_pairs={{0,4},{2,6},{4,0},{6,2},{8,12},{10,14},{12,8},{14,10},{16,20},{18,... | collective-permute-start | bytes 589832 | tf_op jit(solution)/shard_map/ppermute | solution.py:16
  122.6 4.2 %collective-permute-start.28 = (bf16[384,2048]{1,0:T(8,128)(2,1)S(1)}, bf16[384,2048]{1,0:T(8,128)(2,1)S(1)}, u32[]{:S(2)}, u32[]{:S(2)}) collective-permute-start(bf16[384,2048]{1,0:T(8,128)(2,1)S(1)} %get-tuple-element.40), channel_id=1, source_target_pairs={{0,1},{1,0},{2,3},{3,2},{4,5},{5,4},{6,7},{7,6},{8,9},{9,8},{10,11... | collective-permute-start | bytes 4718600 | tf_op jit(solution)/shard_map/ppermute | solution.py:24
  127.1 6.1 %collective-permute-start.31 = (bf16[48,2048]{1,0:T(8,128)(2,1)S(1)}, bf16[48,2048]{1,0:T(8,128)(2,1)S(1)}, u32[]{:S(2)}, u32[]{:S(2)}) collective-permute-start(bf16[48,2048]{1,0:T(8,128)(2,1)S(1)} %get-tuple-element.43), channel_id=1, source_target_pairs={{0,2},{2,0},{4,6},{6,4},{8,10},{10,8},{12,14},{14,12},{16,18},{18,... | collective-permute-start | bytes 589832 | tf_op jit(solution)/shard_map/ppermute | solution.py:20
  127.4 10.0 %collective-permute-start.29 = (bf16[48,2048]{1,0:T(8,128)(2,1)S(1)}, bf16[48,2048]{1,0:T(8,128)(2,1)S(1)}, u32[]{:S(2)}, u32[]{:S(2)}) collective-permute-start(bf16[48,2048]{1,0:T(8,128)(2,1)S(1)} %get-tuple-element.42), channel_id=1, source_target_pairs={{0,2},{2,0},{4,6},{6,4},{8,10},{10,8},{12,14},{14,12},{16,18},{18,... | collective-permute-start | bytes 589832 | tf_op jit(solution)/shard_map/ppermute | solution.py:20
  128.6 13.0 %collective-permute-start.35 = (bf16[48,2048]{1,0:T(8,128)(2,1)S(1)}, bf16[48,2048]{1,0:T(8,128)(2,1)S(1)}, u32[]{:S(2)}, u32[]{:S(2)}) collective-permute-start(bf16[48,2048]{1,0:T(8,128)(2,1)S(1)} %get-tuple-element.45), channel_id=1, source_target_pairs={{0,2},{2,0},{4,6},{6,4},{8,10},{10,8},{12,14},{14,12},{16,18},{18,... | collective-permute-start | bytes 589832 | tf_op jit(solution)/shard_map/ppermute | solution.py:20
  128.9 17.0 %collective-permute-start.33 = (bf16[48,2048]{1,0:T(8,128)(2,1)S(1)}, bf16[48,2048]{1,0:T(8,128)(2,1)S(1)}, u32[]{:S(2)}, u32[]{:S(2)}) collective-permute-start(bf16[48,2048]{1,0:T(8,128)(2,1)S(1)} %get-tuple-element.44), channel_id=1, source_target_pairs={{0,2},{2,0},{4,6},{6,4},{8,10},{10,8},{12,14},{14,12},{16,18},{18,... | collective-permute-start | bytes 589832 | tf_op jit(solution)/shard_map/ppermute | solution.py:20
  133.3 15.0 %collective-permute-start.32 = (bf16[48,2048]{1,0:T(8,128)(2,1)S(1)}, bf16[48,2048]{1,0:T(8,128)(2,1)S(1)}, u32[]{:S(2)}, u32[]{:S(2)}) collective-permute-start(bf16[48,2048]{1,0:T(8,128)(2,1)S(1)} %add_sides.9), channel_id=1, source_target_pairs={{0,28},{2,30},{4,24},{6,26},{8,20},{10,22},{12,16},{14,18},{16,12}... | collective-permute-start | bytes 589832 | tf_op jit(solution)/shard_map/ppermute | solution.py:16
  137.5 14.0 %collective-permute-start.30 = (bf16[48,2048]{1,0:T(8,128)(2,1)S(1)}, bf16[48,2048]{1,0:T(8,128)(2,1)S(1)}, u32[]{:S(2)}, u32[]{:S(2)}) collective-permute-start(bf16[48,2048]{1,0:T(8,128)(2,1)S(1)} %add_sides.8), channel_id=1, source_target_pairs={{0,24},{2,26},{4,28},{6,30},{8,16},{10,18},{12,20},{14,22},{16,8},... | collective-permute-start | bytes 589832 | tf_op jit(solution)/shard_map/ppermute | solution.py:16
  141.7 10.5 %collective-permute-start.36 = (bf16[48,2048]{1,0:T(8,128)(2,1)S(1)}, bf16[48,2048]{1,0:T(8,128)(2,1)S(1)}, u32[]{:S(2)}, u32[]{:S(2)}) collective-permute-start(bf16[48,2048]{1,0:T(8,128)(2,1)S(1)} %add_sides.11), channel_id=1, source_target_pairs={{0,12},{2,14},{4,8},{6,10},{8,4},{10,6},{12,0},{14,2},{16,28},{18,... | collective-permute-start | bytes 589832 | tf_op jit(solution)/shard_map/ppermute | solution.py:16
  145.9 7.3 %collective-permute-start.34 = (bf16[48,2048]{1,0:T(8,128)(2,1)S(1)}, bf16[48,2048]{1,0:T(8,128)(2,1)S(1)}, u32[]{:S(2)}, u32[]{:S(2)}) collective-permute-start(bf16[48,2048]{1,0:T(8,128)(2,1)S(1)} %add_sides.10), channel_id=1, source_target_pairs={{0,8},{2,10},{4,12},{6,14},{8,0},{10,2},{12,4},{14,6},{16,24},{18,... | collective-permute-start | bytes 589832 | tf_op jit(solution)/shard_map/ppermute | solution.py:16
  152.2 5.4 %copy-start.4 = (f32[2048]{0:T(1024)S(1)}, f32[2048]{0:T(1024)}, u32[]{:S(2)}) copy-start(f32[2048]{0:T(1024)} %param.21) | copy-start | bytes 24580
  153.3 5.5 %copy-start.1 = (bf16[128,1024]{1,0:T(8,128)(2,1)S(1)}, bf16[128,1024]{1,0:T(8,128)(2,1)}, u32[]{:S(2)}) copy-start(bf16[128,1024]{1,0:T(8,128)(2,1)} %param.11) | copy-start | bytes 786436
  154.1 3.5 %collective-permute-start.37 = (f32[128,1]{0,1:T(1,128)S(1)}, f32[128,1]{0,1:T(1,128)S(1)}, u32[]{:S(2)}, u32[]{:S(2)}) collective-permute-start(f32[128,1]{0,1:T(1,128)S(1)} %bitcast.25), channel_id=1, source_target_pairs={{0,1},{1,0},{2,3},{3,2},{4,5},{5,4},{6,7},{7,6},{8,9},{9,8},{10,11... | collective-permute-start | bytes 1544 | tf_op jit(solution)/shard_map/ppermute | solution.py:24

commit v4 on v3

--- a/solution.py
+++ b/solution.py
@@ -325,7 +325,8 @@
     near_own = join([arrived[k] for k in near], [])
     near_nbr = join([side_swap(near_own, devices)], [spare])
     far_own = join([arrived[k] for k in far], [near_nbr])
-    far_nbr = side_swap(far_own, devices)
+    spare = join([outgoing[near[0]]], [far_own], LONG)
+    far_nbr = join([side_swap(far_own, devices)], [spare])
     near_later_own = join([arrived[k] for k in near_later], [near_nbr])
     near_later_nbr = side_swap(near_later_own, devices)
 
@@ -447,7 +448,8 @@
         jnp.dot(scaled, router.astype(jnp.float32), precision=lax.Precision.HIGHEST)
     )
     chosen = jnp.sum(match_table.astype(jnp.float32) * logits[:, None, :], axis=2)
-    weights = jax.nn.sigmoid(chosen - chosen[:, ::-1])
+    lead = chosen[:, 0:1] - chosen[:, 1:2]
+    weights = jax.nn.sigmoid(jnp.concatenate([lead, -lead], axis=1))
     mix = jnp.where(slot_index[:, 0:1] == slot_range, weights[:, 0:1], 0.0) + jnp.where(
         slot_index[:, 1:2] == slot_range, weights[:, 1:2], 0.0
     )

time: 161 us -> 158 us (0.981)
  Pallas kernels: 62.3 us -> 60.2 us
    ppermute x14, waiting for transfers between devices: 17.2 us -> 12.8 us  [pair_shift(): lax.ppermute(value, 'req', [(i, 2 * (i // 2 ^ k) + i % 2) for i in range(...]
    ppermute x10, waiting for transfers between devices: 27.2 us -> 31.4 us  [side_swap(): return lax.ppermute(value, 'req', [(i, i ^ 1) for i in range(devices)])]
  transfers between devices with their start and end apart: 38 -> 38, of which waited for: 18 -> 17; matrix products, arithmetic and copies ran while one was open for 1% -> 1% of each run, Pallas kernels for 38% -> 38%
where the time goes in v4:
time: 158 us; the launch traced here: 156 us
  Pallas kernels  60.2 us (38%)
  waiting for transfers between devices  47.7 us (30%)
  starting transfers between devices  35.9 us (23%)
  matrix products  5.48 us (3%)
  other arithmetic  3.48 us (2%)
  between operations  1.74 us (1%)
  local copies, waits for them, and re-layouts  1.69 us (1%)
    pallas_call x3, Pallas kernels, gate_up(): pl.pallas_call(lambda *refs: gate_up_kernel(counts, *refs), grid_spec=plt...  35.3 us
    ppermute x10, waiting for transfers between devices, side_swap(): return lax.ppermute(value, 'req', [(i, i ^ 1) for i in range(devices)])  31.4 us
    ppermute x14, starting transfers between devices, pair_shift(): lax.ppermute(value, 'req', [(i, 2 * (i // 2 ^ k) + i % 2) for i in range(...  16.2 us
    ppermute x14, starting transfers between devices, core_swap(): return lax.ppermute(value, 'tp', [(0, 1), (1, 0)])  13.1 us
    ppermute x14, waiting for transfers between devices, pair_shift(): lax.ppermute(value, 'req', [(i, 2 * (i // 2 ^ k) + i % 2) for i in range(...  12.8 us
    pallas_call x2, Pallas kernels, down(): pl.pallas_call(down_kernel, grid_spec=pltpu.PrefetchScalarGridSpec(num_sc...  10.8 us
    pallas_call x1, Pallas kernels, down_both(): pl.pallas_call(lambda *refs: down_both_kernel(len(activ), *refs), grid_sp...  9.53 us
    ppermute x10, starting transfers between devices, side_swap(): return lax.ppermute(value, 'req', [(i, i ^ 1) for i in range(devices)])  6.57 us
  transfers between devices with their start and end apart: 38, of which 17 were waited for; matrix products, arithmetic and copies ran while one was open for 1% of the time, Pallas kernels for 38%

profile of v4, /device:TPU:15, one launch (start us, length us, event | category | flops | bytes accessed | tf_op | source)
XLA Modules:
  0.0 156.2 jit_solution(8967256731117371794)
XLA Ops:
  0.7 0.9 copy-done
  1.6 4.7 %fusion.18 = f32[128,4096]{1,0:T(8,128)S(1)} fusion(bf16[128,1024]{1,0:T(8,128)(2,1)S(1)} %copy-done, bf16[1024,4096]{1,0:T(8,128)(2,1)} %param.13), kind=kOutput, calls=%fused_computation.50 | convolution fusion | flops 1073741824 | bytes 10747904 | tf_op jit(solution)/shard_map/dot_general | solution.py:440
  6.4 0.7 collective-permute-start
  7.1 0.6 slice.51
  8.8 1.6 multiply_reduce_fusion.1
  10.4 0.4 collective-permute-start.1
  10.8 0.6 fusion.1
  11.8 0.8 collective-permute-done.2
  12.9 0.6 slot_rows.2
  13.4 0.3 collective-permute-start.5
  13.7 2.3 %collective-permute-start.3 = (bf16[48,2048]{1,0:T(8,128)(2,1)S(1)}, bf16[48,2048]{1,0:T(8,128)(2,1)S(1)}, u32[]{:S(2)}, u32[]{:S(2)}) collective-permute-start(bf16[48,2048]{1,0:T(8,128)(2,1)S(1)} %get-tuple-element.24), channel_id=1, source_target_pairs={{0,16},{2,18},{4,20},{6,22},{8,24},{10,26},{12,28},{14,30},{16,0},... | collective-permute-start | bytes 589832 | tf_op jit(solution)/shard_map/ppermute | solution.py:16
  16.0 1.0 collective-permute-start.4
  17.1 2.8 %collective-permute-done.5.refs_1_.refs_2_ = bf16[48,2048]{1,0:T(8,128)(2,1)S(1)} collective-permute-done((bf16[48,2048]{1,0:T(8,128)(2,1)S(1)}, bf16[48,2048]{1,0:T(8,128)(2,1)S(1)}, u32[]{:S(2)}, u32[]{:S(2)}) %collective-permute-start.5) | collective-permute-done | bytes 196640 | tf_op jit(solution)/shard_map/ppermute | solution.py:16
  19.9 0.3 collective-permute-start.6
  20.4 1.2 collective-permute-start.13
  21.7 7.9 %collective-permute-done.6.refs_0_ = bf16[96,2048]{1,0:T(8,128)(2,1)S(1)} collective-permute-done((bf16[96,2048]{1,0:T(8,128)(2,1)S(1)}, bf16[96,2048]{1,0:T(8,128)(2,1)S(1)}, u32[]{:S(2)}, u32[]{:S(2)}) %collective-permute-start.6) | collective-permute-done | bytes 393248 | tf_op jit(solution)/shard_map/ppermute | solution.py:20
  29.6 1.9 %collective-permute-start.8 = (bf16[96,2048]{1,0:T(8,128)(2,1)S(1)}, bf16[96,2048]{1,0:T(8,128)(2,1)S(1)}, u32[]{:S(2)}, u32[]{:S(2)}) collective-permute-start(bf16[96,2048]{1,0:T(8,128)(2,1)S(1)} %join.10.refs_3_), channel_id=1, source_target_pairs={{0,1},{1,0},{2,3},{3,2},{4,5},{5,4},{6,7},{7,6},{8,9},{9,8},{10,11... | collective-permute-start | bytes 1179656 | tf_op jit(solution)/shard_map/ppermute | solution.py:24
  31.5 1.7 %collective-permute-done.4.refs_1_ = bf16[48,2048]{1,0:T(8,128)(2,1)S(1)} collective-permute-done((bf16[48,2048]{1,0:T(8,128)(2,1)S(1)}, bf16[48,2048]{1,0:T(8,128)(2,1)S(1)}, u32[]{:S(2)}, u32[]{:S(2)}) %collective-permute-start.4) | collective-permute-done | bytes 196640 | tf_op jit(solution)/shard_map/ppermute | solution.py:16
  33.3 0.3 collective-permute-start.9
  33.6 0.8 collective-permute-start.7
  34.4 9.1 %collective-permute-done.9.refs_0_ = bf16[96,2048]{1,0:T(8,128)(2,1)S(1)} collective-permute-done((bf16[96,2048]{1,0:T(8,128)(2,1)S(1)}, bf16[96,2048]{1,0:T(8,128)(2,1)S(1)}, u32[]{:S(2)}, u32[]{:S(2)}) %collective-permute-start.9) | collective-permute-done | bytes 393248 | tf_op jit(solution)/shard_map/ppermute | solution.py:20
  43.5 1.3 collective-permute-start.11
  45.0 0.3 slot_rows.3
  45.4 2.4 %collective-permute-start.15 = (bf16[48,2048]{1,0:T(8,128)(2,1)S(1)}, bf16[48,2048]{1,0:T(8,128)(2,1)S(1)}, u32[]{:S(2)}, u32[]{:S(2)}) collective-permute-start(bf16[48,2048]{1,0:T(8,128)(2,1)S(1)} %get-tuple-element.31), channel_id=1, source_target_pairs={{0,28},{2,30},{4,24},{6,26},{8,20},{10,22},{12,16},{14,18},{16,12}... | collective-permute-start | bytes 589832 | tf_op jit(solution)/shard_map/ppermute | solution.py:16
  47.9 0.3 collective-permute-start.17
  48.2 16.6 %gate_up.3.refs_2_.refs_1_.activ_ref = bf16[384,1792]{1,0:T(8,128)(2,1)S(1)} custom-call(s32[1]{0:T(128)} %bitcast.7.refs_0_.core_ref, bf16[96,2048]{1,0:T(8,128)(2,1)S(1)} %join.13.refs_1_, bf16[96,2048]{1,0:T(8,128)(2,1)S(1)} %collective-permute-done.7.refs_2_, bf16[96,2048]{1,0:T(8,128)(2,1)S(1)} %join.10.refs_3_, ...), custom_call_target="tpu_custom_call" | custom-call | flops 1572864 | bytes 4096 | tf_op jit(solution)/shard_map/gate_up/pallas_call | solution.py:168
  65.0 1.1 collective-permute-start.16
  66.1 1.6 %collective-permute-start.21 = (bf16[96,2048]{1,0:T(8,128)(2,1)S(1)}, bf16[96,2048]{1,0:T(8,128)(2,1)S(1)}, u32[]{:S(2)}, u32[]{:S(2)}) collective-permute-start(bf16[96,2048]{1,0:T(8,128)(2,1)S(1)} %join.16.refs_10_.refs_3_), channel_id=1, source_target_pairs={{0,1},{1,0},{2,3},{3,2},{4,5},{5,4},{6,7},{7,6},{8,9},{9,8},{10,11... | collective-permute-start | bytes 1179656 | tf_op jit(solution)/shard_map/ppermute | solution.py:24
  67.8 0.5 collective-permute-start.23
  68.3 5.3 %down_away.1.refs_1_ = bf16[384,2048]{1,0:T(8,128)(2,1)S(1)} custom-call(s32[1]{0:T(128)} %bitcast.7.refs_0_.core_ref, bf16[384,1792]{1,0:T(8,128)(2,1)S(1)} %gate_up.3.refs_2_.refs_1_.activ_ref, bf16[1,1792,4096]{2,1,0:T(8,128)(2,1)} %refs_3_.1, bf16[96,2048]{1,0:T(8,128)(2,1)S(1)} %join.17.refs_0_.refs_1_, bf16[96,2048]{1,0:T(8,128)(2,1)S(1)} %join.18.refs_1_.refs_7_), custom_call_target="tpu_custom_call" | custom-call | flops 688128 | bytes 1792 | tf_op jit(solution)/shard_map/down_away/pallas_call | solution.py:200
  73.7 0.6 collective-permute-done.16.refs_0_
  74.3 5.4 %down_own.1.refs_0_ = f32[384,2048]{1,0:T(8,128)S(1)} custom-call(s32[1]{0:T(128)} %bitcast.7.refs_0_.core_ref, bf16[384,1792]{1,0:T(8,128)(2,1)S(1)} %gate_up.3.refs_2_.refs_1_.activ_ref, bf16[1,1792,4096]{2,1,0:T(8,128)(2,1)} %refs_3_.1, bf16[96,2048]{1,0:T(8,128)(2,1)S(1)} %join.19.refs_0_.refs_5_), custom_call_target="tpu_custom_call" | custom-call | flops 20000000000 | bytes 1792 | tf_op jit(solution)/shard_map/down_own/pallas_call | solution.py:200
  79.8 2.3 %collective-permute-start.22 = (bf16[96,2048]{1,0:T(8,128)(2,1)S(1)}, bf16[96,2048]{1,0:T(8,128)(2,1)S(1)}, u32[]{:S(2)}, u32[]{:S(2)}) collective-permute-start(bf16[96,2048]{1,0:T(8,128)(2,1)S(1)} %join.19.refs_0_.refs_5_), channel_id=1, source_target_pairs={{0,1},{1,0},{2,3},{3,2},{4,5},{5,4},{6,7},{7,6},{8,9},{9,8},{10,11... | collective-permute-start | bytes 1179656 | tf_op jit(solution)/shard_map/ppermute | solution.py:24
  82.1 0.3 add_cores.2
  82.4 1.1 collective-permute-start.19
  83.5 0.4 collective-permute-start.26
  84.1 10.3 %gate_up.4.refs_2_.refs_1_ = bf16[384,1024]{1,0:T(8,128)(2,1)S(1)} custom-call(s32[1]{0:T(128)} %bitcast.7.refs_0_.core_ref, bf16[96,2048]{1,0:T(8,128)(2,1)S(1)} %join.17.refs_0_.refs_1_, bf16[96,2048]{1,0:T(8,128)(2,1)S(1)} %collective-permute-done.20.refs_2_, bf16[96,2048]{1,0:T(8,128)(2,1)S(1)} %join.16.refs_10_.refs_3_, ...), custom_call_target="tpu_custom_call" | custom-call | flops 1572864 | bytes 4096 | tf_op jit(solution)/shard_map/gate_up/pallas_call | solution.py:168
  94.5 4.8 %collective-permute-start.24 = (bf16[48,2048]{1,0:T(8,128)(2,1)S(1)}, bf16[48,2048]{1,0:T(8,128)(2,1)S(1)}, u32[]{:S(2)}, u32[]{:S(2)}) collective-permute-start(bf16[48,2048]{1,0:T(8,128)(2,1)S(1)} %get-tuple-element.34.refs_10_), channel_id=1, source_target_pairs={{0,16},{2,18},{4,20},{6,22},{8,24},{10,26},{12,28},{14,30},{16,0},... | collective-permute-start | bytes 589832 | tf_op jit(solution)/shard_map/ppermute | solution.py:16
  99.3 1.0 collective-permute-start.25
  100.5 8.4 %gate_up.5.refs_2_ = bf16[384,768]{1,0:T(8,128)(2,1)S(1)} custom-call(s32[1]{0:T(128)} %bitcast.7.refs_0_.core_ref, bf16[96,2048]{1,0:T(8,128)(2,1)S(1)} %join.17.refs_0_.refs_1_, bf16[96,2048]{1,0:T(8,128)(2,1)S(1)} %collective-permute-done.20.refs_2_, bf16[96,2048]{1,0:T(8,128)(2,1)S(1)} %join.16.refs_10_.refs_3_, ...), custom_call_target="tpu_custom_call" | custom-call | flops 1572864 | bytes 4096 | tf_op jit(solution)/shard_map/gate_up/pallas_call | solution.py:168
  108.9 0.3 collective-permute-start.27
  109.2 9.5 %down_both.1 = (bf16[384,2048]{1,0:T(8,128)(2,1)S(1)}, f32[384,2048]{1,0:T(8,128)S(1)}) custom-call(s32[1]{0:T(128)} %bitcast.7.refs_0_.core_ref, bf16[384,1024]{1,0:T(8,128)(2,1)S(1)} %gate_up.4.refs_2_.refs_1_, bf16[384,768]{1,0:T(8,128)(2,1)S(1)} %gate_up.5.refs_2_, bf16[1,1792,4096]{2,1,0:T(8,128)(2,1)} %refs_3_.1, ...), custom_call_target="tpu_custom_call" | custom-call | flops 688128 | bytes 1792 | tf_op jit(solution)/shard_map/down_both/pallas_call | solution.py:253
  118.8 1.2 collective-permute-start.28
  120.0 0.7 mix.4.refs_2_
  120.7 0.7 mix.5.refs_2_
  121.3 1.7 %collective-permute-done.28.refs_1_ = bf16[384,2048]{1,0:T(8,128)(2,1)S(1)} collective-permute-done((bf16[384,2048]{1,0:T(8,128)(2,1)S(1)}, bf16[384,2048]{1,0:T(8,128)(2,1)S(1)}, u32[]{:S(2)}, u32[]{:S(2)}) %collective-permute-start.28) | collective-permute-done | bytes 1572896 | tf_op jit(solution)/shard_map/ppermute | solution.py:24
  123.3 1.2 collective-permute-start.31
  124.4 0.4 collective-permute-start.29
  124.8 1.1 collective-permute-start.35
  125.9 0.4 collective-permute-start.33
  126.3 3.2 %collective-permute-done.31.refs_1_ = bf16[48,2048]{1,0:T(8,128)(2,1)S(1)} collective-permute-done((bf16[48,2048]{1,0:T(8,128)(2,1)S(1)}, bf16[48,2048]{1,0:T(8,128)(2,1)S(1)}, u32[]{:S(2)}, u32[]{:S(2)}) %collective-permute-start.31) | collective-permute-done | bytes 196640 | tf_op jit(solution)/shard_map/ppermute | solution.py:20
  129.7 4.0 %collective-permute-done.29.refs_1_ = bf16[48,2048]{1,0:T(8,128)(2,1)S(1)} collective-permute-done((bf16[48,2048]{1,0:T(8,128)(2,1)S(1)}, bf16[48,2048]{1,0:T(8,128)(2,1)S(1)}, u32[]{:S(2)}, u32[]{:S(2)}) %collective-permute-start.29) | collective-permute-done | bytes 196640 | tf_op jit(solution)/shard_map/ppermute | solution.py:20
  133.8 4.1 %collective-permute-done.35.refs_1_ = bf16[48,2048]{1,0:T(8,128)(2,1)S(1)} collective-permute-done((bf16[48,2048]{1,0:T(8,128)(2,1)S(1)}, bf16[48,2048]{1,0:T(8,128)(2,1)S(1)}, u32[]{:S(2)}, u32[]{:S(2)}) %collective-permute-start.35) | collective-permute-done | bytes 196640 | tf_op jit(solution)/shard_map/ppermute | solution.py:20
  137.9 1.6 %collective-permute-start.36 = (bf16[48,2048]{1,0:T(8,128)(2,1)S(1)}, bf16[48,2048]{1,0:T(8,128)(2,1)S(1)}, u32[]{:S(2)}, u32[]{:S(2)}) collective-permute-start(bf16[48,2048]{1,0:T(8,128)(2,1)S(1)} %add_sides.11), channel_id=1, source_target_pairs={{0,12},{2,14},{4,8},{6,10},{8,4},{10,6},{12,0},{14,2},{16,28},{18,... | collective-permute-start | bytes 589832 | tf_op jit(solution)/shard_map/ppermute | solution.py:16
  139.5 2.6 %collective-permute-done.33.refs_1_ = bf16[48,2048]{1,0:T(8,128)(2,1)S(1)} collective-permute-done((bf16[48,2048]{1,0:T(8,128)(2,1)S(1)}, bf16[48,2048]{1,0:T(8,128)(2,1)S(1)}, u32[]{:S(2)}, u32[]{:S(2)}) %collective-permute-start.33) | collective-permute-done | bytes 196640 | tf_op jit(solution)/shard_map/ppermute | solution.py:20
  142.1 0.6 collective-permute-start.34
  142.8 1.8 %collective-permute-done.32.refs_4_ = bf16[48,2048]{1,0:T(8,128)(2,1)S(1)} collective-permute-done((bf16[48,2048]{1,0:T(8,128)(2,1)S(1)}, bf16[48,2048]{1,0:T(8,128)(2,1)S(1)}, u32[]{:S(2)}, u32[]{:S(2)}) %collective-permute-start.32) | collective-permute-done | bytes 196640 | tf_op jit(solution)/shard_map/ppermute | solution.py:16
  144.6 4.1 %collective-permute-done.30.refs_3_ = bf16[48,2048]{1,0:T(8,128)(2,1)S(1)} collective-permute-done((bf16[48,2048]{1,0:T(8,128)(2,1)S(1)}, bf16[48,2048]{1,0:T(8,128)(2,1)S(1)}, u32[]{:S(2)}, u32[]{:S(2)}) %collective-permute-start.30) | collective-permute-done | bytes 196640 | tf_op jit(solution)/shard_map/ppermute | solution.py:16
  148.7 0.7 mix.6.refs_2_
  149.4 2.2 %collective-permute-done.34.refs_3_ = bf16[48,2048]{1,0:T(8,128)(2,1)S(1)} collective-permute-done((bf16[48,2048]{1,0:T(8,128)(2,1)S(1)}, bf16[48,2048]{1,0:T(8,128)(2,1)S(1)}, u32[]{:S(2)}, u32[]{:S(2)}) %collective-permute-start.34) | collective-permute-done | bytes 196640 | tf_op jit(solution)/shard_map/ppermute | solution.py:16
  151.6 0.7 mix.7
  152.4 1.8 %collective-permute-start.37 = (f32[128,1]{0,1:T(1,128)S(1)}, f32[128,1]{0,1:T(1,128)S(1)}, u32[]{:S(2)}, u32[]{:S(2)}) collective-permute-start(f32[128,1]{0,1:T(1,128)S(1)} %bitcast.25), channel_id=1, source_target_pairs={{0,1},{1,0},{2,3},{3,2},{4,5},{5,4},{6,7},{7,6},{8,9},{9,8},{10,11... | collective-permute-start | bytes 1544 | tf_op jit(solution)/shard_map/ppermute | solution.py:24
  154.2 0.8 collective-permute-done.37
  155.1 1.1 multiply_convert_fusion
  (83 shorter events, 3.4 us)
Async XLA Ops:
  0.6 1.0 copy-start
  1.6 5.5 %copy-start.6 = (s32[1,5]{1,0:T(1,128)S(1)}, s32[1,5]{1,0:T(1,128)}, u32[]{:S(2)}) copy-start(s32[1,5]{1,0:T(1,128)} %param.17) | copy-start | bytes 64
  1.6 6.8 %copy-start.7 = (s32[8]{0:T(128)S(1)}, s32[8]{0:T(128)}, u32[]{:S(2)}) copy-start(s32[8]{0:T(128)} %param.18) | copy-start | bytes 100
  6.4 2.4 %collective-permute-start = (bf16[128,2048]{1,0:T(8,128)(2,1)S(1)}, bf16[128,2048]{1,0:T(8,128)(2,1)}, u32[]{:S(2)}, u32[]{:S(2)}) collective-permute-start(bf16[128,2048]{1,0:T(8,128)(2,1)S(1)} %select_convert_fusion), channel_id=1, source_target_pairs={{0,1},{1,0},{2,3},{3,2},{4,5},{5,4},{6,7},{7,6},{8,9},{9,8},{10,11... | collective-permute-start | bytes 1572872 | tf_op jit(solution)/shard_map/ppermute | solution.py:24
  8.5 2.3 %copy-start.2 = (f32[2048]{0:T(1024)S(1)}, f32[2048]{0:T(1024)}, u32[]{:S(2)}) copy-start(f32[2048]{0:T(1024)} %param.14) | copy-start | bytes 24580
  8.5 2.3 %copy-start.3 = (bf16[2048,4]{0,1:T(4,128)(2,1)S(1)}, bf16[2048,4]{0,1:T(4,128)(2,1)}, u32[]{:S(2)}) copy-start(bf16[2048,4]{0,1:T(4,128)(2,1)} %param.15) | copy-start | bytes 49156
  10.3 2.3 %copy-start.5 = (s32[128,2]{0,1:T(2,128)S(1)}, s32[128,2]{0,1:T(2,128)}, u32[]{:S(2)}) copy-start(s32[128,2]{0,1:T(2,128)} %param.16) | copy-start | bytes 3076
  10.4 1.3 collective-permute-start.1
  11.4 1.2 collective-permute-start.2
  13.4 6.4 %collective-permute-start.5 = (bf16[48,2048]{1,0:T(8,128)(2,1)S(1)}, bf16[48,2048]{1,0:T(8,128)(2,1)S(1)}, u32[]{:S(2)}, u32[]{:S(2)}) collective-permute-start(bf16[48,2048]{1,0:T(8,128)(2,1)S(1)} %get-tuple-element.27), channel_id=1, source_target_pairs={{0,4},{2,6},{4,0},{6,2},{8,12},{10,14},{12,8},{14,10},{16,20},{18,... | collective-permute-start | bytes 589832 | tf_op jit(solution)/shard_map/ppermute | solution.py:16
  13.7 17.8 %collective-permute-start.3 = (bf16[48,2048]{1,0:T(8,128)(2,1)S(1)}, bf16[48,2048]{1,0:T(8,128)(2,1)S(1)}, u32[]{:S(2)}, u32[]{:S(2)}) collective-permute-start(bf16[48,2048]{1,0:T(8,128)(2,1)S(1)} %get-tuple-element.24), channel_id=1, source_target_pairs={{0,16},{2,18},{4,20},{6,22},{8,24},{10,26},{12,28},{14,30},{16,0},... | collective-permute-start | bytes 589832 | tf_op jit(solution)/shard_map/ppermute | solution.py:16
  16.0 17.2 %collective-permute-start.4 = (bf16[48,2048]{1,0:T(8,128)(2,1)S(1)}, bf16[48,2048]{1,0:T(8,128)(2,1)S(1)}, u32[]{:S(2)}, u32[]{:S(2)}) collective-permute-start(bf16[48,2048]{1,0:T(8,128)(2,1)S(1)} %get-tuple-element.25), channel_id=1, source_target_pairs={{0,20},{2,22},{4,16},{6,18},{8,28},{10,30},{12,24},{14,26},{16,4},... | collective-permute-start | bytes 589832 | tf_op jit(solution)/shard_map/ppermute | solution.py:16
  19.9 9.7 %collective-permute-start.6 = (bf16[96,2048]{1,0:T(8,128)(2,1)S(1)}, bf16[96,2048]{1,0:T(8,128)(2,1)S(1)}, u32[]{:S(2)}, u32[]{:S(2)}) collective-permute-start(bf16[96,2048]{1,0:T(8,128)(2,1)S(1)} %join.10.refs_3_), channel_id=1, source_target_pairs={{0,2},{2,0},{4,6},{6,4},{8,10},{10,8},{12,14},{14,12},{16,18},{18,... | collective-permute-start | bytes 1179656 | tf_op jit(solution)/shard_map/ppermute | solution.py:20
  20.2 24.7 %collective-permute-start.12 = (bf16[48,2048]{1,0:T(8,128)(2,1)S(1)}, bf16[48,2048]{1,0:T(8,128)(2,1)S(1)}, u32[]{:S(2)}, u32[]{:S(2)}) collective-permute-start(bf16[48,2048]{1,0:T(8,128)(2,1)S(1)} %get-tuple-element.28), channel_id=1, source_target_pairs={{0,8},{2,10},{4,12},{6,14},{8,0},{10,2},{12,4},{14,6},{16,24},{18,... | collective-permute-start | bytes 589832 | tf_op jit(solution)/shard_map/ppermute | solution.py:16
  20.4 24.8 %collective-permute-start.13 = (bf16[48,2048]{1,0:T(8,128)(2,1)S(1)}, bf16[48,2048]{1,0:T(8,128)(2,1)S(1)}, u32[]{:S(2)}, u32[]{:S(2)}) collective-permute-start(bf16[48,2048]{1,0:T(8,128)(2,1)S(1)} %get-tuple-element.29), channel_id=1, source_target_pairs={{0,12},{2,14},{4,8},{6,10},{8,4},{10,6},{12,0},{14,2},{16,28},{18,... | collective-permute-start | bytes 589832 | tf_op jit(solution)/shard_map/ppermute | solution.py:16
  29.6 15.8 %collective-permute-start.8 = (bf16[96,2048]{1,0:T(8,128)(2,1)S(1)}, bf16[96,2048]{1,0:T(8,128)(2,1)S(1)}, u32[]{:S(2)}, u32[]{:S(2)}) collective-permute-start(bf16[96,2048]{1,0:T(8,128)(2,1)S(1)} %join.10.refs_3_), channel_id=1, source_target_pairs={{0,1},{1,0},{2,3},{3,2},{4,5},{5,4},{6,7},{7,6},{8,9},{9,8},{10,11... | collective-permute-start | bytes 1179656 | tf_op jit(solution)/shard_map/ppermute | solution.py:24
  33.3 10.3 %collective-permute-start.9 = (bf16[96,2048]{1,0:T(8,128)(2,1)S(1)}, bf16[96,2048]{1,0:T(8,128)(2,1)S(1)}, u32[]{:S(2)}, u32[]{:S(2)}) collective-permute-start(bf16[96,2048]{1,0:T(8,128)(2,1)S(1)} %join.13.refs_1_), channel_id=1, source_target_pairs={{0,2},{2,0},{4,6},{6,4},{8,10},{10,8},{12,14},{14,12},{16,18},{18,... | collective-permute-start | bytes 1179656 | tf_op jit(solution)/shard_map/ppermute | solution.py:20
  33.6 14.2 %collective-permute-start.7 = (bf16[96,2048]{1,0:T(8,128)(2,1)S(1)}, bf16[96,2048]{1,0:T(8,128)(2,1)S(1)}, u32[]{:S(2)}, u32[]{:S(2)}) collective-permute-start(bf16[96,2048]{1,0:T(8,128)(2,1)S(1)} %join.13.refs_1_), channel_id=1, source_target_pairs={{0,1},{1,0},{2,3},{3,2},{4,5},{5,4},{6,7},{7,6},{8,9},{9,8},{10,11... | collective-permute-start | bytes 1179656 | tf_op jit(solution)/shard_map/ppermute | solution.py:24
  43.5 4.6 %collective-permute-start.11 = (bf16[96,2048]{1,0:T(8,128)(2,1)S(1)}, bf16[96,2048]{1,0:T(8,128)(2,1)S(1)}, u32[]{:S(2)}, u32[]{:S(2)}) collective-permute-start(bf16[96,2048]{1,0:T(8,128)(2,1)S(1)} %join.12.refs_2_.refs_7_), channel_id=1, source_target_pairs={{0,1},{1,0},{2,3},{3,2},{4,5},{5,4},{6,7},{7,6},{8,9},{9,8},{10,11... | collective-permute-start | bytes 1179656 | tf_op jit(solution)/shard_map/ppermute | solution.py:24
  44.9 3.3 %collective-permute-start.10 = (bf16[96,2048]{1,0:T(8,128)(2,1)S(1)}, bf16[96,2048]{1,0:T(8,128)(2,1)S(1)}, u32[]{:S(2)}, u32[]{:S(2)}) collective-permute-start(bf16[96,2048]{1,0:T(8,128)(2,1)S(1)} %join.15.refs_5_), channel_id=1, source_target_pairs={{0,1},{1,0},{2,3},{3,2},{4,5},{5,4},{6,7},{7,6},{8,9},{9,8},{10,11... | collective-permute-start | bytes 1179656 | tf_op jit(solution)/shard_map/ppermute | solution.py:24
  45.3 19.5 %collective-permute-start.14 = (bf16[48,2048]{1,0:T(8,128)(2,1)S(1)}, bf16[48,2048]{1,0:T(8,128)(2,1)S(1)}, u32[]{:S(2)}, u32[]{:S(2)}) collective-permute-start(bf16[48,2048]{1,0:T(8,128)(2,1)S(1)} %get-tuple-element.30), channel_id=1, source_target_pairs={{0,24},{2,26},{4,28},{6,30},{8,16},{10,18},{12,20},{14,22},{16,8},... | collective-permute-start | bytes 589832 | tf_op jit(solution)/shard_map/ppermute | solution.py:16
  45.4 19.6 %collective-permute-start.15 = (bf16[48,2048]{1,0:T(8,128)(2,1)S(1)}, bf16[48,2048]{1,0:T(8,128)(2,1)S(1)}, u32[]{:S(2)}, u32[]{:S(2)}) collective-permute-start(bf16[48,2048]{1,0:T(8,128)(2,1)S(1)} %get-tuple-element.31), channel_id=1, source_target_pairs={{0,28},{2,30},{4,24},{6,26},{8,20},{10,22},{12,16},{14,18},{16,12}... | collective-permute-start | bytes 589832 | tf_op jit(solution)/shard_map/ppermute | solution.py:16
  47.9 19.9 %collective-permute-start.17 = (bf16[96,2048]{1,0:T(8,128)(2,1)S(1)}, bf16[96,2048]{1,0:T(8,128)(2,1)S(1)}, u32[]{:S(2)}, u32[]{:S(2)}) collective-permute-start(bf16[96,2048]{1,0:T(8,128)(2,1)S(1)} %join.16.refs_10_.refs_3_), channel_id=1, source_target_pairs={{0,2},{2,0},{4,6},{6,4},{8,10},{10,8},{12,14},{14,12},{16,18},{18,... | collective-permute-start | bytes 1179656 | tf_op jit(solution)/shard_map/ppermute | solution.py:20
  65.0 9.3 %collective-permute-start.16 = (bf16[96,2048]{1,0:T(8,128)(2,1)S(1)}, bf16[96,2048]{1,0:T(8,128)(2,1)S(1)}, u32[]{:S(2)}, u32[]{:S(2)}) collective-permute-start(bf16[96,2048]{1,0:T(8,128)(2,1)S(1)} %join.17.refs_0_.refs_1_), channel_id=1, source_target_pairs={{0,2},{2,0},{4,6},{6,4},{8,10},{10,8},{12,14},{14,12},{16,18},{18,... | collective-permute-start | bytes 1179656 | tf_op jit(solution)/shard_map/ppermute | solution.py:20
  66.1 17.4 %collective-permute-start.21 = (bf16[96,2048]{1,0:T(8,128)(2,1)S(1)}, bf16[96,2048]{1,0:T(8,128)(2,1)S(1)}, u32[]{:S(2)}, u32[]{:S(2)}) collective-permute-start(bf16[96,2048]{1,0:T(8,128)(2,1)S(1)} %join.16.refs_10_.refs_3_), channel_id=1, source_target_pairs={{0,1},{1,0},{2,3},{3,2},{4,5},{5,4},{6,7},{7,6},{8,9},{9,8},{10,11... | collective-permute-start | bytes 1179656 | tf_op jit(solution)/shard_map/ppermute | solution.py:24
  67.7 16.4 %collective-permute-start.20 = (bf16[96,2048]{1,0:T(8,128)(2,1)S(1)}, bf16[96,2048]{1,0:T(8,128)(2,1)S(1)}, u32[]{:S(2)}, u32[]{:S(2)}) collective-permute-start(bf16[96,2048]{1,0:T(8,128)(2,1)S(1)} %join.17.refs_0_.refs_1_), channel_id=1, source_target_pairs={{0,1},{1,0},{2,3},{3,2},{4,5},{5,4},{6,7},{7,6},{8,9},{9,8},{10,11... | collective-permute-start | bytes 1179656 | tf_op jit(solution)/shard_map/ppermute | solution.py:24
  67.8 16.3 %collective-permute-start.23 = (bf16[96,2048]{1,0:T(8,128)(2,1)S(1)}, bf16[96,2048]{1,0:T(8,128)(2,1)S(1)}, u32[]{:S(2)}, u32[]{:S(2)}) collective-permute-start(bf16[96,2048]{1,0:T(8,128)(2,1)S(1)} %join.18.refs_1_.refs_7_), channel_id=1, source_target_pairs={{0,1},{1,0},{2,3},{3,2},{4,5},{5,4},{6,7},{7,6},{8,9},{9,8},{10,11... | collective-permute-start | bytes 1179656 | tf_op jit(solution)/shard_map/ppermute | solution.py:24
  73.6 8.5 %collective-permute-start.18 = (bf16[384,2048]{1,0:T(8,128)(2,1)S(1)}, bf16[384,2048]{1,0:T(8,128)(2,1)S(1)}, u32[]{:S(2)}, u32[]{:S(2)}) collective-permute-start(bf16[384,2048]{1,0:T(8,128)(2,1)S(1)} %down_away.1.refs_1_), channel_id=1, source_target_pairs={{0,1},{1,0},{2,3},{3,2},{4,5},{5,4},{6,7},{7,6},{8,9},{9,8},{10,11... | collective-permute-start | bytes 4718600 | tf_op jit(solution)/shard_map/ppermute | solution.py:24
  79.8 4.3 %collective-permute-start.22 = (bf16[96,2048]{1,0:T(8,128)(2,1)S(1)}, bf16[96,2048]{1,0:T(8,128)(2,1)S(1)}, u32[]{:S(2)}, u32[]{:S(2)}) collective-permute-start(bf16[96,2048]{1,0:T(8,128)(2,1)S(1)} %join.19.refs_0_.refs_5_), channel_id=1, source_target_pairs={{0,1},{1,0},{2,3},{3,2},{4,5},{5,4},{6,7},{7,6},{8,9},{9,8},{10,11... | collective-permute-start | bytes 1179656 | tf_op jit(solution)/shard_map/ppermute | solution.py:24
  82.4 12.0 %collective-permute-start.19 = (bf16[96,2048]{1,0:T(8,128)(2,1)S(1)}, bf16[96,2048]{1,0:T(8,128)(2,1)S(1)}, u32[]{:S(2)}, u32[]{:S(2)}) collective-permute-start(bf16[96,2048]{1,0:T(8,128)(2,1)S(1)} %get-tuple-element.33), channel_id=1, source_target_pairs={{0,2},{2,0},{4,6},{6,4},{8,10},{10,8},{12,14},{14,12},{16,18},{18,... | collective-permute-start | bytes 1179656 | tf_op jit(solution)/shard_map/ppermute | solution.py:20
  83.5 25.4 %collective-permute-start.26 = (bf16[96,2048]{1,0:T(8,128)(2,1)S(1)}, bf16[96,2048]{1,0:T(8,128)(2,1)S(1)}, u32[]{:S(2)}, u32[]{:S(2)}) collective-permute-start(bf16[96,2048]{1,0:T(8,128)(2,1)S(1)} %get-tuple-element.36), channel_id=1, source_target_pairs={{0,2},{2,0},{4,6},{6,4},{8,10},{10,8},{12,14},{14,12},{16,18},{18,... | collective-permute-start | bytes 1179656 | tf_op jit(solution)/shard_map/ppermute | solution.py:20
  94.5 25.5 %collective-permute-start.24 = (bf16[48,2048]{1,0:T(8,128)(2,1)S(1)}, bf16[48,2048]{1,0:T(8,128)(2,1)S(1)}, u32[]{:S(2)}, u32[]{:S(2)}) collective-permute-start(bf16[48,2048]{1,0:T(8,128)(2,1)S(1)} %get-tuple-element.34.refs_10_), channel_id=1, source_target_pairs={{0,16},{2,18},{4,20},{6,22},{8,24},{10,26},{12,28},{14,30},{16,0},... | collective-permute-start | bytes 589832 | tf_op jit(solution)/shard_map/ppermute | solution.py:16
  99.3 20.7 %collective-permute-start.25 = (bf16[48,2048]{1,0:T(8,128)(2,1)S(1)}, bf16[48,2048]{1,0:T(8,128)(2,1)S(1)}, u32[]{:S(2)}, u32[]{:S(2)}) collective-permute-start(bf16[48,2048]{1,0:T(8,128)(2,1)S(1)} %get-tuple-element.35.refs_11_), channel_id=1, source_target_pairs={{0,20},{2,22},{4,16},{6,18},{8,28},{10,30},{12,24},{14,26},{16,4},... | collective-permute-start | bytes 589832 | tf_op jit(solution)/shard_map/ppermute | solution.py:16
  108.9 11.7 %collective-permute-start.27 = (bf16[48,2048]{1,0:T(8,128)(2,1)S(1)}, bf16[48,2048]{1,0:T(8,128)(2,1)S(1)}, u32[]{:S(2)}, u32[]{:S(2)}) collective-permute-start(bf16[48,2048]{1,0:T(8,128)(2,1)S(1)} %get-tuple-element.38.refs_5_), channel_id=1, source_target_pairs={{0,4},{2,6},{4,0},{6,2},{8,12},{10,14},{12,8},{14,10},{16,20},{18,... | collective-permute-start | bytes 589832 | tf_op jit(solution)/shard_map/ppermute | solution.py:16
  118.8 4.2 %collective-permute-start.28 = (bf16[384,2048]{1,0:T(8,128)(2,1)S(1)}, bf16[384,2048]{1,0:T(8,128)(2,1)S(1)}, u32[]{:S(2)}, u32[]{:S(2)}) collective-permute-start(bf16[384,2048]{1,0:T(8,128)(2,1)S(1)} %get-tuple-element.40), channel_id=1, source_target_pairs={{0,1},{1,0},{2,3},{3,2},{4,5},{5,4},{6,7},{7,6},{8,9},{9,8},{10,11... | collective-permute-start | bytes 4718600 | tf_op jit(solution)/shard_map/ppermute | solution.py:24
  123.3 6.2 %collective-permute-start.31 = (bf16[48,2048]{1,0:T(8,128)(2,1)S(1)}, bf16[48,2048]{1,0:T(8,128)(2,1)S(1)}, u32[]{:S(2)}, u32[]{:S(2)}) collective-permute-start(bf16[48,2048]{1,0:T(8,128)(2,1)S(1)} %get-tuple-element.43), channel_id=1, source_target_pairs={{0,2},{2,0},{4,6},{6,4},{8,10},{10,8},{12,14},{14,12},{16,18},{18,... | collective-permute-start | bytes 589832 | tf_op jit(solution)/shard_map/ppermute | solution.py:20
  124.4 9.2 %collective-permute-start.29 = (bf16[48,2048]{1,0:T(8,128)(2,1)S(1)}, bf16[48,2048]{1,0:T(8,128)(2,1)S(1)}, u32[]{:S(2)}, u32[]{:S(2)}) collective-permute-start(bf16[48,2048]{1,0:T(8,128)(2,1)S(1)} %get-tuple-element.42), channel_id=1, source_target_pairs={{0,2},{2,0},{4,6},{6,4},{8,10},{10,8},{12,14},{14,12},{16,18},{18,... | collective-permute-start | bytes 589832 | tf_op jit(solution)/shard_map/ppermute | solution.py:20
  124.8 13.1 %collective-permute-start.35 = (bf16[48,2048]{1,0:T(8,128)(2,1)S(1)}, bf16[48,2048]{1,0:T(8,128)(2,1)S(1)}, u32[]{:S(2)}, u32[]{:S(2)}) collective-permute-start(bf16[48,2048]{1,0:T(8,128)(2,1)S(1)} %get-tuple-element.45), channel_id=1, source_target_pairs={{0,2},{2,0},{4,6},{6,4},{8,10},{10,8},{12,14},{14,12},{16,18},{18,... | collective-permute-start | bytes 589832 | tf_op jit(solution)/shard_map/ppermute | solution.py:20
  125.9 16.2 %collective-permute-start.33 = (bf16[48,2048]{1,0:T(8,128)(2,1)S(1)}, bf16[48,2048]{1,0:T(8,128)(2,1)S(1)}, u32[]{:S(2)}, u32[]{:S(2)}) collective-permute-start(bf16[48,2048]{1,0:T(8,128)(2,1)S(1)} %get-tuple-element.44), channel_id=1, source_target_pairs={{0,2},{2,0},{4,6},{6,4},{8,10},{10,8},{12,14},{14,12},{16,18},{18,... | collective-permute-start | bytes 589832 | tf_op jit(solution)/shard_map/ppermute | solution.py:20
  129.5 15.1 %collective-permute-start.32 = (bf16[48,2048]{1,0:T(8,128)(2,1)S(1)}, bf16[48,2048]{1,0:T(8,128)(2,1)S(1)}, u32[]{:S(2)}, u32[]{:S(2)}) collective-permute-start(bf16[48,2048]{1,0:T(8,128)(2,1)S(1)} %add_sides.9), channel_id=1, source_target_pairs={{0,28},{2,30},{4,24},{6,26},{8,20},{10,22},{12,16},{14,18},{16,12}... | collective-permute-start | bytes 589832 | tf_op jit(solution)/shard_map/ppermute | solution.py:16
  133.7 15.0 %collective-permute-start.30 = (bf16[48,2048]{1,0:T(8,128)(2,1)S(1)}, bf16[48,2048]{1,0:T(8,128)(2,1)S(1)}, u32[]{:S(2)}, u32[]{:S(2)}) collective-permute-start(bf16[48,2048]{1,0:T(8,128)(2,1)S(1)} %add_sides.8), channel_id=1, source_target_pairs={{0,24},{2,26},{4,28},{6,30},{8,16},{10,18},{12,20},{14,22},{16,8},... | collective-permute-start | bytes 589832 | tf_op jit(solution)/shard_map/ppermute | solution.py:16
  137.9 11.5 %collective-permute-start.36 = (bf16[48,2048]{1,0:T(8,128)(2,1)S(1)}, bf16[48,2048]{1,0:T(8,128)(2,1)S(1)}, u32[]{:S(2)}, u32[]{:S(2)}) collective-permute-start(bf16[48,2048]{1,0:T(8,128)(2,1)S(1)} %add_sides.11), channel_id=1, source_target_pairs={{0,12},{2,14},{4,8},{6,10},{8,4},{10,6},{12,0},{14,2},{16,28},{18,... | collective-permute-start | bytes 589832 | tf_op jit(solution)/shard_map/ppermute | solution.py:16
  142.1 9.5 %collective-permute-start.34 = (bf16[48,2048]{1,0:T(8,128)(2,1)S(1)}, bf16[48,2048]{1,0:T(8,128)(2,1)S(1)}, u32[]{:S(2)}, u32[]{:S(2)}) collective-permute-start(bf16[48,2048]{1,0:T(8,128)(2,1)S(1)} %add_sides.10), channel_id=1, source_target_pairs={{0,8},{2,10},{4,12},{6,14},{8,0},{10,2},{12,4},{14,6},{16,24},{18,... | collective-permute-start | bytes 589832 | tf_op jit(solution)/shard_map/ppermute | solution.py:16
  149.4 5.7 %copy-start.4 = (f32[2048]{0:T(1024)S(1)}, f32[2048]{0:T(1024)}, u32[]{:S(2)}) copy-start(f32[2048]{0:T(1024)} %param.21) | copy-start | bytes 24580
  151.6 4.6 %copy-start.1 = (bf16[128,1024]{1,0:T(8,128)(2,1)S(1)}, bf16[128,1024]{1,0:T(8,128)(2,1)}, u32[]{:S(2)}) copy-start(bf16[128,1024]{1,0:T(8,128)(2,1)} %param.11) | copy-start | bytes 786436
  152.4 2.6 %collective-permute-start.37 = (f32[128,1]{0,1:T(1,128)S(1)}, f32[128,1]{0,1:T(1,128)S(1)}, u32[]{:S(2)}, u32[]{:S(2)}) collective-permute-start(f32[128,1]{0,1:T(1,128)S(1)} %bitcast.25), channel_id=1, source_target_pairs={{0,1},{1,0},{2,3},{3,2},{4,5},{5,4},{6,7},{7,6},{8,9},{9,8},{10,11... | collective-permute-start | bytes 1544 | tf_op jit(solution)/shard_map/ppermute | solution.py:24

commit v5 on v4

--- a/solution.py
+++ b/solution.py
@@ -114,6 +114,28 @@
         + [jax.ShapeDtypeStruct((count, width), jnp.bfloat16) for count in counts],
         compiler_params=pltpu.CompilerParams(vmem_limit_bytes=16 << 20),
         name="add_cores",
+    )(kept, other, *after)
+
+
+def add_sent_kernel(kept_ref, other_ref, *refs):
+    count = len(refs)
+    start = kept_ref.shape[0] - other_ref.shape[0]
+    step = other_ref.shape[0] // count
+    for j, out_ref in enumerate(refs):
+        part = kept_ref[start + j * step : start + (j + 1) * step]
+        part += other_ref[j * step : (j + 1) * step].astype(jnp.float32)
+        out_ref[...] = part.astype(jnp.bfloat16)
+
+
+def add_sent(kept, other, count, after):
+    rows, width = other.shape
+    return pl.pallas_call(
+        lambda *refs: add_sent_kernel(*refs[:2], *refs[-count:]),
+        in_specs=[WHOLE, WHOLE] + [ANYWHERE] * len(after),
+        out_specs=[WHOLE] * count,
+        out_shape=[jax.ShapeDtypeStruct((rows // count, width), jnp.bfloat16)] * count,
+        compiler_params=pltpu.CompilerParams(vmem_limit_bytes=16 << 20),
+        name="add_sent",
     )(kept, other, *after)
 
 
@@ -185,45 +207,10 @@
     )(core, *[part for piece in pieces for part in piece], weights, *after)
 
 
-def down_kernel(core_ref, activ_ref, weights_ref, *refs):
-    out_ref = refs[-1]
-    out_ref[...] = jnp.dot(
-        activ_ref[...], weights_ref[0], preferred_element_type=jnp.float32
-    ).astype(out_ref.dtype)
-
-
-def down(core, activ, weights, away, after, flops=0):
-    rows, units = activ.shape
-    width = weights.shape[2] // 2
-    block = 1024
-    steps = width // block
-    return pl.pallas_call(
-        down_kernel,
-        grid_spec=pltpu.PrefetchScalarGridSpec(
-            num_scalar_prefetch=1,
-            grid=(steps,),
-            in_specs=[
-                pl.BlockSpec((rows, units), lambda i, core: (0, 0)),
-                pl.BlockSpec(
-                    (1, units, block),
-                    lambda i, core: (0, 0, (1 - core[0] if away else core[0]) * steps + i),
-                ),
-            ]
-            + [ANYWHERE] * len(after),
-            out_specs=pl.BlockSpec((rows, block), lambda i, core: (0, i)),
-        ),
-        out_shape=jax.ShapeDtypeStruct((rows, width), jnp.bfloat16 if away else jnp.float32),
-        compiler_params=pltpu.CompilerParams(vmem_limit_bytes=44 << 20),
-        cost_estimate=pl.CostEstimate(
-            flops=flops or rows * units, bytes_accessed=units, transcendentals=0
-        ),
-        name="down_away" if away else "down_own",
-    )(core, activ, weights, *after)
-
-
 def down_both_kernel(count, core_ref, *refs):
     weights_ref = refs[count]
-    away_ref, own_ref = refs[-2:]
+    away_ref, send_ref, own_ref = refs[-3:]
+    keep = away_ref.shape[0]
     product, start = 0.0, 0
     for ref in refs[:count]:
         part = weights_ref[0, start : start + ref.shape[1]]
@@ -233,7 +220,8 @@
 
     @pl.when(pl.program_id(0) < half)
     def _():
-        away_ref[...] = product.astype(jnp.bfloat16)
+        away_ref[...] = product[:keep].astype(jnp.bfloat16)
+        send_ref[...] = product[keep:].astype(jnp.bfloat16)
 
     @pl.when(pl.program_id(0) >= half)
     def _():
@@ -261,12 +249,14 @@
             + [pl.BlockSpec((1, units, block), columns)]
             + [ANYWHERE] * len(after),
             out_specs=[
-                pl.BlockSpec((rows, block), lambda i, core: (0, jnp.minimum(i, half - 1))),
+                pl.BlockSpec((rows // 2, block), lambda i, core: (0, jnp.minimum(i, half - 1))),
+                pl.BlockSpec((rows // 2, block), lambda i, core: (0, jnp.minimum(i, half - 1))),
                 pl.BlockSpec((rows, block), lambda i, core: (0, jnp.maximum(i - half, 0))),
             ],
         ),
         out_shape=[
-            jax.ShapeDtypeStruct((rows, width), jnp.bfloat16),
+            jax.ShapeDtypeStruct((rows // 2, width), jnp.bfloat16),
+            jax.ShapeDtypeStruct((rows // 2, width), jnp.bfloat16),
             jax.ShapeDtypeStruct((rows, width), jnp.float32),
         ],
         compiler_params=pltpu.CompilerParams(vmem_limit_bytes=44 << 20),
@@ -335,11 +325,10 @@
     far_later_own = join([arrived[k] for k in far_later], [activ])
     far_later_nbr = side_swap(far_later_own, devices)
     near_later_nbr = join([near_later_nbr], [activ])
-    away = down(core, activ, w_down, True, [far_later_own, near_later_nbr])
-    far_later_nbr = join([far_later_nbr], [away])
-    away = core_swap(away)
-    kept = down(core, activ, w_down, False, [far_later_nbr], LONG)
-    own, far_other, near_other = add_cores(kept, away, [size, size], [])
+    away, sent, kept = down_both(core, [activ], w_down, [far_later_own, near_later_nbr])
+    far_later_nbr = join([far_later_nbr], [kept], LONG)
+    far_other, near_other = add_sent(kept, core_swap(sent), 2, [far_later_nbr])
+    (own,) = add_cores(kept[: 2 * size], core_swap(away), [], [far_other])
     pieces = [far_later_own, near_later_own, far_later_nbr, near_later_nbr]
     pieces = [(x, core_swap(x)) for x in pieces]
     unit_blocks = w_gate_up.shape[3] // UNITS
@@ -353,10 +342,11 @@
     activ.append(gate_up(core, pieces, w_gate_up, totals, (split, unit_blocks)))
     totals = add_sides(own, size, near_other, [capacity] * quarter, activ[1:])
     near_back = send(near, totals)
-    away, kept = down_both(core, activ, w_down, totals)
+    away, sent, kept = down_both(core, activ, w_down, totals)
     state = mix(columns(far[0]), state, far_back, [kept], LONG)
     state = mix(columns(near[0]), state, near_back, [])
-    own, *others = add_cores(kept, core_swap(away), [capacity] * 2 * quarter, [state])
+    others = add_sent(kept, core_swap(sent), 2 * quarter, [state])
+    (own,) = add_cores(kept[: 2 * size], core_swap(away), [], [others[0]])
     back = []
     for j, k in enumerate(far_later + near_later):
         other = side_swap(others[j], devices)

time: 158 us -> 154 us (0.975); the launches traced: 156 us -> 154 us
  starting transfers between devices: 35.9 us -> 33.6 us
    pallas_call x2, Pallas kernels: 10.8 us -> 0.26 us  [add_sent(): pl.pallas_call(lambda *refs: add_sent_kernel(*refs[:2], *refs[-count:]),...]
    pallas_call x1 -> x2, Pallas kernels: 9.53 us -> 19.1 us  [down_both(): pl.pallas_call(lambda *refs: down_both_kernel(len(activ), *refs), grid_sp...]
    ppermute x14 -> x16, starting transfers between devices: 13.1 us -> 11.7 us  [core_swap(): return lax.ppermute(value, 'tp', [(0, 1), (1, 0)])]
    ppermute x14 -> x16, waiting for transfers between devices: 3.59 us -> 4.53 us  [core_swap(): return lax.ppermute(value, 'tp', [(0, 1), (1, 0)])]
  transfers between devices with their start and end apart: 38 -> 40, of which waited for: 17 -> 18; matrix products, arithmetic and copies ran while one was open for 1% -> 1% of each run, Pallas kernels for 38% -> 38%
where the time goes in v5:
time: 154 us
  Pallas kernels  59 us (38%)
  waiting for transfers between devices  48.9 us (32%)
  starting transfers between devices  33.6 us (22%)
  matrix products  5.51 us (4%)
  other arithmetic  3.08 us (2%)
  local copies, waits for them, and re-layouts  1.99 us (1%)
  between operations  1.77 us (1%)
    pallas_call x3, Pallas kernels, gate_up(): pl.pallas_call(lambda *refs: gate_up_kernel(counts, *refs), grid_spec=plt...  35.3 us
    ppermute x10, waiting for transfers between devices, side_swap(): return lax.ppermute(value, 'req', [(i, i ^ 1) for i in range(devices)])  30.9 us
    pallas_call x2, Pallas kernels, down_both(): pl.pallas_call(lambda *refs: down_both_kernel(len(activ), *refs), grid_sp...  19.1 us
    ppermute x14, starting transfers between devices, pair_shift(): lax.ppermute(value, 'req', [(i, 2 * (i // 2 ^ k) + i % 2) for i in range(...  15.6 us
    ppermute x14, waiting for transfers between devices, pair_shift(): lax.ppermute(value, 'req', [(i, 2 * (i // 2 ^ k) + i % 2) for i in range(...  13.5 us
    ppermute x16, starting transfers between devices, core_swap(): return lax.ppermute(value, 'tp', [(0, 1), (1, 0)])  11.7 us
    ppermute x10, starting transfers between devices, side_swap(): return lax.ppermute(value, 'req', [(i, i ^ 1) for i in range(devices)])  6.32 us
    dot_general x1, matrix products, on_device(): partial_out = jnp.dot(attn_heads, w_out, preferred_element_type=jnp.float32)  4.7 us
  transfers between devices with their start and end apart: 40, of which 18 were waited for; matrix products, arithmetic and copies ran while one was open for 1% of the time, Pallas kernels for 38%

profile of v5, /device:TPU:15, one launch (start us, length us, event | category | flops | bytes accessed | tf_op | source)
XLA Modules:
  0.0 153.8 jit_solution(6736228948791895909)
XLA Ops:
  0.7 0.9 copy-done
  1.6 4.7 %fusion.18 = f32[128,4096]{1,0:T(8,128)S(1)} fusion(bf16[128,1024]{1,0:T(8,128)(2,1)S(1)} %copy-done, bf16[1024,4096]{1,0:T(8,128)(2,1)} %param.13), kind=kOutput, calls=%fused_computation.50 | convolution fusion | flops 1073741824 | bytes 10747904 | tf_op jit(solution)/shard_map/dot_general | solution.py:430
  6.3 0.9 select_convert_fusion
  7.2 0.7 collective-permute-start
  7.9 0.6 slice.57
  9.3 0.3 collective-permute-done
  9.6 0.4 multiply_reduce_fusion.1
  10.0 0.4 collective-permute-start.1
  10.4 0.6 fusion.1
  11.4 0.8 collective-permute-done.2
  12.5 0.6 slot_rows.2
  13.1 0.3 collective-permute-start.5
  13.4 2.3 %collective-permute-start.3 = (bf16[48,2048]{1,0:T(8,128)(2,1)S(1)}, bf16[48,2048]{1,0:T(8,128)(2,1)S(1)}, u32[]{:S(2)}, u32[]{:S(2)}) collective-permute-start(bf16[48,2048]{1,0:T(8,128)(2,1)S(1)} %get-tuple-element.26), channel_id=1, source_target_pairs={{0,16},{2,18},{4,20},{6,22},{8,24},{10,26},{12,28},{14,30},{16,0},... | collective-permute-start | bytes 589832 | tf_op jit(solution)/shard_map/ppermute | solution.py:16
  15.7 1.0 collective-permute-start.4
  16.7 2.8 %collective-permute-done.5.refs_1_.refs_2_ = bf16[48,2048]{1,0:T(8,128)(2,1)S(1)} collective-permute-done((bf16[48,2048]{1,0:T(8,128)(2,1)S(1)}, bf16[48,2048]{1,0:T(8,128)(2,1)S(1)}, u32[]{:S(2)}, u32[]{:S(2)}) %collective-permute-start.5) | collective-permute-done | bytes 196640 | tf_op jit(solution)/shard_map/ppermute | solution.py:16
  19.5 0.3 collective-permute-start.6
  20.1 1.2 collective-permute-start.13
  21.3 7.9 %collective-permute-done.6.refs_0_ = bf16[96,2048]{1,0:T(8,128)(2,1)S(1)} collective-permute-done((bf16[96,2048]{1,0:T(8,128)(2,1)S(1)}, bf16[96,2048]{1,0:T(8,128)(2,1)S(1)}, u32[]{:S(2)}, u32[]{:S(2)}) %collective-permute-start.6) | collective-permute-done | bytes 393248 | tf_op jit(solution)/shard_map/ppermute | solution.py:20
  29.2 1.9 %collective-permute-start.8 = (bf16[96,2048]{1,0:T(8,128)(2,1)S(1)}, bf16[96,2048]{1,0:T(8,128)(2,1)S(1)}, u32[]{:S(2)}, u32[]{:S(2)}) collective-permute-start(bf16[96,2048]{1,0:T(8,128)(2,1)S(1)} %join.10.refs_3_), channel_id=1, source_target_pairs={{0,1},{1,0},{2,3},{3,2},{4,5},{5,4},{6,7},{7,6},{8,9},{9,8},{10,11... | collective-permute-start | bytes 1179656 | tf_op jit(solution)/shard_map/ppermute | solution.py:24
  31.1 1.7 %collective-permute-done.4.refs_1_ = bf16[48,2048]{1,0:T(8,128)(2,1)S(1)} collective-permute-done((bf16[48,2048]{1,0:T(8,128)(2,1)S(1)}, bf16[48,2048]{1,0:T(8,128)(2,1)S(1)}, u32[]{:S(2)}, u32[]{:S(2)}) %collective-permute-start.4) | collective-permute-done | bytes 196640 | tf_op jit(solution)/shard_map/ppermute | solution.py:16
  32.9 0.3 collective-permute-start.9
  33.2 0.8 collective-permute-start.7
  34.1 9.1 %collective-permute-done.9.refs_0_ = bf16[96,2048]{1,0:T(8,128)(2,1)S(1)} collective-permute-done((bf16[96,2048]{1,0:T(8,128)(2,1)S(1)}, bf16[96,2048]{1,0:T(8,128)(2,1)S(1)}, u32[]{:S(2)}, u32[]{:S(2)}) %collective-permute-start.9) | collective-permute-done | bytes 393248 | tf_op jit(solution)/shard_map/ppermute | solution.py:20
  43.2 1.3 collective-permute-start.11
  45.0 2.4 %collective-permute-start.15 = (bf16[48,2048]{1,0:T(8,128)(2,1)S(1)}, bf16[48,2048]{1,0:T(8,128)(2,1)S(1)}, u32[]{:S(2)}, u32[]{:S(2)}) collective-permute-start(bf16[48,2048]{1,0:T(8,128)(2,1)S(1)} %get-tuple-element.33), channel_id=1, source_target_pairs={{0,28},{2,30},{4,24},{6,26},{8,20},{10,22},{12,16},{14,18},{16,12}... | collective-permute-start | bytes 589832 | tf_op jit(solution)/shard_map/ppermute | solution.py:16
  47.5 0.3 collective-permute-start.16
  47.8 16.6 %gate_up.3.refs_2_.refs_1_ = bf16[384,1792]{1,0:T(8,128)(2,1)S(1)} custom-call(s32[1]{0:T(128)} %bitcast.7.refs_0_, bf16[96,2048]{1,0:T(8,128)(2,1)S(1)} %join.13.refs_1_, bf16[96,2048]{1,0:T(8,128)(2,1)S(1)} %collective-permute-done.7.refs_2_, bf16[96,2048]{1,0:T(8,128)(2,1)S(1)} %join.10.refs_3_, bf16[96,2048]{1,0:T(8,128)(2,1)S(1)} %collective-permute-done.8.refs_4_, ...), custom_call_target="tpu_custom_call" | custom-call | flops 1572864 | bytes 4096 | tf_op jit(solution)/shard_map/gate_up/pallas_call | solution.py:190
  64.6 1.1 collective-permute-start.19
  65.7 1.6 %collective-permute-start.22 = (bf16[96,2048]{1,0:T(8,128)(2,1)S(1)}, bf16[96,2048]{1,0:T(8,128)(2,1)S(1)}, u32[]{:S(2)}, u32[]{:S(2)}) collective-permute-start(bf16[96,2048]{1,0:T(8,128)(2,1)S(1)} %join.16.refs_10_.refs_3_), channel_id=1, source_target_pairs={{0,1},{1,0},{2,3},{3,2},{4,5},{5,4},{6,7},{7,6},{8,9},{9,8},{10,11... | collective-permute-start | bytes 1179656 | tf_op jit(solution)/shard_map/ppermute | solution.py:24
  67.4 0.5 collective-permute-start.24
  67.9 9.5 %down_both.2 = (bf16[192,2048]{1,0:T(8,128)(2,1)S(1)}, bf16[192,2048]{1,0:T(8,128)(2,1)S(1)}, f32[384,2048]{1,0:T(8,128)S(1)}) custom-call(s32[1]{0:T(128)} %bitcast.7.refs_0_, bf16[384,1792]{1,0:T(8,128)(2,1)S(1)} %gate_up.3.refs_2_.refs_1_, bf16[1,1792,4096]{2,1,0:T(8,128)(2,1)} %refs_3_.1, bf16[96,2048]{1,0:T(8,128)(2,1)S(1)} %join.17.refs_3_.refs_1_, ...), custom_call_target="tpu_custom_call" | custom-call | flops 688128 | bytes 1792 | tf_op jit(solution)/shard_map/down_both/pallas_call | solution.py:241
  77.6 0.4 collective-permute-start.17
  78.1 1.7 %collective-permute-done.18.refs_1_ = bf16[192,2048]{1,0:T(8,128)(2,1)S(1)} collective-permute-done((bf16[192,2048]{1,0:T(8,128)(2,1)S(1)}, bf16[192,2048]{1,0:T(8,128)(2,1)S(1)}, u32[]{:S(2)}, u32[]{:S(2)}) %collective-permute-start.18) | collective-permute-done | bytes 786464 | tf_op jit(solution)/shard_map/ppermute | solution.py:24
  80.1 0.5 collective-permute-start.20
  80.6 0.3 collective-permute-done.17.refs_1_
  80.9 0.7 collective-permute-start.27
  82.1 10.3 %gate_up.4.refs_2_.refs_1_ = bf16[384,1024]{1,0:T(8,128)(2,1)S(1)} custom-call(s32[1]{0:T(128)} %bitcast.7.refs_0_, bf16[96,2048]{1,0:T(8,128)(2,1)S(1)} %join.17.refs_3_.refs_1_, bf16[96,2048]{1,0:T(8,128)(2,1)S(1)} %collective-permute-done.21.refs_2_, bf16[96,2048]{1,0:T(8,128)(2,1)S(1)} %join.16.refs_10_.refs_3_, ...), custom_call_target="tpu_custom_call" | custom-call | flops 1572864 | bytes 4096 | tf_op jit(solution)/shard_map/gate_up/pallas_call | solution.py:190
  92.5 4.9 %collective-permute-start.25 = (bf16[48,2048]{1,0:T(8,128)(2,1)S(1)}, bf16[48,2048]{1,0:T(8,128)(2,1)S(1)}, u32[]{:S(2)}, u32[]{:S(2)}) collective-permute-start(bf16[48,2048]{1,0:T(8,128)(2,1)S(1)} %get-tuple-element.38.refs_10_), channel_id=1, source_target_pairs={{0,16},{2,18},{4,20},{6,22},{8,24},{10,26},{12,28},{14,30},{16,0},... | collective-permute-start | bytes 589832 | tf_op jit(solution)/shard_map/ppermute | solution.py:16
  97.4 1.0 collective-permute-start.26
  98.6 8.4 %gate_up.5.refs_2_ = bf16[384,768]{1,0:T(8,128)(2,1)S(1)} custom-call(s32[1]{0:T(128)} %bitcast.7.refs_0_, bf16[96,2048]{1,0:T(8,128)(2,1)S(1)} %join.17.refs_3_.refs_1_, bf16[96,2048]{1,0:T(8,128)(2,1)S(1)} %collective-permute-done.21.refs_2_, bf16[96,2048]{1,0:T(8,128)(2,1)S(1)} %join.16.refs_10_.refs_3_, ...), custom_call_target="tpu_custom_call" | custom-call | flops 1572864 | bytes 4096 | tf_op jit(solution)/shard_map/gate_up/pallas_call | solution.py:190
  107.0 0.3 collective-permute-start.28
  107.3 9.5 %down_both.3 = (bf16[192,2048]{1,0:T(8,128)(2,1)S(1)}, bf16[192,2048]{1,0:T(8,128)(2,1)S(1)}, f32[384,2048]{1,0:T(8,128)S(1)}) custom-call(s32[1]{0:T(128)} %bitcast.7.refs_0_, bf16[384,1024]{1,0:T(8,128)(2,1)S(1)} %gate_up.4.refs_2_.refs_1_, bf16[384,768]{1,0:T(8,128)(2,1)S(1)} %gate_up.5.refs_2_, bf16[1,1792,4096]{2,1,0:T(8,128)(2,1)} %refs_3_.1, ...), custom_call_target="tpu_custom_call" | custom-call | flops 688128 | bytes 1792 | tf_op jit(solution)/shard_map/down_both/pallas_call | solution.py:241
  116.9 1.6 %collective-permute-start.30 = (bf16[192,2048]{1,0:T(8,128)(2,1)S(1)}, bf16[192,2048]{1,0:T(8,128)(2,1)S(1)}, u32[]{:S(2)}, u32[]{:S(2)}) collective-permute-start(bf16[192,2048]{1,0:T(8,128)(2,1)S(1)} %get-tuple-element.45), channel_id=1, source_target_pairs={{0,1},{1,0},{2,3},{3,2},{4,5},{5,4},{6,7},{7,6},{8,9},{9,8},{10,11... | collective-permute-start | bytes 2359304 | tf_op jit(solution)/shard_map/ppermute | solution.py:24
  118.5 0.7 mix.4.refs_2_
  119.2 0.7 mix.5.refs_2_
  119.9 0.5 collective-permute-done.30.refs_1_
  120.5 0.3 collective-permute-start.33
  120.8 1.2 collective-permute-start.31
  122.2 0.4 collective-permute-start.37
  122.5 1.2 collective-permute-start.35
  123.8 2.8 %collective-permute-done.33.refs_1_ = bf16[48,2048]{1,0:T(8,128)(2,1)S(1)} collective-permute-done((bf16[48,2048]{1,0:T(8,128)(2,1)S(1)}, bf16[48,2048]{1,0:T(8,128)(2,1)S(1)}, u32[]{:S(2)}, u32[]{:S(2)}) %collective-permute-start.33) | collective-permute-done | bytes 196640 | tf_op jit(solution)/shard_map/ppermute | solution.py:20
  126.8 4.1 %collective-permute-done.31.refs_1_ = bf16[48,2048]{1,0:T(8,128)(2,1)S(1)} collective-permute-done((bf16[48,2048]{1,0:T(8,128)(2,1)S(1)}, bf16[48,2048]{1,0:T(8,128)(2,1)S(1)}, u32[]{:S(2)}, u32[]{:S(2)}) %collective-permute-start.31) | collective-permute-done | bytes 196640 | tf_op jit(solution)/shard_map/ppermute | solution.py:20
  131.0 4.1 %collective-permute-done.37.refs_1_ = bf16[48,2048]{1,0:T(8,128)(2,1)S(1)} collective-permute-done((bf16[48,2048]{1,0:T(8,128)(2,1)S(1)}, bf16[48,2048]{1,0:T(8,128)(2,1)S(1)}, u32[]{:S(2)}, u32[]{:S(2)}) %collective-permute-start.37) | collective-permute-done | bytes 196640 | tf_op jit(solution)/shard_map/ppermute | solution.py:20
  135.1 1.3 collective-permute-start.38
  136.4 2.9 %collective-permute-done.35.refs_1_ = bf16[48,2048]{1,0:T(8,128)(2,1)S(1)} collective-permute-done((bf16[48,2048]{1,0:T(8,128)(2,1)S(1)}, bf16[48,2048]{1,0:T(8,128)(2,1)S(1)}, u32[]{:S(2)}, u32[]{:S(2)}) %collective-permute-start.35) | collective-permute-done | bytes 196640 | tf_op jit(solution)/shard_map/ppermute | solution.py:20
  139.4 0.4 collective-permute-start.36
  139.7 2.5 %collective-permute-done.34.refs_4_ = bf16[48,2048]{1,0:T(8,128)(2,1)S(1)} collective-permute-done((bf16[48,2048]{1,0:T(8,128)(2,1)S(1)}, bf16[48,2048]{1,0:T(8,128)(2,1)S(1)}, u32[]{:S(2)}, u32[]{:S(2)}) %collective-permute-start.34) | collective-permute-done | bytes 196640 | tf_op jit(solution)/shard_map/ppermute | solution.py:16
  142.2 4.0 %collective-permute-done.32.refs_3_ = bf16[48,2048]{1,0:T(8,128)(2,1)S(1)} collective-permute-done((bf16[48,2048]{1,0:T(8,128)(2,1)S(1)}, bf16[48,2048]{1,0:T(8,128)(2,1)S(1)}, u32[]{:S(2)}, u32[]{:S(2)}) %collective-permute-start.32) | collective-permute-done | bytes 196640 | tf_op jit(solution)/shard_map/ppermute | solution.py:16
  146.2 0.7 mix.6.refs_2_
  146.9 2.3 %collective-permute-done.36.refs_3_ = bf16[48,2048]{1,0:T(8,128)(2,1)S(1)} collective-permute-done((bf16[48,2048]{1,0:T(8,128)(2,1)S(1)}, bf16[48,2048]{1,0:T(8,128)(2,1)S(1)}, u32[]{:S(2)}, u32[]{:S(2)}) %collective-permute-start.36) | collective-permute-done | bytes 196640 | tf_op jit(solution)/shard_map/ppermute | solution.py:16
  149.2 0.7 mix.7
  150.1 1.8 %collective-permute-start.39 = (f32[128,1]{0,1:T(1,128)S(1)}, f32[128,1]{0,1:T(1,128)S(1)}, u32[]{:S(2)}, u32[]{:S(2)}) collective-permute-start(f32[128,1]{0,1:T(1,128)S(1)} %bitcast.25), channel_id=1, source_target_pairs={{0,1},{1,0},{2,3},{3,2},{4,5},{5,4},{6,7},{7,6},{8,9},{9,8},{10,11... | collective-permute-start | bytes 1544 | tf_op jit(solution)/shard_map/ppermute | solution.py:24
  151.9 0.8 collective-permute-done.39
  152.7 1.1 multiply_convert_fusion
  (92 shorter events, 4.0 us)
Async XLA Ops:
  0.6 1.0 copy-start
  1.6 6.3 %copy-start.7 = (s32[1,5]{1,0:T(1,128)S(1)}, s32[1,5]{1,0:T(1,128)}, u32[]{:S(2)}) copy-start(s32[1,5]{1,0:T(1,128)} %param.17) | copy-start | bytes 64
  1.6 7.5 %copy-start.8 = (s32[8]{0:T(128)S(1)}, s32[8]{0:T(128)}, u32[]{:S(2)}) copy-start(s32[8]{0:T(128)} %param.18) | copy-start | bytes 100
  1.6 8.0 %copy-start.2 = (bf16[128,2048]{1,0:T(8,128)(2,1)S(1)}, bf16[128,2048]{1,0:T(8,128)(2,1)}, u32[]{:S(2)}) copy-start(bf16[128,2048]{1,0:T(8,128)(2,1)} %param.12) | copy-start | bytes 1572868
  7.2 2.4 %collective-permute-start = (bf16[128,2048]{1,0:T(8,128)(2,1)}, bf16[128,2048]{1,0:T(8,128)(2,1)S(1)}, u32[]{:S(2)}, u32[]{:S(2)}) collective-permute-start(bf16[128,2048]{1,0:T(8,128)(2,1)} %select_convert_fusion), channel_id=1, source_target_pairs={{0,1},{1,0},{2,3},{3,2},{4,5},{5,4},{6,7},{7,6},{8,9},{9,8},{10,11... | collective-permute-start | bytes 1572872 | tf_op jit(solution)/shard_map/ppermute | solution.py:24
  9.3 1.1 copy-start.3
  9.3 1.1 copy-start.4
  10.0 2.2 %copy-start.6 = (s32[128,2]{0,1:T(2,128)S(1)}, s32[128,2]{0,1:T(2,128)}, u32[]{:S(2)}) copy-start(s32[128,2]{0,1:T(2,128)} %param.16) | copy-start | bytes 3076
  10.0 1.3 collective-permute-start.1
  11.0 1.2 collective-permute-start.2
  13.1 6.4 %collective-permute-start.5 = (bf16[48,2048]{1,0:T(8,128)(2,1)S(1)}, bf16[48,2048]{1,0:T(8,128)(2,1)S(1)}, u32[]{:S(2)}, u32[]{:S(2)}) collective-permute-start(bf16[48,2048]{1,0:T(8,128)(2,1)S(1)} %get-tuple-element.29), channel_id=1, source_target_pairs={{0,4},{2,6},{4,0},{6,2},{8,12},{10,14},{12,8},{14,10},{16,20},{18,... | collective-permute-start | bytes 589832 | tf_op jit(solution)/shard_map/ppermute | solution.py:16
  13.4 17.8 %collective-permute-start.3 = (bf16[48,2048]{1,0:T(8,128)(2,1)S(1)}, bf16[48,2048]{1,0:T(8,128)(2,1)S(1)}, u32[]{:S(2)}, u32[]{:S(2)}) collective-permute-start(bf16[48,2048]{1,0:T(8,128)(2,1)S(1)} %get-tuple-element.26), channel_id=1, source_target_pairs={{0,16},{2,18},{4,20},{6,22},{8,24},{10,26},{12,28},{14,30},{16,0},... | collective-permute-start | bytes 589832 | tf_op jit(solution)/shard_map/ppermute | solution.py:16
  15.7 17.2 %collective-permute-start.4 = (bf16[48,2048]{1,0:T(8,128)(2,1)S(1)}, bf16[48,2048]{1,0:T(8,128)(2,1)S(1)}, u32[]{:S(2)}, u32[]{:S(2)}) collective-permute-start(bf16[48,2048]{1,0:T(8,128)(2,1)S(1)} %get-tuple-element.27), channel_id=1, source_target_pairs={{0,20},{2,22},{4,16},{6,18},{8,28},{10,30},{12,24},{14,26},{16,4},... | collective-permute-start | bytes 589832 | tf_op jit(solution)/shard_map/ppermute | solution.py:16
  19.5 9.7 %collective-permute-start.6 = (bf16[96,2048]{1,0:T(8,128)(2,1)S(1)}, bf16[96,2048]{1,0:T(8,128)(2,1)S(1)}, u32[]{:S(2)}, u32[]{:S(2)}) collective-permute-start(bf16[96,2048]{1,0:T(8,128)(2,1)S(1)} %join.10.refs_3_), channel_id=1, source_target_pairs={{0,2},{2,0},{4,6},{6,4},{8,10},{10,8},{12,14},{14,12},{16,18},{18,... | collective-permute-start | bytes 1179656 | tf_op jit(solution)/shard_map/ppermute | solution.py:20
  19.8 24.7 %collective-permute-start.12 = (bf16[48,2048]{1,0:T(8,128)(2,1)S(1)}, bf16[48,2048]{1,0:T(8,128)(2,1)S(1)}, u32[]{:S(2)}, u32[]{:S(2)}) collective-permute-start(bf16[48,2048]{1,0:T(8,128)(2,1)S(1)} %get-tuple-element.30), channel_id=1, source_target_pairs={{0,8},{2,10},{4,12},{6,14},{8,0},{10,2},{12,4},{14,6},{16,24},{18,... | collective-permute-start | bytes 589832 | tf_op jit(solution)/shard_map/ppermute | solution.py:16
  20.1 24.8 %collective-permute-start.13 = (bf16[48,2048]{1,0:T(8,128)(2,1)S(1)}, bf16[48,2048]{1,0:T(8,128)(2,1)S(1)}, u32[]{:S(2)}, u32[]{:S(2)}) collective-permute-start(bf16[48,2048]{1,0:T(8,128)(2,1)S(1)} %get-tuple-element.31), channel_id=1, source_target_pairs={{0,12},{2,14},{4,8},{6,10},{8,4},{10,6},{12,0},{14,2},{16,28},{18,... | collective-permute-start | bytes 589832 | tf_op jit(solution)/shard_map/ppermute | solution.py:16
  29.2 15.8 %collective-permute-start.8 = (bf16[96,2048]{1,0:T(8,128)(2,1)S(1)}, bf16[96,2048]{1,0:T(8,128)(2,1)S(1)}, u32[]{:S(2)}, u32[]{:S(2)}) collective-permute-start(bf16[96,2048]{1,0:T(8,128)(2,1)S(1)} %join.10.refs_3_), channel_id=1, source_target_pairs={{0,1},{1,0},{2,3},{3,2},{4,5},{5,4},{6,7},{7,6},{8,9},{9,8},{10,11... | collective-permute-start | bytes 1179656 | tf_op jit(solution)/shard_map/ppermute | solution.py:24
  32.9 10.3 %collective-permute-start.9 = (bf16[96,2048]{1,0:T(8,128)(2,1)S(1)}, bf16[96,2048]{1,0:T(8,128)(2,1)S(1)}, u32[]{:S(2)}, u32[]{:S(2)}) collective-permute-start(bf16[96,2048]{1,0:T(8,128)(2,1)S(1)} %join.13.refs_1_), channel_id=1, source_target_pairs={{0,2},{2,0},{4,6},{6,4},{8,10},{10,8},{12,14},{14,12},{16,18},{18,... | collective-permute-start | bytes 1179656 | tf_op jit(solution)/shard_map/ppermute | solution.py:20
  33.2 14.2 %collective-permute-start.7 = (bf16[96,2048]{1,0:T(8,128)(2,1)S(1)}, bf16[96,2048]{1,0:T(8,128)(2,1)S(1)}, u32[]{:S(2)}, u32[]{:S(2)}) collective-permute-start(bf16[96,2048]{1,0:T(8,128)(2,1)S(1)} %join.13.refs_1_), channel_id=1, source_target_pairs={{0,1},{1,0},{2,3},{3,2},{4,5},{5,4},{6,7},{7,6},{8,9},{9,8},{10,11... | collective-permute-start | bytes 1179656 | tf_op jit(solution)/shard_map/ppermute | solution.py:24
  43.2 4.6 %collective-permute-start.11 = (bf16[96,2048]{1,0:T(8,128)(2,1)S(1)}, bf16[96,2048]{1,0:T(8,128)(2,1)S(1)}, u32[]{:S(2)}, u32[]{:S(2)}) collective-permute-start(bf16[96,2048]{1,0:T(8,128)(2,1)S(1)} %join.12.refs_2_.refs_7_), channel_id=1, source_target_pairs={{0,1},{1,0},{2,3},{3,2},{4,5},{5,4},{6,7},{7,6},{8,9},{9,8},{10,11... | collective-permute-start | bytes 1179656 | tf_op jit(solution)/shard_map/ppermute | solution.py:24
  44.5 3.3 %collective-permute-start.10 = (bf16[96,2048]{1,0:T(8,128)(2,1)S(1)}, bf16[96,2048]{1,0:T(8,128)(2,1)S(1)}, u32[]{:S(2)}, u32[]{:S(2)}) collective-permute-start(bf16[96,2048]{1,0:T(8,128)(2,1)S(1)} %join.15.refs_5_), channel_id=1, source_target_pairs={{0,1},{1,0},{2,3},{3,2},{4,5},{5,4},{6,7},{7,6},{8,9},{9,8},{10,11... | collective-permute-start | bytes 1179656 | tf_op jit(solution)/shard_map/ppermute | solution.py:24
  44.9 19.5 %collective-permute-start.14 = (bf16[48,2048]{1,0:T(8,128)(2,1)S(1)}, bf16[48,2048]{1,0:T(8,128)(2,1)S(1)}, u32[]{:S(2)}, u32[]{:S(2)}) collective-permute-start(bf16[48,2048]{1,0:T(8,128)(2,1)S(1)} %get-tuple-element.32), channel_id=1, source_target_pairs={{0,24},{2,26},{4,28},{6,30},{8,16},{10,18},{12,20},{14,22},{16,8},... | collective-permute-start | bytes 589832 | tf_op jit(solution)/shard_map/ppermute | solution.py:16
  45.0 19.5 %collective-permute-start.15 = (bf16[48,2048]{1,0:T(8,128)(2,1)S(1)}, bf16[48,2048]{1,0:T(8,128)(2,1)S(1)}, u32[]{:S(2)}, u32[]{:S(2)}) collective-permute-start(bf16[48,2048]{1,0:T(8,128)(2,1)S(1)} %get-tuple-element.33), channel_id=1, source_target_pairs={{0,28},{2,30},{4,24},{6,26},{8,20},{10,22},{12,16},{14,18},{16,12}... | collective-permute-start | bytes 589832 | tf_op jit(solution)/shard_map/ppermute | solution.py:16
  47.5 19.9 %collective-permute-start.16 = (bf16[96,2048]{1,0:T(8,128)(2,1)S(1)}, bf16[96,2048]{1,0:T(8,128)(2,1)S(1)}, u32[]{:S(2)}, u32[]{:S(2)}) collective-permute-start(bf16[96,2048]{1,0:T(8,128)(2,1)S(1)} %join.16.refs_10_.refs_3_), channel_id=1, source_target_pairs={{0,2},{2,0},{4,6},{6,4},{8,10},{10,8},{12,14},{14,12},{16,18},{18,... | collective-permute-start | bytes 1179656 | tf_op jit(solution)/shard_map/ppermute | solution.py:20
  64.6 13.0 %collective-permute-start.19 = (bf16[96,2048]{1,0:T(8,128)(2,1)S(1)}, bf16[96,2048]{1,0:T(8,128)(2,1)S(1)}, u32[]{:S(2)}, u32[]{:S(2)}) collective-permute-start(bf16[96,2048]{1,0:T(8,128)(2,1)S(1)} %join.17.refs_3_.refs_1_), channel_id=1, source_target_pairs={{0,2},{2,0},{4,6},{6,4},{8,10},{10,8},{12,14},{14,12},{16,18},{18,... | collective-permute-start | bytes 1179656 | tf_op jit(solution)/shard_map/ppermute | solution.py:20
  65.7 14.4 %collective-permute-start.22 = (bf16[96,2048]{1,0:T(8,128)(2,1)S(1)}, bf16[96,2048]{1,0:T(8,128)(2,1)S(1)}, u32[]{:S(2)}, u32[]{:S(2)}) collective-permute-start(bf16[96,2048]{1,0:T(8,128)(2,1)S(1)} %join.16.refs_10_.refs_3_), channel_id=1, source_target_pairs={{0,1},{1,0},{2,3},{3,2},{4,5},{5,4},{6,7},{7,6},{8,9},{9,8},{10,11... | collective-permute-start | bytes 1179656 | tf_op jit(solution)/shard_map/ppermute | solution.py:24
  67.3 14.8 %collective-permute-start.21 = (bf16[96,2048]{1,0:T(8,128)(2,1)S(1)}, bf16[96,2048]{1,0:T(8,128)(2,1)S(1)}, u32[]{:S(2)}, u32[]{:S(2)}) collective-permute-start(bf16[96,2048]{1,0:T(8,128)(2,1)S(1)} %join.17.refs_3_.refs_1_), channel_id=1, source_target_pairs={{0,1},{1,0},{2,3},{3,2},{4,5},{5,4},{6,7},{7,6},{8,9},{9,8},{10,11... | collective-permute-start | bytes 1179656 | tf_op jit(solution)/shard_map/ppermute | solution.py:24
  67.4 14.7 %collective-permute-start.24 = (bf16[96,2048]{1,0:T(8,128)(2,1)S(1)}, bf16[96,2048]{1,0:T(8,128)(2,1)S(1)}, u32[]{:S(2)}, u32[]{:S(2)}) collective-permute-start(bf16[96,2048]{1,0:T(8,128)(2,1)S(1)} %join.18.refs_4_.refs_7_), channel_id=1, source_target_pairs={{0,1},{1,0},{2,3},{3,2},{4,5},{5,4},{6,7},{7,6},{8,9},{9,8},{10,11... | collective-permute-start | bytes 1179656 | tf_op jit(solution)/shard_map/ppermute | solution.py:24
  77.5 2.4 %collective-permute-start.18 = (bf16[192,2048]{1,0:T(8,128)(2,1)S(1)}, bf16[192,2048]{1,0:T(8,128)(2,1)S(1)}, u32[]{:S(2)}, u32[]{:S(2)}) collective-permute-start(bf16[192,2048]{1,0:T(8,128)(2,1)S(1)} %get-tuple-element.36), channel_id=1, source_target_pairs={{0,1},{1,0},{2,3},{3,2},{4,5},{5,4},{6,7},{7,6},{8,9},{9,8},{10,11... | collective-permute-start | bytes 2359304 | tf_op jit(solution)/shard_map/ppermute | solution.py:24
  77.6 3.3 %collective-permute-start.17 = (bf16[192,2048]{1,0:T(8,128)(2,1)S(1)}, bf16[192,2048]{1,0:T(8,128)(2,1)S(1)}, u32[]{:S(2)}, u32[]{:S(2)}) collective-permute-start(bf16[192,2048]{1,0:T(8,128)(2,1)S(1)} %get-tuple-element.35), channel_id=1, source_target_pairs={{0,1},{1,0},{2,3},{3,2},{4,5},{5,4},{6,7},{7,6},{8,9},{9,8},{10,11... | collective-permute-start | bytes 2359304 | tf_op jit(solution)/shard_map/ppermute | solution.py:24
  79.8 2.3 %collective-permute-start.23 = (bf16[96,2048]{1,0:T(8,128)(2,1)S(1)}, bf16[96,2048]{1,0:T(8,128)(2,1)S(1)}, u32[]{:S(2)}, u32[]{:S(2)}) collective-permute-start(bf16[96,2048]{1,0:T(8,128)(2,1)S(1)} %join.19.refs_2_.refs_5_), channel_id=1, source_target_pairs={{0,1},{1,0},{2,3},{3,2},{4,5},{5,4},{6,7},{7,6},{8,9},{9,8},{10,11... | collective-permute-start | bytes 1179656 | tf_op jit(solution)/shard_map/ppermute | solution.py:24
  80.1 12.3 %collective-permute-start.20 = (bf16[96,2048]{1,0:T(8,128)(2,1)S(1)}, bf16[96,2048]{1,0:T(8,128)(2,1)S(1)}, u32[]{:S(2)}, u32[]{:S(2)}) collective-permute-start(bf16[96,2048]{1,0:T(8,128)(2,1)S(1)} %get-tuple-element.37.refs_2_), channel_id=1, source_target_pairs={{0,2},{2,0},{4,6},{6,4},{8,10},{10,8},{12,14},{14,12},{16,18},{18,... | collective-permute-start | bytes 1179656 | tf_op jit(solution)/shard_map/ppermute | solution.py:20
  80.9 26.0 %collective-permute-start.27 = (bf16[96,2048]{1,0:T(8,128)(2,1)S(1)}, bf16[96,2048]{1,0:T(8,128)(2,1)S(1)}, u32[]{:S(2)}, u32[]{:S(2)}) collective-permute-start(bf16[96,2048]{1,0:T(8,128)(2,1)S(1)} %get-tuple-element.40), channel_id=1, source_target_pairs={{0,2},{2,0},{4,6},{6,4},{8,10},{10,8},{12,14},{14,12},{16,18},{18,... | collective-permute-start | bytes 1179656 | tf_op jit(solution)/shard_map/ppermute | solution.py:20
  92.5 26.0 %collective-permute-start.25 = (bf16[48,2048]{1,0:T(8,128)(2,1)S(1)}, bf16[48,2048]{1,0:T(8,128)(2,1)S(1)}, u32[]{:S(2)}, u32[]{:S(2)}) collective-permute-start(bf16[48,2048]{1,0:T(8,128)(2,1)S(1)} %get-tuple-element.38.refs_10_), channel_id=1, source_target_pairs={{0,16},{2,18},{4,20},{6,22},{8,24},{10,26},{12,28},{14,30},{16,0},... | collective-permute-start | bytes 589832 | tf_op jit(solution)/shard_map/ppermute | solution.py:16
  97.4 21.1 %collective-permute-start.26 = (bf16[48,2048]{1,0:T(8,128)(2,1)S(1)}, bf16[48,2048]{1,0:T(8,128)(2,1)S(1)}, u32[]{:S(2)}, u32[]{:S(2)}) collective-permute-start(bf16[48,2048]{1,0:T(8,128)(2,1)S(1)} %get-tuple-element.39.refs_11_), channel_id=1, source_target_pairs={{0,20},{2,22},{4,16},{6,18},{8,28},{10,30},{12,24},{14,26},{16,4},... | collective-permute-start | bytes 589832 | tf_op jit(solution)/shard_map/ppermute | solution.py:16
  107.0 12.2 %collective-permute-start.28 = (bf16[48,2048]{1,0:T(8,128)(2,1)S(1)}, bf16[48,2048]{1,0:T(8,128)(2,1)S(1)}, u32[]{:S(2)}, u32[]{:S(2)}) collective-permute-start(bf16[48,2048]{1,0:T(8,128)(2,1)S(1)} %get-tuple-element.42.refs_5_), channel_id=1, source_target_pairs={{0,4},{2,6},{4,0},{6,2},{8,12},{10,14},{12,8},{14,10},{16,20},{18,... | collective-permute-start | bytes 589832 | tf_op jit(solution)/shard_map/ppermute | solution.py:16
  116.9 3.5 %collective-permute-start.30 = (bf16[192,2048]{1,0:T(8,128)(2,1)S(1)}, bf16[192,2048]{1,0:T(8,128)(2,1)S(1)}, u32[]{:S(2)}, u32[]{:S(2)}) collective-permute-start(bf16[192,2048]{1,0:T(8,128)(2,1)S(1)} %get-tuple-element.45), channel_id=1, source_target_pairs={{0,1},{1,0},{2,3},{3,2},{4,5},{5,4},{6,7},{7,6},{8,9},{9,8},{10,11... | collective-permute-start | bytes 2359304 | tf_op jit(solution)/shard_map/ppermute | solution.py:24
  118.4 5.3 %collective-permute-start.29 = (bf16[192,2048]{1,0:T(8,128)(2,1)S(1)}, bf16[192,2048]{1,0:T(8,128)(2,1)S(1)}, u32[]{:S(2)}, u32[]{:S(2)}) collective-permute-start(bf16[192,2048]{1,0:T(8,128)(2,1)S(1)} %get-tuple-element.44), channel_id=1, source_target_pairs={{0,1},{1,0},{2,3},{3,2},{4,5},{5,4},{6,7},{7,6},{8,9},{9,8},{10,11... | collective-permute-start | bytes 2359304 | tf_op jit(solution)/shard_map/ppermute | solution.py:24
  120.5 6.2 %collective-permute-start.33 = (bf16[48,2048]{1,0:T(8,128)(2,1)S(1)}, bf16[48,2048]{1,0:T(8,128)(2,1)S(1)}, u32[]{:S(2)}, u32[]{:S(2)}) collective-permute-start(bf16[48,2048]{1,0:T(8,128)(2,1)S(1)} %get-tuple-element.47), channel_id=1, source_target_pairs={{0,2},{2,0},{4,6},{6,4},{8,10},{10,8},{12,14},{14,12},{16,18},{18,... | collective-permute-start | bytes 589832 | tf_op jit(solution)/shard_map/ppermute | solution.py:20
  120.8 10.0 %collective-permute-start.31 = (bf16[48,2048]{1,0:T(8,128)(2,1)S(1)}, bf16[48,2048]{1,0:T(8,128)(2,1)S(1)}, u32[]{:S(2)}, u32[]{:S(2)}) collective-permute-start(bf16[48,2048]{1,0:T(8,128)(2,1)S(1)} %get-tuple-element.46.refs_2_), channel_id=1, source_target_pairs={{0,2},{2,0},{4,6},{6,4},{8,10},{10,8},{12,14},{14,12},{16,18},{18,... | collective-permute-start | bytes 589832 | tf_op jit(solution)/shard_map/ppermute | solution.py:20
  122.2 12.9 %collective-permute-start.37 = (bf16[48,2048]{1,0:T(8,128)(2,1)S(1)}, bf16[48,2048]{1,0:T(8,128)(2,1)S(1)}, u32[]{:S(2)}, u32[]{:S(2)}) collective-permute-start(bf16[48,2048]{1,0:T(8,128)(2,1)S(1)} %get-tuple-element.49), channel_id=1, source_target_pairs={{0,2},{2,0},{4,6},{6,4},{8,10},{10,8},{12,14},{14,12},{16,18},{18,... | collective-permute-start | bytes 589832 | tf_op jit(solution)/shard_map/ppermute | solution.py:20
  122.5 16.8 %collective-permute-start.35 = (bf16[48,2048]{1,0:T(8,128)(2,1)S(1)}, bf16[48,2048]{1,0:T(8,128)(2,1)S(1)}, u32[]{:S(2)}, u32[]{:S(2)}) collective-permute-start(bf16[48,2048]{1,0:T(8,128)(2,1)S(1)} %get-tuple-element.48), channel_id=1, source_target_pairs={{0,2},{2,0},{4,6},{6,4},{8,10},{10,8},{12,14},{14,12},{16,18},{18,... | collective-permute-start | bytes 589832 | tf_op jit(solution)/shard_map/ppermute | solution.py:20
  126.7 15.5 %collective-permute-start.34 = (bf16[48,2048]{1,0:T(8,128)(2,1)S(1)}, bf16[48,2048]{1,0:T(8,128)(2,1)S(1)}, u32[]{:S(2)}, u32[]{:S(2)}) collective-permute-start(bf16[48,2048]{1,0:T(8,128)(2,1)S(1)} %add_sides.9), channel_id=1, source_target_pairs={{0,28},{2,30},{4,24},{6,26},{8,20},{10,22},{12,16},{14,18},{16,12}... | collective-permute-start | bytes 589832 | tf_op jit(solution)/shard_map/ppermute | solution.py:16
  130.9 15.3 %collective-permute-start.32 = (bf16[48,2048]{1,0:T(8,128)(2,1)S(1)}, bf16[48,2048]{1,0:T(8,128)(2,1)S(1)}, u32[]{:S(2)}, u32[]{:S(2)}) collective-permute-start(bf16[48,2048]{1,0:T(8,128)(2,1)S(1)} %add_sides.8), channel_id=1, source_target_pairs={{0,24},{2,26},{4,28},{6,30},{8,16},{10,18},{12,20},{14,22},{16,8},... | collective-permute-start | bytes 589832 | tf_op jit(solution)/shard_map/ppermute | solution.py:16
  135.1 11.8 %collective-permute-start.38 = (bf16[48,2048]{1,0:T(8,128)(2,1)S(1)}, bf16[48,2048]{1,0:T(8,128)(2,1)S(1)}, u32[]{:S(2)}, u32[]{:S(2)}) collective-permute-start(bf16[48,2048]{1,0:T(8,128)(2,1)S(1)} %add_sides.11), channel_id=1, source_target_pairs={{0,12},{2,14},{4,8},{6,10},{8,4},{10,6},{12,0},{14,2},{16,28},{18,... | collective-permute-start | bytes 589832 | tf_op jit(solution)/shard_map/ppermute | solution.py:16
  139.4 9.9 %collective-permute-start.36 = (bf16[48,2048]{1,0:T(8,128)(2,1)S(1)}, bf16[48,2048]{1,0:T(8,128)(2,1)S(1)}, u32[]{:S(2)}, u32[]{:S(2)}) collective-permute-start(bf16[48,2048]{1,0:T(8,128)(2,1)S(1)} %add_sides.10), channel_id=1, source_target_pairs={{0,8},{2,10},{4,12},{6,14},{8,0},{10,2},{12,4},{14,6},{16,24},{18,... | collective-permute-start | bytes 589832 | tf_op jit(solution)/shard_map/ppermute | solution.py:16
  146.9 5.8 %copy-start.5 = (f32[2048]{0:T(1024)S(1)}, f32[2048]{0:T(1024)}, u32[]{:S(2)}) copy-start(f32[2048]{0:T(1024)} %param.21) | copy-start | bytes 24580
  149.2 4.6 %copy-start.1 = (bf16[128,1024]{1,0:T(8,128)(2,1)S(1)}, bf16[128,1024]{1,0:T(8,128)(2,1)}, u32[]{:S(2)}) copy-start(bf16[128,1024]{1,0:T(8,128)(2,1)} %param.11) | copy-start | bytes 786436
  150.1 2.6 %collective-permute-start.39 = (f32[128,1]{0,1:T(1,128)S(1)}, f32[128,1]{0,1:T(1,128)S(1)}, u32[]{:S(2)}, u32[]{:S(2)}) collective-permute-start(f32[128,1]{0,1:T(1,128)S(1)} %bitcast.25), channel_id=1, source_target_pairs={{0,1},{1,0},{2,3},{3,2},{4,5},{5,4},{6,7},{7,6},{8,9},{9,8},{10,11... | collective-permute-start | bytes 1544 | tf_op jit(solution)/shard_map/ppermute | solution.py:24
